TPU v7x, 128 devices: a whole 4x4x4 slice. The times are simulated.
128 devices in a mesh: dp: 32 (over z, y, x_hi), mp: 4 (over x_lo, core).
Axes of the slice: x: 4 (x_hi: 2, x_lo: 2; x = x_hi * 2 + x_lo), y: 4, z: 4, core: 2. Of those that a mesh axis runs over, the one named last changes fastest.
Arguments:
- gen_input: bfloat16 [12288, 3072], P(('dp', 'mp')), may hold values from -6 to 6
- noise_score: bfloat16 [12288, 3072], P(('dp', 'mp')), may hold values from -24 to 24
- gen_steps: int32 [12], replicated, may hold values from 0 to 999
- score_steps: int32 [12], replicated, may hold values from 20 to 979
- base_up: bfloat16 [3072, 6144], P('dp', 'mp'), may hold values from -0.109375 to 0.109375
- base_down: bfloat16 [6144, 3072], P('mp', 'dp'), may hold values from -0.078125 to 0.078125
- gen_adapt_in: bfloat16 [3072, 64], replicated, may hold values from -0.109375 to 0.109375
- gen_adapt_out: bfloat16 [64, 6144], P(None, 'mp'), may hold values from -0.75 to 0.75
- fake_adapt_in: bfloat16 [3072, 64], replicated, may hold values from -0.109375 to 0.109375
- fake_adapt_out: bfloat16 [64, 6144], P(None, 'mp'), may hold values from -0.75 to 0.75
- modulation_scale: float32 [3072], replicated, may hold values from -1.8 to 1.8
- modulation_shift: float32 [3072], replicated, may hold values from -1.8 to 1.8
- output_gate: float32 [3072], replicated, may hold values from 0.5 to 1.5
Outputs:
- score_diff: bfloat16 [12288, 3072], P(('dp', 'mp'))
- gen_grad_in: float32 [3072, 64], P(('dp', 'mp'))
- gen_grad_out: float32 [64, 6144], P('dp', 'mp')
- fake_grad_in: float32 [3072, 64], P(('dp', 'mp'))
- fake_grad_out: float32 [64, 6144], P('dp', 'mp')
All inputs are finite; a program needn't handle non-finite values.
Results may differ from a plain program's by a relative error of at most 0.035.
Values may be sent and summed in bfloat16 or wider, within the bound.
No kernel may reach another device: no remote copies, remote signals or barrier semaphores. Data moves between devices by JAX's collectives and lax.ppermute only.
A program may use at most 128 MiB of HBM per device.

v0:
```python
import math

import jax
import jax.numpy as jnp
from jax import lax
from jax.sharding import PartitionSpec as P

IMG_TOK = 1024


gelu_coef = 0.044715
root_two_pi = math.sqrt(2.0 / math.pi)


def gelu_value(pre):
    inner_arg = root_two_pi * (pre + gelu_coef * pre * pre * pre)
    return 0.5 * pre * (1.0 + jnp.tanh(inner_arg))


def gelu_slope(pre):
    tanh_val = jnp.tanh(root_two_pi * (pre + gelu_coef * pre * pre * pre))
    return 0.5 * (1.0 + tanh_val) + 0.5 * pre * (1.0 - tanh_val * tanh_val) * root_two_pi * (
        1.0 + 3.0 * gelu_coef * pre * pre
    )


def embedding(steps, feature_count):
    half_width = feature_count // 2
    frequency = jnp.exp(-math.log(10000.0) * jnp.arange(half_width, dtype=jnp.float32) / half_width)
    phase_angle = steps.astype(jnp.float32)[:, None] * frequency[None, :]
    return jnp.concatenate([jnp.sin(phase_angle), jnp.cos(phase_angle)], axis=1)


def modulate(rows, embed, modulation_scale, modulation_shift):
    widened = rows.astype(jnp.float32)
    normed = widened * lax.rsqrt(jnp.mean(widened * widened, axis=1, keepdims=True) + 1e-06)
    return (normed * (1.0 + modulation_scale * embed) + modulation_shift * embed).astype(
        jnp.bfloat16
    )


def matmul(left, right):
    return jnp.dot(left, right, preferred_element_type=jnp.float32)


def contract(left, right, left_dim, right_dim):
    return lax.dot_general(
        left, right, (((left_dim,), (right_dim,)), ((), ())), preferred_element_type=jnp.float32
    )


def row_steps(steps, first_row, row_count):
    image_ids = (first_row + jnp.arange(row_count, dtype=jnp.int32)) // IMG_TOK
    matches = image_ids[:, None] == jnp.arange(steps.shape[0], dtype=jnp.int32)[None, :]
    return jnp.sum(jnp.where(matches, steps[None, :], 0), axis=1)


def local(
    gen_input,
    noise_score,
    gen_steps,
    score_steps,
    base_up,
    base_down,
    gen_adapt_in,
    gen_adapt_out,
    fake_adapt_in,
    fake_adapt_out,
    modulation_scale,
    modulation_shift,
    output_gate,
):
    feature_count = gen_input.shape[1]
    shard_rows = gen_input.shape[0]
    group_rows = shard_rows * lax.axis_size("mp")
    image_count = gen_steps.shape[0]
    loss_scale = 1.0 / math.sqrt(image_count * IMG_TOK)
    group_first = lax.axis_index("dp") * group_rows
    shard_first = group_first + lax.axis_index("mp") * shard_rows
    group_gen_steps = row_steps(gen_steps, group_first, group_rows)
    group_score_steps = row_steps(score_steps, group_first, group_rows)
    shard_score_steps = row_steps(score_steps, shard_first, shard_rows)
    given_rows = lax.all_gather(gen_input, "mp", axis=0, tiled=True)
    u_gen = modulate(
        given_rows, embedding(group_gen_steps, feature_count), modulation_scale, modulation_shift
    )
    low_gen = matmul(u_gen, gen_adapt_in).astype(jnp.bfloat16)
    up_full, down_full = (
        lax.all_gather(base_up, "dp", axis=0, tiled=True),
        lax.all_gather(base_down, "dp", axis=1, tiled=True),
    )
    pre_gen = matmul(u_gen, up_full) + matmul(low_gen, gen_adapt_out)
    act_gen = gelu_value(pre_gen).astype(jnp.bfloat16)
    out_gen = matmul(act_gen, down_full)
    out_mine = lax.psum_scatter(
        out_gen.astype(jnp.bfloat16), "mp", scatter_dimension=0, tiled=True
    ).astype(jnp.float32)
    latents = (gen_input.astype(jnp.float32) + output_gate * out_mine).astype(jnp.bfloat16)
    blend = ((shard_score_steps.astype(jnp.float32) + 0.5) / 1000.0)[:, None]
    noised = (
        (1.0 - blend) * latents.astype(jnp.float32) + blend * noise_score.astype(jnp.float32)
    ).astype(jnp.bfloat16)
    noised_group = lax.all_gather(noised, "mp", axis=0, tiled=True)
    u_score = modulate(
        noised_group,
        embedding(group_score_steps, feature_count),
        modulation_scale,
        modulation_shift,
    )
    low_fake = matmul(u_score, fake_adapt_in).astype(jnp.bfloat16)
    pre_real = matmul(u_score, up_full)
    pre_fake = pre_real + matmul(low_fake, fake_adapt_out)
    act_real = gelu_value(pre_real).astype(jnp.bfloat16)
    act_fake = gelu_value(pre_fake).astype(jnp.bfloat16)
    out_real, out_fake = (
        lax.psum_scatter(
            matmul(act_real, down_full).astype(jnp.bfloat16), "mp", scatter_dimension=0, tiled=True
        ).astype(jnp.float32),
        lax.psum_scatter(
            matmul(act_fake, down_full).astype(jnp.bfloat16), "mp", scatter_dimension=0, tiled=True
        ).astype(jnp.float32),
    )
    score_diff = (output_gate * (out_fake - out_real)).astype(jnp.bfloat16)
    cot_gen = (output_gate * score_diff.astype(jnp.float32) * loss_scale).astype(jnp.bfloat16)
    target = noise_score.astype(jnp.float32) - latents.astype(jnp.float32)
    cot_fake = (
        output_gate * (noised.astype(jnp.float32) + output_gate * out_fake - target) * loss_scale
    ).astype(jnp.bfloat16)
    cot_gen_group, cot_fake_group = (
        lax.all_gather(cot_gen, "mp", axis=0, tiled=True),
        lax.all_gather(cot_fake, "mp", axis=0, tiled=True),
    )
    back_gen = (contract(cot_gen_group, down_full, 1, 1) * gelu_slope(pre_gen)).astype(jnp.bfloat16)
    back_fake = (contract(cot_fake_group, down_full, 1, 1) * gelu_slope(pre_fake)).astype(
        jnp.bfloat16
    )
    out_grad_gen = contract(low_gen, back_gen, 0, 0)
    out_grad_fake = contract(low_fake, back_fake, 0, 0)
    mix_gen = contract(back_gen, gen_adapt_out, 1, 1)
    mix_fake = contract(back_fake, fake_adapt_out, 1, 1)
    in_grad_gen = lax.dot_general(
        u_gen.astype(jnp.float32),
        mix_gen,
        (((0,), (0,)), ((), ())),
        precision=lax.Precision.HIGHEST,
        preferred_element_type=jnp.float32,
    )
    in_grad_fake = lax.dot_general(
        u_score.astype(jnp.float32),
        mix_fake,
        (((0,), (0,)), ((), ())),
        precision=lax.Precision.HIGHEST,
        preferred_element_type=jnp.float32,
    )
    gen_grad_in, fake_grad_in = (
        lax.psum_scatter(in_grad_gen, ("dp", "mp"), scatter_dimension=0, tiled=True),
        lax.psum_scatter(in_grad_fake, ("dp", "mp"), scatter_dimension=0, tiled=True),
    )
    gen_grad_out, fake_grad_out = (
        lax.psum_scatter(
            out_grad_gen.astype(jnp.bfloat16), "dp", scatter_dimension=0, tiled=True
        ).astype(jnp.float32),
        lax.psum_scatter(
            out_grad_fake.astype(jnp.bfloat16), "dp", scatter_dimension=0, tiled=True
        ).astype(jnp.float32),
    )
    return (score_diff, gen_grad_in, gen_grad_out, fake_grad_in, fake_grad_out)


def solution(mesh):
    return jax.shard_map(
        local,
        mesh=mesh,
        in_specs=(
            P(("dp", "mp"), None),
            P(("dp", "mp"), None),
            P(),
            P(),
            P("dp", "mp"),
            P("mp", "dp"),
            P(),
            P(None, "mp"),
            P(),
            P(None, "mp"),
            P(),
            P(),
            P(),
        ),
        out_specs=(
            P(("dp", "mp"), None),
            P(("dp", "mp"), None),
            P("dp", "mp"),
            P(("dp", "mp"), None),
            P("dp", "mp"),
        ),
        check_vma=False,
    )
```

profile of v0, /device:TPU:0, one launch (start us, length us, event | category | flops | bytes accessed | tf_op | source)
XLA Modules:
  0.0 1278.0 jit_solution(7179291030866452118)
XLA Ops:
  7.2 0.0 all-gather.7.cloned.1.call-start
  7.2 0.7 all-gather.7.cloned.1.call-update
  7.9 0.0 all-gather.9.cloned.1.call-start
  8.0 0.7 all-gather.9.cloned.1.call-update
  8.7 0.0 all-gather.11.cloned.1.call-start
  8.7 0.7 all-gather.11.cloned.1.call-update
  9.4 0.0 reduce-scatter.10.cloned.1.call-start
  9.5 0.8 select_reduce_fusion
  10.3 18.5 %multiply_sine_fusion = (f32[384,1536]{1,0:T(8,128)}, f32[384,1536]{1,0:T(8,128)}, f32[384,1536]{1,0:T(8,128)}, f32[384,1536]{1,0:T(8,128)}) fusion(f32[384]{0:T(512)S(1)} %convert_element_type.135, f32[1536]{0:T(1024)S(1)} %multiply_exponential_fusion, f32[384]{0:T(512)S(1)} %convert_element_type.124), kind=kLoop, calls=%fused_computation.23 | loop fusion | flops 1179648 | bytes 9446400 | tf_op jit(solution)/shard_map/sin | solution.py:31
  28.8 14.4 %all-gather.7.cloned.1.call-done = bf16[384,3072]{1,0:T(8,128)(2,1)} async-done(((bf16[96,3072]{1,0:T(8,128)(2,1)}), bf16[384,3072]{1,0:T(8,128)(2,1)}) %all-gather.7.cloned.1.call-update) | async-done | bytes 2359312 | tf_op jit(solution)/shard_map/all_gather | solution.py:83
  43.2 2.4 fusion
  45.6 3.0 fusion.3
  48.7 0.8 convolution_convert_fusion.6
  49.5 108.4 %all-gather.9.cloned.1.call-done = bf16[3072,1536]{1,0:T(8,128)(2,1)} async-done(((bf16[96,1536]{1,0:T(8,128)(2,1)}), bf16[3072,1536]{1,0:T(8,128)(2,1)}) %all-gather.9.cloned.1.call-update) | async-done | bytes 9437200 | tf_op jit(solution)/shard_map/all_gather | solution.py:89
  157.9 6.3 fusion.63
  164.3 1.9 convolution_add_fusion.1
  166.2 103.3 %all-gather.11.cloned.1.call-done = bf16[1536,3072]{0,1:T(8,128)(2,1)} async-done(((bf16[1536,96]{0,1:T(8,128)(2,1)}), bf16[1536,3072]{0,1:T(8,128)(2,1)}) %all-gather.11.cloned.1.call-update) | async-done | bytes 9437200 | tf_op jit(solution)/shard_map/all_gather | solution.py:90
  269.5 9.7 convolution_convert_fusion.2
  279.2 0.0 reduce-scatter.10.cloned.1.call-update
  279.3 0.0 all-gather.13.cloned.1.call-start
  279.3 0.5 copy-done.19
  279.9 0.1 select_reduce_fusion.2
  280.0 27.7 %reduce-scatter.10.cloned.1.call-done = bf16[96,3072]{1,0:T(8,128)(2,1)} async-done(((bf16[384,3072]{1,0:T(8,128)(2,1)}), bf16[96,3072]{1,0:T(8,128)(2,1)}) %reduce-scatter.10.cloned.1.call-update) | async-done | bytes 589840 | tf_op jit(solution)/shard_map/reduce_scatter | solution.py:95
  307.7 2.4 fusion.26
  310.2 0.0 all-gather.13.cloned.1.call-update
  310.2 0.2 reduce-scatter.12.cloned.1.call-start
  310.4 31.9 %all-gather.13.cloned.1.call-done = bf16[384,3072]{1,0:T(8,128)(2,1)} async-done(((bf16[96,3072]{1,0:T(8,128)(2,1)}), bf16[384,3072]{1,0:T(8,128)(2,1)}) %all-gather.13.cloned.1.call-update) | async-done | bytes 2359312 | tf_op jit(solution)/shard_map/all_gather | solution.py:103
  342.3 2.4 fusion.4
  344.7 3.2 fusion.7
  347.9 0.8 convolution_convert_fusion.5
  348.8 2.0 copy-done.20
  350.8 3.8 fusion.64
  354.7 0.5 convolution_add_fusion
  355.2 0.9 copy-done.9
  356.1 1.4 copy-done.8
  357.5 5.4 convolution_convert_fusion.1
  362.9 0.0 reduce-scatter.14.cloned.1.call-start
  362.9 9.8 convolution_convert_fusion
  372.8 0.0 all-gather.17.cloned.1.call-start
  372.8 21.7 %reduce-scatter.12.cloned.1.call-done = bf16[96,3072]{1,0:T(8,128)(2,1)} async-done(((bf16[384,3072]{1,0:T(8,128)(2,1)}), bf16[96,3072]{1,0:T(8,128)(2,1)}) %reduce-scatter.12.cloned.1.call-update) | async-done | bytes 589840 | tf_op jit(solution)/shard_map/reduce_scatter | solution.py:119
  394.5 33.7 %reduce-scatter.14.cloned.1.call-done = bf16[96,3072]{1,0:T(8,128)(2,1)} async-done(((bf16[384,3072]{1,0:T(8,128)(2,1)}), bf16[96,3072]{1,0:T(8,128)(2,1)}) %reduce-scatter.14.cloned.1.call-update) | async-done | bytes 589840 | tf_op jit(solution)/shard_map/reduce_scatter | solution.py:116
  428.2 3.5 multiply_convert_fusion.4
  431.8 0.0 all-gather.15.cloned.1.call-start
  431.8 0.7 all-gather.15.cloned.1.call-update
  432.5 0.3 all-reduce.7.cloned.1.call-start
  432.8 31.2 %all-gather.17.cloned.1.call-done = bf16[384,3072]{1,0:T(8,128)(2,1)} async-done(((bf16[96,3072]{1,0:T(8,128)(2,1)}), bf16[384,3072]{1,0:T(8,128)(2,1)}) %all-gather.17.cloned.1.call-update) | async-done | bytes 2359312 | tf_op jit(solution)/shard_map/all_gather | solution.py:131
  463.9 9.6 fusion.9
  473.6 1.0 copy-done.7
  474.6 1.0 convolution_convert_fusion.3
  475.6 22.2 %all-gather.15.cloned.1.call-done = bf16[384,3072]{1,0:T(8,128)(2,1)} async-done(((bf16[96,3072]{1,0:T(8,128)(2,1)}), bf16[384,3072]{1,0:T(8,128)(2,1)}) %all-gather.15.cloned.1.call-update) | async-done | bytes 2359312 | tf_op jit(solution)/shard_map/all_gather | solution.py:130
  497.8 9.6 fusion.8
  507.4 1.0 copy-done.6
  508.4 1.0 convolution_convert_fusion.4
  509.5 0.0 reduce-scatter.18.cloned.1.call-start
  509.5 1.8 fusion.67
  511.3 5.3 fusion.68
  516.6 0.3 reduce-scatter.16.cloned.1.call-start
  517.0 1.8 fusion.65
  518.8 3.6 fusion.66
  522.5 0.6 dynamic-slice.1
  523.7 325.6 %all-reduce.7.cloned.1.call-done = (bf16[64,1536]{1,0:T(8,128)(2,1)}, bf16[64,1536]{1,0:T(8,128)(2,1)}) async-done(((bf16[64,1536]{1,0:T(8,128)(2,1)}, bf16[64,1536]{1,0:T(8,128)(2,1)}), (bf16[64,1536]{1,0:T(8,128)(2,1)}, bf16[64,1536]{1,0:T(8,128)(2,1)})) %all-reduce.7.cloned.1.call-update) | async-done | bytes 393232
  849.2 1.4 dynamic-slice_convert_fusion
  850.6 209.7 %reduce-scatter.18.cloned.1.call-done = f32[24,64]{1,0:T(8,128)} async-done(((f32[3072,64]{1,0:T(8,128)}), f32[24,64]{1,0:T(8,128)}) %reduce-scatter.18.cloned.1.call-update) | async-done | bytes 6160
  1060.3 210.9 %reduce-scatter.16.cloned.1.call-done = f32[24,64]{1,0:T(8,128)} async-done(((f32[3072,64]{1,0:T(8,128)}), f32[24,64]{1,0:T(8,128)}) %reduce-scatter.16.cloned.1.call-update) | async-done | bytes 6160
  (59 shorter events, 0.3 us)
Async XLA Ops:
  7.2 41.5 %copy-start = (bf16[3072,64]{0,1:T(8,128)(2,1)S(1)}, bf16[3072,64]{0,1:T(8,128)(2,1)}, u32[]{:S(2)}) copy-start(bf16[3072,64]{0,1:T(8,128)(2,1)} %param.19) | copy-start | bytes 1179652
  7.2 36.0 %all-gather.7.cloned.1.call-start = ((), (), s32[]{:S(2)}) async-start(), calls=%async_computation.5 | async-start | bytes 2949120 | tf_op jit(solution)/shard_map/all_gather | solution.py:83
  7.9 150.0 %all-gather.9.cloned.1.call-start = ((), (), s32[]{:S(2)}) async-start(), calls=%async_computation.6 | async-start | bytes 9732096 | tf_op jit(solution)/shard_map/all_gather | solution.py:89
  8.7 260.8 %all-gather.11.cloned.1.call-start = ((), (), s32[]{:S(2)}) async-start(), calls=%async_computation.7 | async-start | bytes 9732096 | tf_op jit(solution)/shard_map/all_gather | solution.py:90
  9.4 298.3 %reduce-scatter.10.cloned.1.call-start = ((), (), s32[]{:S(2)}) async-start(), calls=%async_computation.8 | async-start | bytes 2949120 | tf_op jit(solution)/shard_map/reduce_scatter | solution.py:95
  10.3 35.3 %copy-start.15 = (f32[3072]{0:T(1024)S(1)}, f32[3072]{0:T(1024)}, u32[]{:S(2)}) copy-start(f32[3072]{0:T(1024)} %param.24) | copy-start | bytes 36868
  10.3 35.3 %copy-start.16 = (f32[3072]{0:T(1024)S(1)}, f32[3072]{0:T(1024)}, u32[]{:S(2)}) copy-start(f32[3072]{0:T(1024)} %param.23) | copy-start | bytes 36868
  43.2 2.4 copy-start.4
  49.5 114.8 %copy-start.12 = (bf16[384,64]{0,1:T(8,128)(2,1)}, bf16[384,64]{0,1:T(8,128)(2,1)S(1)}, u32[]{:S(2)}) copy-start(bf16[384,64]{0,1:T(8,128)(2,1)S(1)} %convolution_convert_fusion.6) | copy-start | bytes 147460
  49.5 114.8 %copy-start.11 = (bf16[64,1536]{1,0:T(8,128)(2,1)S(1)}, bf16[64,1536]{1,0:T(8,128)(2,1)}, u32[]{:S(2)}) copy-start(bf16[64,1536]{1,0:T(8,128)(2,1)} %param.20) | copy-start | bytes 589828
  279.2 0.7 copy-start.19
  279.2 28.5 %copy-start.5 = (bf16[96,3072]{1,0:T(8,128)(2,1)S(1)}, bf16[96,3072]{1,0:T(8,128)(2,1)}, u32[]{:S(2)}) copy-start(bf16[96,3072]{1,0:T(8,128)(2,1)} %param.13) | copy-start | bytes 1769476
  279.2 28.5 %copy-start.18 = (f32[3072]{0:T(1024)S(1)}, f32[3072]{0:T(1024)}, u32[]{:S(2)}) copy-start(f32[3072]{0:T(1024)} %param.25) | copy-start | bytes 36868
  279.3 63.1 %all-gather.13.cloned.1.call-start = ((), (), s32[]{:S(2)}) async-start(), calls=%async_computation.9 | async-start | bytes 2949120 | tf_op jit(solution)/shard_map/all_gather | solution.py:103
  307.7 37.0 %copy-start.17 = (f32[3072]{0:T(1024)S(1)}, f32[3072]{0:T(1024)}, u32[]{:S(2)}) copy-start(f32[3072]{0:T(1024)} %param.23) | copy-start | bytes 36868
  310.2 84.3 %reduce-scatter.12.cloned.1.call-start = ((), (), s32[]{:S(2)}) async-start(), calls=%async_computation.10 | async-start | bytes 2949120 | tf_op jit(solution)/shard_map/reduce_scatter | solution.py:119
  342.3 2.4 copy-start.3
  344.7 3.2 copy-start.14
  344.7 6.1 copy-start.20
  347.9 6.7 copy-start.2
  347.9 9.6 slice-start
  350.8 3.9 copy-start.10
  350.8 6.7 slice-start.1
  350.8 6.7 slice-start.2
  354.7 1.4 copy-start.9
  356.1 1.4 copy-start.8
  362.9 65.3 %reduce-scatter.14.cloned.1.call-start = ((), (), s32[]{:S(2)}) async-start(), calls=%async_computation.11 | async-start | bytes 2949120 | tf_op jit(solution)/shard_map/reduce_scatter | solution.py:116
  372.8 91.2 %all-gather.17.cloned.1.call-start = ((), (), s32[]{:S(2)}) async-start(), calls=%async_computation.13 | async-start | bytes 2949120 | tf_op jit(solution)/shard_map/all_gather | solution.py:131
  431.8 66.0 %all-gather.15.cloned.1.call-start = ((), (), s32[]{:S(2)}) async-start(), calls=%async_computation.12 | async-start | bytes 2949120 | tf_op jit(solution)/shard_map/all_gather | solution.py:130
  432.5 416.7 %all-reduce.7.cloned.1.call-start = ((), (), s32[]{:S(2)}) async-start(), calls=%async_computation.16 | async-start | bytes 786432
  473.6 1.0 copy-start.7
  475.6 32.8 %copy-start.13 = (bf16[384,64]{0,1:T(8,128)(2,1)S(1)}, bf16[384,64]{0,1:T(8,128)(2,1)}, u32[]{:S(2)}) copy-start(bf16[384,64]{0,1:T(8,128)(2,1)} %copy-done.12) | copy-start | bytes 147460
  507.4 1.0 copy-start.6
  509.5 550.8 %reduce-scatter.18.cloned.1.call-start = ((), (), s32[]{:S(2)}) async-start(), calls=%async_computation.15 | async-start | bytes 1585152
  516.6 754.5 %reduce-scatter.16.cloned.1.call-start = ((), (), s32[]{:S(2)}) async-start(), calls=%async_computation.14 | async-start | bytes 1585152
  517.0 754.2 %copy-start.1 = (bf16[3072,64]{0,1:T(8,128)(2,1)S(1)}, bf16[3072,64]{0,1:T(8,128)(2,1)}, u32[]{:S(2)}) copy-start(bf16[3072,64]{0,1:T(8,128)(2,1)} %param.19) | copy-start | bytes 1179652
  518.8 3.6 copy-start.21
Sparse Core Ops, SparseCore 0:
  9.7 33.5 all-gather.6
  46.2 111.6 all-gather.8
  161.0 108.4 all-gather.10
  279.4 28.2 reduce-scatter.9
  310.3 31.9 all-gather.12
  363.0 31.4 reduce-scatter.11
  396.9 31.2 reduce-scatter.13
  431.9 31.9 all-gather.16
  465.6 32.1 all-gather.14
  509.6 339.6 all-reduce.6
  855.3 204.9 reduce-scatter.17
  1065.4 205.7 reduce-scatter.15
where the time goes:
time: 1280 us
  waiting for transfers between devices  1140 us (89%)
  matrix products  73 us (6%)
  other arithmetic  37.7 us (3%)
  between operations  15.2 us (1%)
    unnamed x15, waiting for transfers between devices  749 us
    all_gather x1, waiting for transfers between devices, local(): lax.all_gather(base_up, 'dp', axis=0, tiled=True)  108 us
    all_gather x1, waiting for transfers between devices, local(): lax.all_gather(base_down, 'dp', axis=1, tiled=True)  103 us
    dot_general x9, matrix products, matmul(): return jnp.dot(left, right, preferred_element_type=jnp.float32)  39.2 us
    reduce_scatter x1, waiting for transfers between devices, local(): lax.psum_scatter(matmul(act_real, down_full).astype(jnp.bfloat16), 'mp',...  33.7 us
    all_gather x1, waiting for transfers between devices, local(): noised_group = lax.all_gather(noised, 'mp', axis=0, tiled=True)  31.9 us
    all_gather x1, waiting for transfers between devices, local(): lax.all_gather(cot_fake, 'mp', axis=0, tiled=True)  31.2 us
    reduce_scatter x1, waiting for transfers between devices, local(): lax.psum_scatter(out_gen.astype(jnp.bfloat16), 'mp', scatter_dimension=0,...  27.7 us
  transfers between devices with their start and end apart: 12, of which 12 were waited for; matrix products, arithmetic and copies ran while one was open for 5% of the time, Pallas kernels for 0%

commit v1 on v0

v1 whole, which is shorter than its diff:
```python
import math

import jax
import jax.numpy as jnp
from jax import lax
from jax.sharding import Mesh
from jax.sharding import PartitionSpec as P

IMG_TOK = 1024
AXES = ("z", "y", "xh", "xl", "core")
CHIPS = ("z", "y", "xh", "xl")

gelu_coef = 0.044715
root_two_pi = math.sqrt(2.0 / math.pi)


def gelu_value(pre):
    inner_arg = root_two_pi * (pre + gelu_coef * pre * pre * pre)
    return 0.5 * pre * (1.0 + jnp.tanh(inner_arg))


def gelu_slope(pre):
    tanh_val = jnp.tanh(root_two_pi * (pre + gelu_coef * pre * pre * pre))
    return 0.5 * (1.0 + tanh_val) + 0.5 * pre * (1.0 - tanh_val * tanh_val) * root_two_pi * (
        1.0 + 3.0 * gelu_coef * pre * pre
    )


def embedding(steps, feature_count):
    half_width = feature_count // 2
    frequency = jnp.exp(-math.log(10000.0) * jnp.arange(half_width, dtype=jnp.float32) / half_width)
    phase_angle = steps.astype(jnp.float32)[:, None] * frequency[None, :]
    return jnp.concatenate([jnp.sin(phase_angle), jnp.cos(phase_angle)], axis=1)


def modulate(rows, scale_rows, shift_rows):
    widened = rows.astype(jnp.float32)
    normed = widened * lax.rsqrt(jnp.mean(widened * widened, axis=1, keepdims=True) + 1e-06)
    return (normed * scale_rows + shift_rows).astype(jnp.bfloat16)


def matmul(left, right):
    return jnp.dot(left, right, preferred_element_type=jnp.float32)


def contract(left, right, left_dim, right_dim):
    return lax.dot_general(
        left, right, (((left_dim,), (right_dim,)), ((), ())), preferred_element_type=jnp.float32
    )


def swap_cores(value):
    return lax.ppermute(value, "core", [(0, 1), (1, 0)])


def three_terms(value):
    high = lax.reduce_precision(value, 8, 7)
    rest = value - high
    middle = lax.reduce_precision(rest, 8, 7)
    low = rest - middle
    return jnp.concatenate([high, middle, low], axis=1).astype(jnp.bfloat16)


def local(
    gen_input,
    noise_score,
    gen_steps,
    score_steps,
    base_up,
    base_down,
    gen_adapt_in,
    gen_adapt_out,
    fake_adapt_in,
    fake_adapt_out,
    modulation_scale,
    modulation_shift,
    output_gate,
):
    bf16, f32 = jnp.bfloat16, jnp.float32
    shard_rows, width = gen_input.shape
    hidden = base_up.shape[1]
    rank = gen_adapt_in.shape[1]
    image_count = gen_steps.shape[0]
    loss_scale = 1.0 / math.sqrt(image_count * IMG_TOK)
    core = lax.axis_index("core")
    xl = lax.axis_index("xl")
    first_row = lax.axis_index(AXES) * shard_rows
    first_image = first_row // IMG_TOK
    last_image = (first_row + shard_rows - 1) // IMG_TOK
    row_ids = first_row + jnp.arange(shard_rows, dtype=jnp.int32)
    in_last = (row_ids >= last_image * IMG_TOK)[:, None]

    def two_steps(steps):
        return jnp.stack([steps[first_image], steps[last_image]])

    def modulation(steps):
        embed = embedding(two_steps(steps), width)
        scale = 1.0 + modulation_scale[None, :] * embed
        shift = modulation_shift[None, :] * embed
        return (
            jnp.where(in_last, scale[1:], scale[:1]),
            jnp.where(in_last, shift[1:], shift[:1]),
        )

    def both_rows(mine):
        return jnp.concatenate([mine, swap_cores(mine)], axis=0)

    up_all = lax.all_gather(base_up, ("xl", "z", "y", "xh"), axis=0, tiled=True)
    down_all = lax.all_gather(base_down.T, ("xl", "z", "y", "xh"), axis=0, tiled=True)
    up_all = up_all.reshape(2, width, hidden)
    down_all = down_all.reshape(2, width, hidden)

    def other_quarter(mine):
        theirs = lax.ppermute(mine, "xl", [(0, 1), (1, 0)])
        return jnp.stack([jnp.where(xl == 0, mine, theirs), jnp.where(xl == 0, theirs, mine)])

    adapt_out = other_quarter(jnp.concatenate([gen_adapt_out, fake_adapt_out], axis=0))
    gen_out, fake_out = adapt_out[:, :rank], adapt_out[:, rank:]

    u_mine = modulate(gen_input, *modulation(gen_steps))
    u_gen = both_rows(u_mine)
    low_gen = matmul(u_gen, gen_adapt_in).astype(bf16)
    pre_gen = [matmul(u_gen, up_all[q]) + matmul(low_gen, gen_out[q]) for q in range(2)]
    act_gen = [gelu_value(p).astype(bf16) for p in pre_gen]

    def down(acts):
        return contract(acts[0], down_all[0], 1, 1) + contract(acts[1], down_all[1], 1, 1)

    out_gen = down(act_gen)
    out_mine = out_gen[:shard_rows] + swap_cores(out_gen[shard_rows:].astype(bf16)).astype(f32)
    latents = (gen_input.astype(f32) + output_gate * out_mine).astype(bf16)
    two_blend = (two_steps(score_steps).astype(f32) + 0.5) / 1000.0
    blend = jnp.where(in_last, two_blend[1], two_blend[0])
    noised = ((1.0 - blend) * latents.astype(f32) + blend * noise_score.astype(f32)).astype(bf16)
    u_score = both_rows(modulate(noised, *modulation(score_steps)))
    low_fake = matmul(u_score, fake_adapt_in).astype(bf16)
    pre_real = [matmul(u_score, up_all[q]) for q in range(2)]
    pre_fake = [pre_real[q] + matmul(low_fake, fake_out[q]) for q in range(2)]
    acts = [
        jnp.concatenate([gelu_value(pre_real[q]), gelu_value(pre_fake[q])], axis=0).astype(bf16)
        for q in range(2)
    ]
    outs = down(acts)
    parts = [outs[i * shard_rows : (i + 1) * shard_rows] for i in range(4)]
    got = swap_cores(jnp.concatenate([parts[1], parts[3]], axis=0).astype(bf16)).astype(f32)
    out_real = parts[0] + got[:shard_rows]
    out_fake = parts[2] + got[shard_rows:]
    score_diff = (output_gate * (out_fake - out_real)).astype(bf16)
    cot_gen = (output_gate * score_diff.astype(f32) * loss_scale).astype(bf16)
    target = noise_score.astype(f32) - latents.astype(f32)
    cot_fake = (
        output_gate * (noised.astype(f32) + output_gate * out_fake - target) * loss_scale
    ).astype(bf16)
    cots = jnp.concatenate([cot_gen, cot_fake], axis=0)
    cots_other = swap_cores(cots)
    cots = jnp.concatenate(
        [cot_gen, cots_other[:shard_rows], cot_fake, cots_other[shard_rows:]], axis=0
    )
    group = 2 * shard_rows
    backs = [matmul(cots, down_all[q]) for q in range(2)]
    back_gen = [(backs[q][:group] * gelu_slope(pre_gen[q])).astype(bf16) for q in range(2)]
    back_fake = [(backs[q][group:] * gelu_slope(pre_fake[q])).astype(bf16) for q in range(2)]

    def out_grad(low, back):
        return [contract(low, back[q], 0, 0) for q in range(2)]

    def mixed(back, adapter):
        return contract(back[0], adapter[0], 1, 1) + contract(back[1], adapter[1], 1, 1)

    mix = jnp.concatenate([mixed(back_gen, gen_out), mixed(back_fake, fake_out)], axis=1)
    mix_other = swap_cores(mix)
    mix = mix + jnp.concatenate([mix_other[shard_rows:], mix_other[:shard_rows]], axis=0)

    def in_grad(u, mix_part):
        product = contract(u, three_terms(mix_part), 0, 0)
        total = product[:, :rank] + product[:, rank : 2 * rank] + product[:, 2 * rank :]
        chips = total.reshape(-1, 2, width // 128, rank)
        return jnp.where(core == 0, chips[:, 0], chips[:, 1])

    in_grads = jnp.concatenate([in_grad(u_gen, mix[:, :rank]), in_grad(u_score, mix[:, rank:])], axis=2)
    chips, in_rows = in_grads.shape[0], in_grads.shape[1]
    groups = chips // 2
    out_grads = jnp.stack(
        [jnp.stack(out_grad(low_gen, back_gen)), jnp.stack(out_grad(low_fake, back_fake))]
    )
    out_grads = out_grads.reshape(2, 2, groups, rank // groups, hidden).transpose(2, 1, 0, 3, 4)
    out_rows = 2 * (rank // groups) * hidden // 128
    packed = jnp.concatenate(
        [in_grads.astype(bf16), out_grads.astype(bf16).reshape(chips, out_rows, 128)], axis=1
    )
    received = lax.all_to_all(packed, CHIPS, 0, 0, tiled=True)
    summed = jnp.sum(received.astype(f32), axis=0)
    gen_grad_in, fake_grad_in = summed[:in_rows, :rank], summed[:in_rows, rank:]
    grads_out = summed[in_rows:].reshape(2, rank // groups, hidden)
    return (score_diff, gen_grad_in, grads_out[0], fake_grad_in, grads_out[1])


def solution(mesh):
    fine = Mesh(mesh.devices.reshape(4, 4, 2, 2, 2), AXES)
    dp, mp = ("z", "y", "xh"), ("xl", "core")
    return jax.shard_map(
        local,
        mesh=fine,
        in_specs=(
            P(AXES, None),
            P(AXES, None),
            P(),
            P(),
            P(dp, mp),
            P(mp, dp),
            P(),
            P(None, mp),
            P(),
            P(None, mp),
            P(),
            P(),
            P(),
        ),
        out_specs=(
            P(AXES, None),
            P(AXES, None),
            P(dp, mp),
            P(AXES, None),
            P(dp, mp),
        ),
        check_vma=False,
    )
```

time: 1280 us -> 1220 us (0.953)
  waiting for transfers between devices: 1140 us -> 1070 us
  blocking collectives: 0 us -> 25.6 us
  other arithmetic: 37.7 us -> 16.3 us
    unnamed x15 -> x2, waiting for transfers between devices: 749 us -> 1.38 us
    all_gather x6 -> x2, waiting for transfers between devices: 311 us -> 1060 us  [the longest x1 554 us: local(): lax.all_gather(base_down.T, ('xl', 'z', 'y', 'xh'), axis=0, tiled=True)]
    reduce_scatter x3 -> x0, waiting for transfers between devices: 83.1 us -> none  [the longest x1 33.7 us: local(): lax.psum_scatter(matmul(act_real, down_full).astype(jnp.bfloat16), 'mp',...]
    all_to_all x0 -> x1, blocking collectives: none -> 25.6 us  [local(): received = lax.all_to_all(packed, CHIPS, 0, 0, tiled=True)]
    sin x1, other arithmetic: 18.5 us -> 0.43 us  [embedding(): return jnp.concatenate([jnp.sin(phase_angle), jnp.cos(phase_angle)], axis=1)]
    dot_general x6 -> x14, matrix products: 24.9 us -> 31.8 us  [contract(): lax.dot_general(left, right, (((left_dim,), (right_dim,)), ((), ())), pre...]
    dot_general x9 -> x12, matrix products: 39.2 us -> 41.8 us  [matmul(): return jnp.dot(left, right, preferred_element_type=jnp.float32)]
  transfers between devices with their start and end apart: 12 -> 9, of which waited for: 12 -> 7; matrix products, arithmetic and copies ran while one was open for 5% -> 2% of each run, Pallas kernels for 0% -> 0%
where the time goes in v1:
time: 1220 us; the launch traced here: 1210 us
  waiting for transfers between devices  1070 us (88%)
  matrix products  73.6 us (6%)
  blocking collectives  25.6 us (2%)
  other arithmetic  16.3 us (1%)
  between operations  14.8 us (1%)
    all_gather x1, waiting for transfers between devices, local(): lax.all_gather(base_down.T, ('xl', 'z', 'y', 'xh'), axis=0, tiled=True)  554 us
    all_gather x1, waiting for transfers between devices, local(): up_all = lax.all_gather(base_up, ('xl', 'z', 'y', 'xh'), axis=0, tiled=True)  504 us
    dot_general x12, matrix products, matmul(): return jnp.dot(left, right, preferred_element_type=jnp.float32)  41.8 us
    dot_general x14, matrix products, contract(): lax.dot_general(left, right, (((left_dim,), (right_dim,)), ((), ())), pre...  31.8 us
    all_to_all x1, blocking collectives, local(): received = lax.all_to_all(packed, CHIPS, 0, 0, tiled=True)  25.6 us
  transfers between devices with their start and end apart: 9, of which 7 were waited for; matrix products, arithmetic and copies ran while one was open for 2% of the time, Pallas kernels for 0%

profile of v1, /device:TPU:0, one launch (start us, length us, event | category | flops | bytes accessed | tf_op | source)
XLA Modules:
  0.0 1214.9 jit_solution(12654068995471322442)
XLA Ops:
  7.3 0.7 all-gather.3.cloned.1.call-update
  8.0 0.7 all-gather.5.cloned.1.call-update
  8.7 0.9 constant_dynamic-update-slice_fusion.1
  9.7 0.9 constant_dynamic-update-slice_fusion
  10.6 1.7 collective-permute-start.1
  12.3 0.6 fusion.151
  12.9 1.4 add_convert_fusion.1
  14.2 1.4 add_multiply_fusion
  15.6 0.6 fusion.152
  16.2 1.8 broadcast_subtract_fusion
  18.2 0.4 multiply_sine_fusion
  18.7 0.7 multiply_add_fusion.7
  19.4 0.3 fusion.41
  19.8 0.6 fusion.148
  20.4 1.0 collective-permute-done.1
  21.5 1.1 select_bitcast_fusion.1
  22.6 0.5 convolution_convert_fusion.5
  23.4 0.3 fusion.109
  24.0 1.3 fusion.107
  25.3 504.2 %all-gather.3.cloned.1.call-done = bf16[6144,1536]{1,0:T(8,128)(2,1)} async-done(((bf16[96,1536]{1,0:T(8,128)(2,1)}), bf16[6144,1536]{1,0:T(8,128)(2,1)}) %all-gather.3.cloned.1.call-update) | async-done | bytes 18874384 | tf_op jit(solution)/shard_map/all_gather | solution.py:108
  529.5 7.0 fusion.29
  536.5 5.8 fusion.26
  542.3 554.3 %all-gather.5.cloned.1.call-done = bf16[6144,1536]{1,0:T(8,128)(2,1)} async-done(((bf16[96,1536]{1,0:T(8,128)(2,1)}), bf16[6144,1536]{1,0:T(8,128)(2,1)}) %all-gather.5.cloned.1.call-update) | async-done | bytes 18874384 | tf_op jit(solution)/shard_map/all_gather | solution.py:109
  1096.5 6.1 fusion.12
  1102.7 5.9 fusion.23
  1108.8 0.5 copy-done.19
  1109.4 1.5 collective-permute-done.2
  1110.9 0.7 fusion.47
  1111.5 0.3 fusion.50
  1111.9 0.4 collective-permute-start.3
  1112.3 1.9 collective-permute-done.3
  1114.2 5.6 fusion.62
  1119.8 0.5 convolution_convert_fusion.4
  1120.3 1.7 multiply_convert_fusion.1
  1122.0 2.1 fusion.55
  1124.1 1.7 multiply_convert_fusion.2
  1125.8 6.4 fusion.10
  1132.2 9.6 fusion.154
  1142.3 2.7 collective-permute-done.4
  1145.2 1.5 multiply_convert_fusion
  1146.8 1.1 pad_maximum_fusion.4
  1148.0 3.1 collective-permute-done.5
  1151.1 1.3 fusion.143
  1152.4 7.6 fusion.8
  1160.1 1.5 fusion.74
  1162.0 0.9 convolution_convert_fusion.2
  1162.9 0.3 fusion.110
  1163.4 7.6 fusion.14
  1171.1 1.5 fusion.69
  1172.9 0.3 convolution_add_fusion.2
  1173.4 0.3 convolution_add_fusion.3
  1174.0 0.4 copy-done.11
  1174.7 1.2 maximum_bitcast_fusion
  1175.8 0.5 reshape.126
  1176.6 0.8 copy-done.14
  1177.4 0.5 fusion.111
  1178.0 0.4 copy.22
  1178.4 0.7 copy-done.16
  1179.0 0.5 fusion.117
  1179.6 0.4 copy.23
  1180.4 25.6 %all_to_all.5 = bf16[64,72,128]{2,1,0:T(8,128)(2,1)S(1)} all-to-all(bf16[64,72,128]{2,1,0:T(8,128)(2,1)S(1)} %pad_maximum_fusion.5), channel_id=1, replica_groups=mesh['z'=4,'y'=4,'xh'=2,'xl'=2,'core'=2] {'z','y','xh','xl'}, dimensions={0} | all-to-all | bytes 2359296 | tf_op jit(solution)/shard_map/all_to_all | solution.py:191
  1206.2 0.7 fusion.146
  1206.9 0.6 squeeze.23
  1207.5 0.6 squeeze.22
  (104 shorter events, 4.6 us)
Async XLA Ops:
  7.2 15.4 %copy-start = (bf16[3072,64]{0,1:T(8,128)(2,1)S(1)}, bf16[3072,64]{0,1:T(8,128)(2,1)}, u32[]{:S(2)}) copy-start(bf16[3072,64]{0,1:T(8,128)(2,1)} %param.19) | copy-start | bytes 1179652
  7.2 5.1 copy-start.27
  7.2 5.1 copy-start.26
  7.2 10.8 copy-start.2
  7.2 11.5 copy-start.23
  7.2 11.5 copy-start.22
  7.2 522.2 %all-gather.3.cloned.1.call-start = ((), (), s32[]{:S(2)}) async-start(), calls=%async_computation.1 | async-start | bytes 19169280 | tf_op jit(solution)/shard_map/all_gather | solution.py:108
  8.0 1088.5 %all-gather.5.cloned.1.call-start = ((), (), s32[]{:S(2)}) async-start(), calls=%async_computation.2 | async-start | bytes 19169280 | tf_op jit(solution)/shard_map/all_gather | solution.py:109
  10.6 10.9 collective-permute-start.1
  19.7 2.8 collective-permute-start
  22.6 0.8 copy-start.12
  23.4 0.6 copy-start.17
  529.5 7.0 copy-start.4
  529.5 7.0 copy-start.13
  542.3 560.4 %copy-start.6 = (f32[192,1536]{1,0:T(8,128)}, f32[192,1536]{1,0:T(8,128)S(1)}, u32[]{:S(2)}) copy-start(f32[192,1536]{1,0:T(8,128)S(1)} %fusion.26) | copy-start | bytes 3538948
  1102.6 19.3 %slice-start = ((s8[18874368]{0:T(1024)(128)(4,1)}), s8[2097152]{0:T(1024)(128)(4,1)S(1)}, s32[]{:S(2)}) async-start(s8[18874368]{0:T(1024)(128)(4,1)} %bitcast.80), calls=%async_computation.3 | async-start | bytes 4194304
  1102.7 19.3 %slice-start.1 = ((s8[18874368]{0:T(1024)(128)(4,1)}), s8[4194304]{0:T(1024)(128)(4,1)S(1)}, s32[]{:S(2)}) async-start(s8[18874368]{0:T(1024)(128)(4,1)} %bitcast.80), calls=%async_computation.4 | async-start | bytes 8388608
  1108.6 0.7 copy-start.19
  1108.6 2.2 copy-start.3
  1108.6 2.2 copy-start.21
  1108.6 2.2 copy-start.24
  1108.6 2.2 copy-start.25
  1108.7 2.1 collective-permute-start.2
  1110.8 0.7 copy-start.20
  1110.8 11.2 slice-start.2
  1111.9 7.9 copy-start.28
  1111.9 10.1 slice-start.3
  1111.9 10.1 slice-start.4
  1111.9 2.3 collective-permute-start.3
  1114.2 7.8 copy-start.15
  1142.0 3.3 copy-start.5
  1142.1 2.9 collective-permute-start.4
  1147.9 3.2 collective-permute-start.5
  1152.4 7.7 copy-start.8
  1152.4 7.7 copy-start.10
  1160.1 1.9 copy-start.18
  1163.4 7.7 copy-start.7
  1163.4 7.7 copy-start.9
  1173.4 0.9 copy-start.11
  1174.4 1.9 collective-permute-start.6
  1176.3 1.1 copy-start.14
  1178.0 1.1 copy-start.16
  1180.3 27.7 %copy-start.1 = (bf16[3072,64]{0,1:T(8,128)(2,1)S(1)}, bf16[3072,64]{0,1:T(8,128)(2,1)}, u32[]{:S(2)}) copy-start(bf16[3072,64]{0,1:T(8,128)(2,1)} %param.19) | copy-start | bytes 1179652
Sparse Core Ops, SparseCore 0:
  9.7 519.6 all-gather.2
  531.1 565.3 all-gather.4

commit v2 on v1

--- a/solution.py
+++ b/solution.py
@@ -3,6 +3,8 @@
 import jax
 import jax.numpy as jnp
 from jax import lax
+from jax.experimental import pallas as pl
+from jax.experimental.pallas import tpu as pltpu
 from jax.sharding import Mesh
 from jax.sharding import PartitionSpec as P
 
@@ -51,6 +53,107 @@
 
 def swap_cores(value):
     return lax.ppermute(value, "core", [(0, 1), (1, 0)])
+
+
+RING_AXES = (("y", "z", "x"), ("z", "x", "y"), ("x", "y", "z"))
+RING = 4
+
+
+def chip_ring(axis):
+    pairs = []
+    for device in range(128):
+        place = {"z": device // 32, "y": device // 8 % 4, "x": device // 2 % 4, "core": device % 2}
+        step = 1 if place["core"] == 0 else -1
+        place[axis] = (place[axis] + step) % RING
+        target = place["z"] * 32 + place["y"] * 8 + place["x"] * 2 + place["core"]
+        pairs.append((device, target))
+    return pairs
+
+
+def ring_slots(pieces):
+    for phase in range(3):
+        slots = [[piece] for piece in pieces]
+        for _ in range(RING - 1):
+            for i, held in enumerate(slots):
+                held.append(lax.ppermute(held[-1], AXES, chip_ring(RING_AXES[i][phase])))
+        if phase < 2:
+            pieces = [jnp.concatenate(held, axis=0) for held in slots]
+    return slots
+
+
+def place_kernel(steps, whole, place_ref, *refs):
+    count = 3 * len(steps)
+    slots, rest = refs[:count], refs[count:]
+    whole_ref = rest[0] if whole else None
+    up_ref, down_ref, sems = rest[-3:]
+    me = {"z": place_ref[0], "y": place_ref[1], "x": place_ref[2]}
+    direction = place_ref[3]
+    targets = ((up_ref, 0), (up_ref, 1), (down_ref, 0))
+
+    def source(axis, step):
+        return lax.rem(me[axis] - step * direction + RING, RING)
+
+    def where(axis_steps):
+        at = {axis: source(axis, step) for axis, step in axis_steps}
+        quarter = lax.rem(at["x"], 2)
+        group = (at["z"] * 4 + at["y"]) * 2 + at["x"] // 2
+        return quarter, group
+
+    if whole:
+        for quarter in range(2):
+            pltpu.make_async_copy(
+                whole_ref.at[:, quarter], down_ref.at[quarter, :, 1], sems.at[count + quarter]
+            ).start()
+    for n, step in enumerate(steps):
+        for i in range(3):
+            first, second, third = RING_AXES[i]
+            target, part = targets[i]
+            slot = slots[n * 3 + i]
+            for t in range(RING):
+                for u in range(RING):
+                    quarter, group = where(((first, u), (second, t), (third, step)))
+                    pltpu.make_async_copy(
+                        slot.at[t * RING + u], target.at[quarter, group, part], sems.at[n * 3 + i]
+                    ).start()
+    if whole:
+        for quarter in range(2):
+            pltpu.make_async_copy(
+                whole_ref.at[:, quarter], down_ref.at[quarter, :, 1], sems.at[count + quarter]
+            ).wait()
+    for n in range(len(steps)):
+        for i in range(3):
+            target, part = targets[i]
+            slot = slots[n * 3 + i]
+            pltpu.make_async_copy(
+                slot, target.at[0, pl.ds(0, 16), part], sems.at[n * 3 + i]
+            ).wait()
+
+
+def place(steps, slots, whole, placed, coords):
+    flat = [slots[i][step] for step in steps for i in range(3)]
+    rows, hidden = flat[0].shape[0] // 16, flat[0].shape[1]
+    flat = [x.reshape(16, rows, hidden) for x in flat]
+    shape = jax.ShapeDtypeStruct((2, 32, 2, rows, hidden), flat[0].dtype)
+    extra = [] if whole is None else [whole.reshape(32, 2, rows, hidden)]
+    kept = [] if placed is None else list(placed)
+    count = 1 + len(flat) + len(extra)
+    anywhere = pl.BlockSpec(memory_space=pl.ANY)
+
+    def body(place_ref, *refs):
+        inputs = refs[: len(flat) + len(extra)]
+        outputs = refs[len(flat) + len(extra) + len(kept) :]
+        place_kernel(steps, whole is not None, place_ref, *inputs, *outputs)
+
+    moved = 2 * 2 * rows * hidden * (16 * len(flat) + 64 * len(extra))
+    return pl.pallas_call(
+        body,
+        out_shape=(shape, shape),
+        in_specs=[pl.BlockSpec(memory_space=pltpu.SMEM)] + [anywhere] * (count - 1 + len(kept)),
+        out_specs=(anywhere, anywhere),
+        scratch_shapes=[pltpu.SemaphoreType.DMA((len(flat) + 2,))],
+        input_output_aliases={count: 0, count + 1: 1} if kept else {},
+        cost_estimate=pl.CostEstimate(flops=0, bytes_accessed=moved, transcendentals=0),
+    )(coords, *flat, *extra, *kept)
 
 
 def three_terms(value):
@@ -105,8 +208,20 @@
     def both_rows(mine):
         return jnp.concatenate([mine, swap_cores(mine)], axis=0)
 
-    up_all = lax.all_gather(base_up, ("xl", "z", "y", "xh"), axis=0, tiled=True)
-    down_all = lax.all_gather(base_down.T, ("xl", "z", "y", "xh"), axis=0, tiled=True)
+    coords = jnp.stack(
+        [
+            lax.axis_index("z"),
+            lax.axis_index("y"),
+            lax.axis_index("xh") * 2 + xl,
+            1 - 2 * core,
+        ]
+    ).astype(jnp.int32)
+    down_rows = base_down.T
+    half = base_up.shape[0] // 2
+    last_quarter = lax.all_gather(down_rows[half:], CHIPS, axis=0, tiled=True)
+    slots = ring_slots([base_up[:half], base_up[half:], down_rows[:half]])
+    placed = place((0, 1, 2), slots, last_quarter, None, coords)
+    up_all, down_all = place((3,), slots, None, placed, coords)
     up_all = up_all.reshape(2, width, hidden)
     down_all = down_all.reshape(2, width, hidden)
 

time: 1220 us -> 1510 us (1.24)
  Pallas kernels: 0 us -> 1150 us
  waiting for transfers between devices: 1070 us -> 140 us
  local copies, waits for them, and re-layouts: 11.8 us -> 44.1 us
  starting transfers between devices: 2.85 us -> 26.5 us
    pallas_call x0 -> x2, Pallas kernels: none -> 1150 us  [place(): pl.pallas_call(body, out_shape=(shape, shape), in_specs=[pl.BlockSpec(mem...]
    all_gather x2 -> x1, waiting for transfers between devices: 1060 us -> 0.01 us  [local(): last_quarter = lax.all_gather(down_rows[half:], CHIPS, axis=0, tiled=True)]
    ppermute x0 -> x27, waiting for transfers between devices: none -> 101 us  [ring_slots(): held.append(lax.ppermute(held[-1], AXES, chip_ring(RING_AXES[i][phase])))]
    ppermute x1, waiting for transfers between devices: 1.04 us -> 29.8 us  [other_quarter(): theirs = lax.ppermute(mine, 'xl', [(0, 1), (1, 0)])]
    ppermute x0 -> x27, starting transfers between devices: none -> 23 us  [ring_slots(): held.append(lax.ppermute(held[-1], AXES, chip_ring(RING_AXES[i][phase])))]
    slice x0 -> x3, local copies, waits for them, and re-layouts: none -> 22.6 us  [the longest x1 19.1 us: local(): up_all[q]]
  transfers between devices with their start and end apart: 9 -> 35, of which waited for: 7 -> 23; matrix products, arithmetic and copies ran while one was open for 2% -> 2% of each run, Pallas kernels for 0% -> 62%
where the time goes in v2:
time: 1510 us; the launch traced here: 1500 us
  Pallas kernels  1150 us (76%)
  waiting for transfers between devices  140 us (9%)
  matrix products  79.5 us (5%)
  local copies, waits for them, and re-layouts  44.1 us (3%)
  blocking collectives  28.2 us (2%)
  starting transfers between devices  26.5 us (2%)
  other arithmetic  19.8 us (1%)
  between operations  15.4 us (1%)
    pallas_call x2, Pallas kernels, place(): pl.pallas_call(body, out_shape=(shape, shape), in_specs=[pl.BlockSpec(mem...  1150 us
    ppermute x27, waiting for transfers between devices, ring_slots(): held.append(lax.ppermute(held[-1], AXES, chip_ring(RING_AXES[i][phase])))  101 us
    dot_general x12, matrix products, matmul(): return jnp.dot(left, right, preferred_element_type=jnp.float32)  45.9 us
    dot_general x14, matrix products, contract(): lax.dot_general(left, right, (((left_dim,), (right_dim,)), ((), ())), pre...  33.6 us
  transfers between devices with their start and end apart: 35, of which 23 were waited for; matrix products, arithmetic and copies ran while one was open for 2% of the time, Pallas kernels for 62%

profile of v2, /device:TPU:0, one launch (start us, length us, event | category | flops | bytes accessed | tf_op | source)
XLA Modules:
  0.0 1501.2 jit_solution(2917907231496329193)
XLA Ops:
  7.2 1.8 fusion.120
  9.0 1.7 fusion.121
  10.7 1.7 collective-permute-start.1
  12.4 1.9 collective-permute-start.10
  14.3 1.5 collective-permute-start.19
  15.8 1.3 collective-permute-done.1
  17.5 2.0 collective-permute-done.10
  23.9 1.9 collective-permute-done.11
  28.7 1.6 collective-permute-done.3
  30.3 1.9 collective-permute-start.4
  32.3 1.6 collective-permute-start.13
  33.9 2.1 collective-permute-start.22
  37.3 5.1 collective-permute-done.4
  43.6 1.2 collective-permute-start.14
  46.8 11.5 collective-permute-done.5
  59.6 2.1 collective-permute-start.15
  63.0 6.4 collective-permute-done.6
  70.2 2.6 collective-permute-start.7
  72.9 1.2 collective-permute-start.16
  74.0 2.3 collective-permute-done.24
  77.2 1.3 fusion.129
  78.6 1.4 add_convert_fusion.1
  79.9 1.4 add_multiply_fusion
  82.5 1.4 multiply_add_fusion.7
  83.9 37.9 %collective-permute-done.7 = bf16[768,1536]{1,0:T(8,128)(2,1)} collective-permute-done((bf16[768,1536]{1,0:T(8,128)(2,1)}, bf16[768,1536]{1,0:T(8,128)(2,1)}, u32[]{:S(2)}, u32[]{:S(2)}) %collective-permute-start.7) | collective-permute-done | bytes 2359328 | tf_op jit(solution)/shard_map/ppermute | solution.py:78
  122.3 1.3 collective-permute-done.16
  124.4 1.9 broadcast_subtract_fusion
  126.4 1.2 fusion.9
  128.5 23.7 %collective-permute-done.8 = bf16[768,1536]{1,0:T(8,128)(2,1)} collective-permute-done((bf16[768,1536]{1,0:T(8,128)(2,1)}, bf16[768,1536]{1,0:T(8,128)(2,1)}, u32[]{:S(2)}, u32[]{:S(2)}) %collective-permute-start.8) | collective-permute-done | bytes 2359328 | tf_op jit(solution)/shard_map/ppermute | solution.py:78
  152.2 1.8 collective-permute-done.17
  155.0 1.2 collective-permute-start.28
  157.4 29.8 %collective-permute-done.28 = bf16[128,1536]{1,0:T(8,128)(2,1)S(1)} collective-permute-done((bf16[128,1536]{1,0:T(8,128)(2,1)S(1)}, bf16[128,1536]{1,0:T(8,128)(2,1)S(1)}, u32[]{:S(2)}, u32[]{:S(2)}) %collective-permute-start.28) | collective-permute-done | bytes 393248 | tf_op jit(solution)/shard_map/ppermute | solution.py:229
  187.3 2.0 convolution_convert_fusion.5
  189.3 1.4 fusion.79
  190.7 1.4 fusion.81
  192.1 931.0 %shard_map.164 = (bf16[2,32,2,48,1536]{4,3,2,1,0:T(8,128)(2,1)}, bf16[2,32,2,48,1536]{4,3,2,1,0:T(8,128)(2,1)}) custom-call(s32[4]{0:T(128)} %pad_add_fusion.place_ref, bf16[16,48,1536]{2,1,0:T(8,128)(2,1)} %bitcast.14.refs_0_, bf16[16,48,1536]{2,1,0:T(8,128)(2,1)} %bitcast.115, bf16[16,48,1536]{2,1,0:T(8,128)(2,1)} %bitcast.16.refs_2_, ...), custom_call_target="tpu_custom_call" | custom-call | bytes 61341696 | tf_op jit(solution)/shard_map/pallas_call | solution.py:148
  1123.1 1.4 copy-done.12
  1124.5 216.2 %shard_map.165 = (bf16[2,32,2,48,1536]{4,3,2,1,0:T(8,128)(2,1)}, bf16[2,32,2,48,1536]{4,3,2,1,0:T(8,128)(2,1)}) custom-call(s32[4]{0:T(128)} %pad_add_fusion.place_ref, bf16[16,48,1536]{2,1,0:T(8,128)(2,1)} %bitcast.116, bf16[16,48,1536]{2,1,0:T(8,128)(2,1)} %bitcast.11.refs_1_, ...), custom_call_target="tpu_custom_call", output_to_operand_aliasing={{0}: (4, {}), {1}: (5, {})} | custom-call | bytes 14155776 | tf_op jit(solution)/shard_map/pallas_call | solution.py:148
  1340.8 19.1 %fusion.116 = (bf16[1,32,2,48,1536]{4,3,2,1,0:T(8,128)(2,1)}, bf16[1,32,2,48,1536]{4,3,2,1,0:T(8,128)(2,1)}, bf16[1,32,2,48,1536]{4,3,2,1,0:T(8,128)(2,1)S(1)}, bf16[1,32,2,48,1536]{4,3,2,1,0:T(8,128)(2,1)S(1)}) fusion(bf16[2,32,2,48,1536]{4,3,2,1,0:T(8,128)(2,1)} %get-tuple-element.11, bf16[2,32,2,48,1536]{4,3,2,1,0:T(8,128)(2,1)} %get-tuple-element.12), kind=kLoop, calls=%fused_computation.231 | loop fusion | bytes 75497472 | tf_op jit(solution)/shard_map/slice | solution.py:238
  1359.9 12.6 convolution_add_fusion.5
  1372.5 4.6 fusion.66
  1377.2 7.2 convolution_add_fusion.4
  1384.4 5.4 convolution_add_fusion.1
  1390.0 2.0 collective-permute-done.29
  1392.0 1.4 fusion.15
  1394.3 1.9 collective-permute-done.30
  1396.2 3.1 fusion.23
  1400.2 1.6 multiply_convert_fusion.2
  1401.9 3.0 fusion.30
  1404.8 1.6 multiply_convert_fusion.1
  1406.5 11.7 fusion.57
  1418.2 7.6 fusion.132
  1425.8 1.3 fusion.118
  1427.4 2.7 collective-permute-done.31
  1430.4 1.5 multiply_convert_fusion
  1431.9 1.2 pad_maximum_fusion.4
  1433.6 3.0 collective-permute-done.32
  1436.6 1.5 fusion.119
  1438.1 6.5 fusion.75
  1444.7 5.2 fusion.76
  1449.9 1.5 fusion.42
  1453.2 3.0 fusion.37
  1461.1 1.7 fusion.83
  1463.7 28.2 %all_to_all.5 = bf16[64,72,128]{2,1,0:T(8,128)(2,1)S(1)} all-to-all(bf16[64,72,128]{2,1,0:T(8,128)(2,1)S(1)} %pad_maximum_fusion.5), channel_id=1, replica_groups=mesh['z'=4,'y'=4,'xh'=2,'xl'=2,'core'=2] {'z','y','xh','xl'}, dimensions={0} | all-to-all | bytes 2359296 | tf_op jit(solution)/shard_map/all_to_all | solution.py:306
  (214 shorter events, 35.1 us)
Async XLA Ops:
  7.2 180.2 %copy-start = (bf16[3072,64]{0,1:T(8,128)(2,1)S(1)}, bf16[3072,64]{0,1:T(8,128)(2,1)}, u32[]{:S(2)}) copy-start(bf16[3072,64]{0,1:T(8,128)(2,1)} %param.19) | copy-start | bytes 1179652
  7.2 184.9 %all-gather.2.cloned.1.call-start = ((), (), s32[]{:S(2)}) async-start(), calls=%async_computation.1 | async-start | bytes 9584640 | tf_op jit(solution)/shard_map/all_gather | solution.py:221
  10.7 6.4 collective-permute-start.1
  12.4 7.2 collective-permute-start.10
  14.3 6.4 collective-permute-start.19
  17.1 6.4 collective-permute-start.2
  19.5 6.4 collective-permute-start.11
  20.6 6.4 collective-permute-start.20
  23.4 6.9 collective-permute-start.3
  25.9 6.4 collective-permute-start.12
  27.0 6.8 collective-permute-start.21
  30.3 12.1 collective-permute-start.4
  32.3 11.4 collective-permute-start.13
  33.9 11.2 collective-permute-start.22
  42.4 15.9 %collective-permute-start.5 = (bf16[192,1536]{1,0:T(8,128)(2,1)S(1)}, bf16[192,1536]{1,0:T(8,128)(2,1)S(1)}, u32[]{:S(2)}, u32[]{:S(2)}) collective-permute-start(bf16[192,1536]{1,0:T(8,128)(2,1)S(1)} %collective-permute-done.4), channel_id=1, source_target_pairs={{0,32},{1,97},{2,34},{3,99},{4,36},{5,101},{6,38},{7,103},{8,40},{... | collective-permute-start | bytes 1769480 | tf_op jit(solution)/shard_map/ppermute | solution.py:78
  43.6 16.0 %collective-permute-start.14 = (bf16[192,1536]{1,0:T(8,128)(2,1)S(1)}, bf16[192,1536]{1,0:T(8,128)(2,1)S(1)}, u32[]{:S(2)}, u32[]{:S(2)}) collective-permute-start(bf16[192,1536]{1,0:T(8,128)(2,1)S(1)} %collective-permute-done.13), channel_id=1, source_target_pairs={{0,2},{1,7},{2,4},{3,1},{4,6},{5,3},{6,0},{7,5},{8,10},{9,15},{10,... | collective-permute-start | bytes 1769480 | tf_op jit(solution)/shard_map/ppermute | solution.py:78
  45.0 16.7 %collective-permute-start.23 = (bf16[192,1536]{1,0:T(8,128)(2,1)S(1)}, bf16[192,1536]{1,0:T(8,128)(2,1)S(1)}, u32[]{:S(2)}, u32[]{:S(2)}) collective-permute-start(bf16[192,1536]{1,0:T(8,128)(2,1)S(1)} %collective-permute-done.22), channel_id=1, source_target_pairs={{0,8},{1,25},{2,10},{3,27},{4,12},{5,29},{6,14},{7,31},{8,16},{9,1... | collective-permute-start | bytes 1769480 | tf_op jit(solution)/shard_map/ppermute | solution.py:78
  58.3 11.1 collective-permute-start.6
  59.6 13.2 collective-permute-start.15
  61.8 14.6 collective-permute-start.24
  70.2 7.0 copy-start.36
  70.2 11.7 copy-start.4
  70.2 51.6 %collective-permute-start.7 = (bf16[768,1536]{1,0:T(8,128)(2,1)}, bf16[768,1536]{1,0:T(8,128)(2,1)}, u32[]{:S(2)}, u32[]{:S(2)}) collective-permute-start(bf16[768,1536]{1,0:T(8,128)(2,1)} %constant_dynamic-update-slice_fusion), channel_id=1, source_target_pairs={{0,2},{1,7},{2,4},{3,1},{4,6},{5,3},{6,0},{7,5},{8,10},{9,15},{10,... | collective-permute-start | bytes 7077896 | tf_op jit(solution)/shard_map/ppermute | solution.py:78
  72.9 54.7 %copy-start.7 = (bf16[768,1536]{1,0:T(8,128)(2,1)}, bf16[768,1536]{1,0:T(8,128)(2,1)S(1)}, u32[]{:S(2)}) copy-start(bf16[768,1536]{1,0:T(8,128)(2,1)S(1)} %constant_dynamic-update-slice_fusion.7) | copy-start | bytes 7077892
  72.9 9.7 copy-start.33
  72.9 50.7 %collective-permute-start.16 = (bf16[768,1536]{1,0:T(8,128)(2,1)S(1)}, bf16[768,1536]{1,0:T(8,128)(2,1)}, u32[]{:S(2)}, u32[]{:S(2)}) collective-permute-start(bf16[768,1536]{1,0:T(8,128)(2,1)S(1)} %constant_dynamic-update-slice_fusion.7), channel_id=1, source_target_pairs={{0,8},{1,25},{2,10},{3,27},{4,12},{5,29},{6,14},{7,31},{8,16},{9,1... | collective-permute-start | bytes 7077896 | tf_op jit(solution)/shard_map/ppermute | solution.py:78
  77.2 77.8 %copy-start.28 = (bf16[64,1536]{1,0:T(8,128)(2,1)S(1)}, bf16[64,1536]{1,0:T(8,128)(2,1)}, u32[]{:S(2)}) copy-start(bf16[64,1536]{1,0:T(8,128)(2,1)} %param.20) | copy-start | bytes 589828
  77.2 46.5 %collective-permute-start.25 = (bf16[768,1536]{1,0:T(8,128)(2,1)}, bf16[768,1536]{1,0:T(8,128)(2,1)}, u32[]{:S(2)}, u32[]{:S(2)}) collective-permute-start(bf16[768,1536]{1,0:T(8,128)(2,1)} %constant_dynamic-update-slice_fusion.14), channel_id=1, source_target_pairs={{0,32},{1,97},{2,34},{3,99},{4,36},{5,101},{6,38},{7,103},{8,40},{... | collective-permute-start | bytes 7077896 | tf_op jit(solution)/shard_map/ppermute | solution.py:78
  81.9 73.1 %copy-start.29 = (bf16[64,1536]{1,0:T(8,128)(2,1)S(1)}, bf16[64,1536]{1,0:T(8,128)(2,1)}, u32[]{:S(2)}) copy-start(bf16[64,1536]{1,0:T(8,128)(2,1)} %param.22) | copy-start | bytes 589828
  121.9 30.4 %collective-permute-start.8 = (bf16[768,1536]{1,0:T(8,128)(2,1)}, bf16[768,1536]{1,0:T(8,128)(2,1)}, u32[]{:S(2)}, u32[]{:S(2)}) collective-permute-start(bf16[768,1536]{1,0:T(8,128)(2,1)} %collective-permute-done.7), channel_id=1, source_target_pairs={{0,2},{1,7},{2,4},{3,1},{4,6},{5,3},{6,0},{7,5},{8,10},{9,15},{10,... | collective-permute-start | bytes 7077896 | tf_op jit(solution)/shard_map/ppermute | solution.py:78
  123.6 30.4 %collective-permute-start.17 = (bf16[768,1536]{1,0:T(8,128)(2,1)}, bf16[768,1536]{1,0:T(8,128)(2,1)}, u32[]{:S(2)}, u32[]{:S(2)}) collective-permute-start(bf16[768,1536]{1,0:T(8,128)(2,1)} %collective-permute-done.16), channel_id=1, source_target_pairs={{0,8},{1,25},{2,10},{3,27},{4,12},{5,29},{6,14},{7,31},{8,16},{9,1... | collective-permute-start | bytes 7077896 | tf_op jit(solution)/shard_map/ppermute | solution.py:78
  123.8 30.5 %collective-permute-start.26 = (bf16[768,1536]{1,0:T(8,128)(2,1)}, bf16[768,1536]{1,0:T(8,128)(2,1)}, u32[]{:S(2)}, u32[]{:S(2)}) collective-permute-start(bf16[768,1536]{1,0:T(8,128)(2,1)} %collective-permute-done.25), channel_id=1, source_target_pairs={{0,32},{1,97},{2,34},{3,99},{4,36},{5,101},{6,38},{7,103},{8,40},{... | collective-permute-start | bytes 7077896 | tf_op jit(solution)/shard_map/ppermute | solution.py:78
  127.5 59.8 %collective-permute-start = (bf16[96,3072]{1,0:T(8,128)(2,1)}, bf16[96,3072]{1,0:T(8,128)(2,1)}, u32[]{:S(2)}, u32[]{:S(2)}) collective-permute-start(bf16[96,3072]{1,0:T(8,128)(2,1)} %fusion.9), channel_id=1, source_target_pairs={{0,1},{1,0},{2,3},{3,2},{4,5},{5,4},{6,7},{7,6},{8,9},{9,8},{10,11... | collective-permute-start | bytes 1769480 | tf_op jit(solution)/shard_map/ppermute | solution.py:55
  152.2 970.9 %collective-permute-start.9 = (bf16[768,1536]{1,0:T(8,128)(2,1)}, bf16[768,1536]{1,0:T(8,128)(2,1)S(1)}, u32[]{:S(2)}, u32[]{:S(2)}) collective-permute-start(bf16[768,1536]{1,0:T(8,128)(2,1)} %collective-permute-done.8), channel_id=1, source_target_pairs={{0,2},{1,7},{2,4},{3,1},{4,6},{5,3},{6,0},{7,5},{8,10},{9,15},{10,... | collective-permute-start | bytes 7077896 | tf_op jit(solution)/shard_map/ppermute | solution.py:78
  154.0 969.1 %collective-permute-start.18 = (bf16[768,1536]{1,0:T(8,128)(2,1)}, bf16[768,1536]{1,0:T(8,128)(2,1)}, u32[]{:S(2)}, u32[]{:S(2)}) collective-permute-start(bf16[768,1536]{1,0:T(8,128)(2,1)} %collective-permute-done.17), channel_id=1, source_target_pairs={{0,8},{1,25},{2,10},{3,27},{4,12},{5,29},{6,14},{7,31},{8,16},{9,1... | collective-permute-start | bytes 7077896 | tf_op jit(solution)/shard_map/ppermute | solution.py:78
  154.3 968.8 %collective-permute-start.27 = (bf16[768,1536]{1,0:T(8,128)(2,1)}, bf16[768,1536]{1,0:T(8,128)(2,1)}, u32[]{:S(2)}, u32[]{:S(2)}) collective-permute-start(bf16[768,1536]{1,0:T(8,128)(2,1)} %collective-permute-done.26), channel_id=1, source_target_pairs={{0,32},{1,97},{2,34},{3,99},{4,36},{5,101},{6,38},{7,103},{8,40},{... | collective-permute-start | bytes 7077896 | tf_op jit(solution)/shard_map/ppermute | solution.py:78
  155.0 32.2 %collective-permute-start.28 = (bf16[128,1536]{1,0:T(8,128)(2,1)S(1)}, bf16[128,1536]{1,0:T(8,128)(2,1)S(1)}, u32[]{:S(2)}, u32[]{:S(2)}) collective-permute-start(bf16[128,1536]{1,0:T(8,128)(2,1)S(1)} %constant_dynamic-update-slice_fusion.21), channel_id=1, source_target_pairs={{0,2},{2,0},{1,3},{3,1},{4,6},{6,4},{5,7},{7,5},{8,10},{10,8},{9,1... | collective-permute-start | bytes 1179656 | tf_op jit(solution)/shard_map/ppermute | solution.py:229
  1340.8 19.2 %copy-start.21 = (f32[192,1536]{1,0:T(8,128)S(1)}, f32[192,1536]{1,0:T(8,128)}, u32[]{:S(2)}) copy-start(f32[192,1536]{1,0:T(8,128)} %fusion.79) | copy-start | bytes 3538948
  1359.9 12.6 copy-start.3
  1359.9 58.3 %copy-start.2 = (bf16[1,32,2,48,1536]{4,3,2,1,0:T(8,128)(2,1)}, bf16[1,32,2,48,1536]{4,3,2,1,0:T(8,128)(2,1)S(1)}, u32[]{:S(2)}) copy-start(bf16[1,32,2,48,1536]{4,3,2,1,0:T(8,128)(2,1)S(1)} %get-tuple-element.94) | copy-start | bytes 28311556
  1372.5 4.7 copy-start.23
  1372.5 4.6 copy-start.20
  1384.4 11.8 slice-start.6
  1384.4 5.6 copy-start.30
  1384.4 11.8 slice-start.7
  1384.4 11.8 slice-start.8
  1389.9 2.1 collective-permute-start.29
  1393.5 8.4 slice-start.3
  1393.8 8.0 copy-start.18
  1393.8 5.4 copy-start.37
  1393.8 8.0 slice-start.4
  1393.8 8.0 slice-start.5
  1393.8 2.3 collective-permute-start.30
  1396.2 5.7 copy-start.26
  1406.5 11.7 copy-start.38
  1427.2 2.9 collective-permute-start.31
  1433.2 3.4 collective-permute-start.32
  1436.6 8.0 slice-start
  1438.1 6.5 slice-start.1
  1438.1 6.5 slice-start.2
  1444.6 5.2 copy-start.6
  1444.7 5.2 copy-start.25
  1457.5 1.9 collective-permute-start.33
  1463.7 30.3 %copy-start.1 = (bf16[3072,64]{0,1:T(8,128)(2,1)S(1)}, bf16[3072,64]{0,1:T(8,128)(2,1)}, u32[]{:S(2)}) copy-start(bf16[3072,64]{0,1:T(8,128)(2,1)} %param.19) | copy-start | bytes 1179652
  (20 other events, 44.0 us)
Sparse Core Ops, SparseCore 0:
  11.3 97.7 all-gather.1

commit v3 on v1

--- a/solution.py
+++ b/solution.py
@@ -3,6 +3,8 @@
 import jax
 import jax.numpy as jnp
 from jax import lax
+from jax.experimental import pallas as pl
+from jax.experimental.pallas import tpu as pltpu
 from jax.sharding import Mesh
 from jax.sharding import PartitionSpec as P
 
@@ -51,6 +53,303 @@
 
 def swap_cores(value):
     return lax.ppermute(value, "core", [(0, 1), (1, 0)])
+
+
+RING_AXES = (("y", "z", "x"), ("z", "x", "y"), ("x", "y", "z"))
+RING = 4
+
+
+def chip_ring(axis):
+    pairs = []
+    for device in range(128):
+        place = {"z": device // 32, "y": device // 8 % 4, "x": device // 2 % 4, "core": device % 2}
+        step = 1 if place["core"] == 0 else -1
+        place[axis] = (place[axis] + step) % RING
+        target = place["z"] * 32 + place["y"] * 8 + place["x"] * 2 + place["core"]
+        pairs.append((device, target))
+    return pairs
+
+
+def ring_slots(pieces):
+    for phase in range(3):
+        slots = [[piece] for piece in pieces]
+        for _ in range(RING - 1):
+            for i, held in enumerate(slots):
+                held.append(lax.ppermute(held[-1], AXES, chip_ring(RING_AXES[i][phase])))
+        if phase < 2:
+            pieces = [jnp.concatenate(held, axis=0) for held in slots]
+    return slots
+
+
+PIECE = 48
+TILE = 256
+SCOPED = 20 * 2**20
+ANYWHERE = pl.BlockSpec(memory_space=pl.ANY)
+IN_VMEM = pl.BlockSpec(memory_space=pltpu.VMEM)
+IN_SMEM = pl.BlockSpec(memory_space=pltpu.SMEM)
+NT = (((1,), (1,)), ((), ()))
+TN = (((0,), (0,)), ((), ()))
+
+
+def dot(left, right, dims=(((1,), (0,)), ((), ()))):
+    return lax.dot_general(left, right, dims, preferred_element_type=jnp.float32)
+
+
+def gelu_and_slope(pre):
+    square = pre * pre
+    tanh_val = jnp.tanh(root_two_pi * (pre + gelu_coef * square * pre))
+    half = 0.5 * (1.0 + tanh_val)
+    slope = half + 0.5 * pre * (1.0 - tanh_val * tanh_val) * root_two_pi * (
+        1.0 + 3.0 * gelu_coef * square
+    )
+    return pre * half, slope
+
+
+def start_slot(place_ref, i, step, slot, target, part, sem):
+    me = {"z": place_ref[0], "y": place_ref[1], "x": place_ref[2]}
+    direction = place_ref[3]
+    first, second, third = RING_AXES[i]
+
+    def source(axis, distance):
+        return lax.rem(me[axis] - distance * direction + RING, RING)
+
+    def one(k, carry):
+        at = {
+            first: source(first, lax.rem(k, RING)),
+            second: source(second, lax.div(k, RING)),
+            third: source(third, step),
+        }
+        quarter = lax.rem(at["x"], 2)
+        group = (at["z"] * 4 + at["y"]) * 2 + lax.div(at["x"], 2)
+        rows = pl.ds(pl.multiple_of(group * 2 * PIECE + part * PIECE, 16), PIECE)
+        pltpu.make_async_copy(slot.at[k], target.at[quarter, rows], sem).start()
+        return carry
+
+    lax.fori_loop(0, 16, one, 0, unroll=4)
+
+
+def wait_slot(slot, sem):
+    pltpu.make_async_copy(slot, slot, sem).wait()
+
+
+def load_body(place_ref, *refs):
+    slots, (whole, up, down, sems) = refs[:9], refs[9:]
+    targets = ((up, 0), (up, 1), (down, 0))
+    for step in range(3):
+        for i, (target, part) in enumerate(targets):
+            n = step * 3 + i
+            start_slot(place_ref, i, step, slots[n], target, part, sems.at[n])
+
+    def one(group, carry):
+        rows = pl.ds(pl.multiple_of(group * 2 * PIECE + PIECE, 16), PIECE)
+        for quarter in range(2):
+            pltpu.make_async_copy(
+                whole.at[group, quarter], down.at[quarter, rows], sems.at[9]
+            ).start()
+        return carry
+
+    lax.fori_loop(0, 32, one, 0, unroll=2)
+    for n in range(9):
+        wait_slot(slots[n], sems.at[n])
+    wait_slot(whole, sems.at[9])
+
+
+def weights_shape(width, hidden):
+    return pltpu.VMEM((2, width, hidden), jnp.bfloat16)
+
+
+def in_vmem(value):
+    return pltpu.with_memory_space_constraint(value, pltpu.VMEM)
+
+
+def load_weights(coords, slots, whole, width, hidden):
+    flat = [slots[i][step].reshape(16, PIECE, hidden) for step in range(3) for i in range(3)]
+    shape = weights_shape(width, hidden)
+    return pl.pallas_call(
+        load_body,
+        out_shape=(shape, shape),
+        in_specs=[IN_SMEM] + [ANYWHERE] * 10,
+        out_specs=(IN_VMEM, IN_VMEM),
+        scratch_shapes=[pltpu.SemaphoreType.DMA((10,))],
+        compiler_params=pltpu.CompilerParams(vmem_limit_bytes=SCOPED),
+        cost_estimate=pl.CostEstimate(
+            flops=0, bytes_accessed=13 * 16 * PIECE * hidden * 4, transcendentals=0
+        ),
+        name="load_weights",
+    )(coords, *flat, whole.reshape(32, 2, PIECE, hidden))
+
+
+def gen_body(
+    place_ref, u, low, adapt, slot_a, slot_b, slot_c, up_in, down_in, up, down, slope, mine, other, act, sems
+):
+    rows = mine.shape[0]
+    start_slot(place_ref, 0, 3, slot_a, up, 0, sems.at[0])
+    start_slot(place_ref, 1, 3, slot_b, up, 1, sems.at[1])
+    start_slot(place_ref, 2, 3, slot_c, down, 0, sems.at[2])
+    wait_slot(slot_a, sems.at[0])
+    wait_slot(slot_b, sems.at[1])
+    for q in range(2):
+
+        def hidden_tile(n, carry, q=q):
+            cols = pl.ds(pl.multiple_of(n * TILE, TILE), TILE)
+            pre = dot(u[...], up[q, :, cols]) + dot(low[...], adapt[q, :, cols])
+            value, slope[q, :, cols] = gelu_and_slope(pre)
+            act[q, :, cols] = value.astype(act.dtype)
+            return carry
+
+        lax.fori_loop(0, up.shape[2] // TILE, hidden_tile, 0)
+    wait_slot(slot_c, sems.at[2])
+
+    def width_tile(n, carry):
+        cols = pl.ds(pl.multiple_of(n * TILE, TILE), TILE)
+        out = dot(act[0], down[0, cols, :], NT) + dot(act[1], down[1, cols, :], NT)
+        mine[:, cols] = out[:rows]
+        other[:, cols] = out[rows:].astype(other.dtype)
+        return carry
+
+    lax.fori_loop(0, down.shape[1] // TILE, width_tile, 0)
+
+
+def gen_forward(coords, u, low, adapt, slots, up, down):
+    group, width = u.shape
+    hidden = up.shape[2]
+    rows = group // 2
+    shape = weights_shape(width, hidden)
+    f32, bf16 = jnp.float32, jnp.bfloat16
+    last = [slots[i][3].reshape(16, PIECE, hidden) for i in range(3)]
+    return pl.pallas_call(
+        gen_body,
+        out_shape=(
+            shape,
+            shape,
+            jax.ShapeDtypeStruct((2, group, hidden), f32),
+            jax.ShapeDtypeStruct((rows, width), f32),
+            jax.ShapeDtypeStruct((rows, width), bf16),
+        ),
+        in_specs=[IN_SMEM] + [IN_VMEM] * 3 + [ANYWHERE] * 3 + [IN_VMEM] * 2,
+        out_specs=(IN_VMEM,) * 5,
+        scratch_shapes=[pltpu.VMEM((2, group, hidden), bf16), pltpu.SemaphoreType.DMA((3,))],
+        input_output_aliases={7: 0, 8: 1},
+        compiler_params=pltpu.CompilerParams(vmem_limit_bytes=SCOPED),
+        cost_estimate=pl.CostEstimate(
+            flops=8 * group * width * hidden,
+            bytes_accessed=10 * 2**20,
+            transcendentals=2 * group * hidden,
+        ),
+        name="gen_forward",
+    )(coords, u, low, adapt, *last, in_vmem(up), in_vmem(down))
+
+
+def score_body(
+    u_mine, u_other, adapt_in, adapt_out, up, down, slope, low_ref, real, fake, others, u, act
+):
+    rows = u_mine.shape[0]
+    group = 2 * rows
+    u[:rows] = u_mine[...]
+    u[rows:] = u_other[...]
+    low = dot(u[...], adapt_in[...]).astype(low_ref.dtype)
+    low_ref[...] = low
+    for q in range(2):
+
+        def hidden_tile(n, carry, q=q):
+            cols = pl.ds(pl.multiple_of(n * TILE, TILE), TILE)
+            pre_real = dot(u[...], up[q, :, cols])
+            pre_fake = pre_real + dot(low_ref[...], adapt_out[q, :, cols])
+            act[q, :group, cols] = gelu_value(pre_real).astype(act.dtype)
+            value, slope[q, :, cols] = gelu_and_slope(pre_fake)
+            act[q, group:, cols] = value.astype(act.dtype)
+            return carry
+
+        lax.fori_loop(0, up.shape[2] // TILE, hidden_tile, 0)
+
+    def width_tile(n, carry):
+        cols = pl.ds(pl.multiple_of(n * TILE, TILE), TILE)
+        out = dot(act[0], down[0, cols, :], NT) + dot(act[1], down[1, cols, :], NT)
+        real[:, cols] = out[:rows]
+        others[:rows, cols] = out[rows:group].astype(others.dtype)
+        fake[:, cols] = out[group : group + rows]
+        others[rows:, cols] = out[group + rows :].astype(others.dtype)
+        return carry
+
+    lax.fori_loop(0, down.shape[1] // TILE, width_tile, 0)
+
+
+def score_forward(u_mine, u_other, adapt_in, adapt_out, up, down):
+    rows, width = u_mine.shape
+    hidden = up.shape[2]
+    group = 2 * rows
+    f32, bf16 = jnp.float32, jnp.bfloat16
+    return pl.pallas_call(
+        score_body,
+        out_shape=(
+            jax.ShapeDtypeStruct((2, group, hidden), f32),
+            jax.ShapeDtypeStruct((group, adapt_in.shape[1]), bf16),
+            jax.ShapeDtypeStruct((rows, width), f32),
+            jax.ShapeDtypeStruct((rows, width), f32),
+            jax.ShapeDtypeStruct((group, width), bf16),
+        ),
+        in_specs=[IN_VMEM] * 6,
+        out_specs=(IN_VMEM,) * 5,
+        scratch_shapes=[pltpu.VMEM((group, width), bf16), pltpu.VMEM((2, 2 * group, hidden), bf16)],
+        compiler_params=pltpu.CompilerParams(vmem_limit_bytes=SCOPED),
+        cost_estimate=pl.CostEstimate(
+            flops=12 * group * width * hidden,
+            bytes_accessed=10 * 2**20,
+            transcendentals=4 * group * hidden,
+        ),
+        name="score_forward",
+    )(u_mine, u_other, adapt_in, adapt_out, in_vmem(up), in_vmem(down))
+
+
+def back_body(
+    cots_mine, cots_other, slope_gen, slope_fake, low_gen, low_fake, gen_out, fake_out, down, grads, mix, cots
+):
+    group = cots_mine.shape[0]
+    rows = group // 2
+    for i in range(2):
+        cots[i * group : i * group + rows] = cots_mine[i * rows : (i + 1) * rows]
+        cots[i * group + rows : (i + 1) * group] = cots_other[i * rows : (i + 1) * rows]
+    zero = jnp.zeros((group, low_gen.shape[1]), jnp.float32)
+    mixed = (zero, zero)
+    for q in range(2):
+
+        def hidden_tile(n, carry, q=q):
+            cols = pl.ds(pl.multiple_of(n * TILE, TILE), TILE)
+            raw = dot(cots[...], down[q, :, cols])
+            back_gen = (raw[:group] * slope_gen[q, :, cols]).astype(jnp.bfloat16)
+            back_fake = (raw[group:] * slope_fake[q, :, cols]).astype(jnp.bfloat16)
+            grads[0, q, :, cols] = dot(low_gen[...], back_gen, TN).astype(grads.dtype)
+            grads[1, q, :, cols] = dot(low_fake[...], back_fake, TN).astype(grads.dtype)
+            return (
+                carry[0] + dot(back_gen, gen_out[q, :, cols], NT),
+                carry[1] + dot(back_fake, fake_out[q, :, cols], NT),
+            )
+
+        mixed = lax.fori_loop(0, down.shape[2] // TILE, hidden_tile, mixed)
+    mix[0] = mixed[0]
+    mix[1] = mixed[1]
+
+
+def backward(cots_mine, cots_other, slope_gen, slope_fake, low_gen, low_fake, gen_out, fake_out, down):
+    group, width = cots_mine.shape
+    hidden = down.shape[2]
+    rank = low_gen.shape[1]
+    f32, bf16 = jnp.float32, jnp.bfloat16
+    return pl.pallas_call(
+        back_body,
+        out_shape=(
+            jax.ShapeDtypeStruct((2, 2, rank, hidden), bf16),
+            jax.ShapeDtypeStruct((2, group, rank), f32),
+        ),
+        in_specs=[IN_VMEM] * 9,
+        out_specs=(IN_VMEM,) * 2,
+        scratch_shapes=[pltpu.VMEM((2 * group, width), bf16)],
+        compiler_params=pltpu.CompilerParams(vmem_limit_bytes=SCOPED),
+        cost_estimate=pl.CostEstimate(
+            flops=8 * group * width * hidden, bytes_accessed=10 * 2**20, transcendentals=0
+        ),
+        name="backward",
+    )(cots_mine, cots_other, slope_gen, slope_fake, low_gen, low_fake, gen_out, fake_out, in_vmem(down))
 
 
 def three_terms(value):
@@ -105,10 +404,19 @@
     def both_rows(mine):
         return jnp.concatenate([mine, swap_cores(mine)], axis=0)
 
-    up_all = lax.all_gather(base_up, ("xl", "z", "y", "xh"), axis=0, tiled=True)
-    down_all = lax.all_gather(base_down.T, ("xl", "z", "y", "xh"), axis=0, tiled=True)
-    up_all = up_all.reshape(2, width, hidden)
-    down_all = down_all.reshape(2, width, hidden)
+    coords = jnp.stack(
+        [
+            lax.axis_index("z"),
+            lax.axis_index("y"),
+            lax.axis_index("xh") * 2 + xl,
+            1 - 2 * core,
+        ]
+    ).astype(jnp.int32)
+    down_rows = base_down.T
+    half = base_up.shape[0] // 2
+    last_quarter = lax.all_gather(down_rows[half:], CHIPS, axis=0, tiled=True)
+    slots = ring_slots([base_up[:half], base_up[half:], down_rows[:half]])
+    up_part, down_part = load_weights(coords, slots, last_quarter, width, hidden)
 
     def other_quarter(mine):
         theirs = lax.ppermute(mine, "xl", [(0, 1), (1, 0)])
@@ -120,31 +428,22 @@
     u_mine = modulate(gen_input, *modulation(gen_steps))
     u_gen = both_rows(u_mine)
     low_gen = matmul(u_gen, gen_adapt_in).astype(bf16)
-    pre_gen = [matmul(u_gen, up_all[q]) + matmul(low_gen, gen_out[q]) for q in range(2)]
-    act_gen = [gelu_value(p).astype(bf16) for p in pre_gen]
-
-    def down(acts):
-        return contract(acts[0], down_all[0], 1, 1) + contract(acts[1], down_all[1], 1, 1)
-
-    out_gen = down(act_gen)
-    out_mine = out_gen[:shard_rows] + swap_cores(out_gen[shard_rows:].astype(bf16)).astype(f32)
+    up_all, down_all, slope_gen, out_mine, out_other = gen_forward(
+        coords, u_gen, low_gen, gen_out, slots, up_part, down_part
+    )
+    out_mine = out_mine + swap_cores(out_other).astype(f32)
     latents = (gen_input.astype(f32) + output_gate * out_mine).astype(bf16)
     two_blend = (two_steps(score_steps).astype(f32) + 0.5) / 1000.0
     blend = jnp.where(in_last, two_blend[1], two_blend[0])
     noised = ((1.0 - blend) * latents.astype(f32) + blend * noise_score.astype(f32)).astype(bf16)
-    u_score = both_rows(modulate(noised, *modulation(score_steps)))
-    low_fake = matmul(u_score, fake_adapt_in).astype(bf16)
-    pre_real = [matmul(u_score, up_all[q]) for q in range(2)]
-    pre_fake = [pre_real[q] + matmul(low_fake, fake_out[q]) for q in range(2)]
-    acts = [
-        jnp.concatenate([gelu_value(pre_real[q]), gelu_value(pre_fake[q])], axis=0).astype(bf16)
-        for q in range(2)
-    ]
-    outs = down(acts)
-    parts = [outs[i * shard_rows : (i + 1) * shard_rows] for i in range(4)]
-    got = swap_cores(jnp.concatenate([parts[1], parts[3]], axis=0).astype(bf16)).astype(f32)
-    out_real = parts[0] + got[:shard_rows]
-    out_fake = parts[2] + got[shard_rows:]
+    u_score = modulate(noised, *modulation(score_steps))
+    u_score_other = swap_cores(u_score)
+    slope_fake, low_fake, out_real, out_fake, outs_other = score_forward(
+        u_score, u_score_other, fake_adapt_in, fake_out, up_all, down_all
+    )
+    got = swap_cores(outs_other).astype(f32)
+    out_real = out_real + got[:shard_rows]
+    out_fake = out_fake + got[shard_rows:]
     score_diff = (output_gate * (out_fake - out_real)).astype(bf16)
     cot_gen = (output_gate * score_diff.astype(f32) * loss_scale).astype(bf16)
     target = noise_score.astype(f32) - latents.astype(f32)
@@ -152,22 +451,10 @@
         output_gate * (noised.astype(f32) + output_gate * out_fake - target) * loss_scale
     ).astype(bf16)
     cots = jnp.concatenate([cot_gen, cot_fake], axis=0)
-    cots_other = swap_cores(cots)
-    cots = jnp.concatenate(
-        [cot_gen, cots_other[:shard_rows], cot_fake, cots_other[shard_rows:]], axis=0
-    )
-    group = 2 * shard_rows
-    backs = [matmul(cots, down_all[q]) for q in range(2)]
-    back_gen = [(backs[q][:group] * gelu_slope(pre_gen[q])).astype(bf16) for q in range(2)]
-    back_fake = [(backs[q][group:] * gelu_slope(pre_fake[q])).astype(bf16) for q in range(2)]
-
-    def out_grad(low, back):
-        return [contract(low, back[q], 0, 0) for q in range(2)]
-
-    def mixed(back, adapter):
-        return contract(back[0], adapter[0], 1, 1) + contract(back[1], adapter[1], 1, 1)
-
-    mix = jnp.concatenate([mixed(back_gen, gen_out), mixed(back_fake, fake_out)], axis=1)
+    out_grads, mix = backward(
+        cots, swap_cores(cots), slope_gen, slope_fake, low_gen, low_fake, gen_out, fake_out, down_all
+    )
+    mix = jnp.concatenate([mix[0], mix[1]], axis=1)
     mix_other = swap_cores(mix)
     mix = mix + jnp.concatenate([mix_other[shard_rows:], mix_other[:shard_rows]], axis=0)
 
@@ -177,16 +464,16 @@
         chips = total.reshape(-1, 2, width // 128, rank)
         return jnp.where(core == 0, chips[:, 0], chips[:, 1])
 
-    in_grads = jnp.concatenate([in_grad(u_gen, mix[:, :rank]), in_grad(u_score, mix[:, rank:])], axis=2)
+    u_score_group = jnp.concatenate([u_score, u_score_other], axis=0)
+    in_grads = jnp.concatenate(
+        [in_grad(u_gen, mix[:, :rank]), in_grad(u_score_group, mix[:, rank:])], axis=2
+    )
     chips, in_rows = in_grads.shape[0], in_grads.shape[1]
     groups = chips // 2
-    out_grads = jnp.stack(
-        [jnp.stack(out_grad(low_gen, back_gen)), jnp.stack(out_grad(low_fake, back_fake))]
-    )
     out_grads = out_grads.reshape(2, 2, groups, rank // groups, hidden).transpose(2, 1, 0, 3, 4)
     out_rows = 2 * (rank // groups) * hidden // 128
     packed = jnp.concatenate(
-        [in_grads.astype(bf16), out_grads.astype(bf16).reshape(chips, out_rows, 128)], axis=1
+        [in_grads.astype(bf16), out_grads.reshape(chips, out_rows, 128)], axis=1
     )
     received = lax.all_to_all(packed, CHIPS, 0, 0, tiled=True)
     summed = jnp.sum(received.astype(f32), axis=0)

time: 1220 us -> 348 us (0.29)
  waiting for transfers between devices: 1070 us -> 140 us
  matrix products: 73.6 us -> 2.26 us
  Pallas kernels: 0 us -> 65.8 us
  local copies, waits for them, and re-layouts: 11.8 us -> 56.1 us
  starting transfers between devices: 2.85 us -> 26.3 us
    all_gather x2 -> x1, waiting for transfers between devices: 1060 us -> 0.01 us  [local(): last_quarter = lax.all_gather(down_rows[half:], CHIPS, axis=0, tiled=True)]
    ppermute x0 -> x27, waiting for transfers between devices: none -> 102 us  [ring_slots(): held.append(lax.ppermute(held[-1], AXES, chip_ring(RING_AXES[i][phase])))]
    pallas_call x0 -> x4, Pallas kernels: none -> 65.8 us  [the longest x1 21.5 us: score_forward(): pl.pallas_call(score_body, out_shape=(jax.ShapeDtypeStruct((2, group, hid...]
    dot_general x12 -> x1, matrix products: 41.8 us -> 1.08 us  [matmul(): return jnp.dot(left, right, preferred_element_type=jnp.float32)]
    unnamed x69 -> x89, local copies, waits for them, and re-layouts: 4.04 us -> 44.2 us
    dot_general x14 -> x2, matrix products: 31.8 us -> 1.18 us  [contract(): lax.dot_general(left, right, (((left_dim,), (right_dim,)), ((), ())), pre...]
    ppermute x1, waiting for transfers between devices: 1.04 us -> 30.1 us  [other_quarter(): theirs = lax.ppermute(mine, 'xl', [(0, 1), (1, 0)])]
    ppermute x0 -> x27, starting transfers between devices: none -> 22.5 us  [ring_slots(): held.append(lax.ppermute(held[-1], AXES, chip_ring(RING_AXES[i][phase])))]
  transfers between devices with their start and end apart: 9 -> 35, of which waited for: 7 -> 23; matrix products, arithmetic and copies ran while one was open for 2% -> 8% of each run, Pallas kernels for 0% -> 3%
where the time goes in v3:
time: 348 us
  waiting for transfers between devices  140 us (40%)
  Pallas kernels  65.8 us (19%)
  local copies, waits for them, and re-layouts  56.1 us (16%)
  blocking collectives  27.9 us (8%)
  starting transfers between devices  26.3 us (8%)
  other arithmetic  14.7 us (4%)
  between operations  14.6 us (4%)
    ppermute x27, waiting for transfers between devices, ring_slots(): held.append(lax.ppermute(held[-1], AXES, chip_ring(RING_AXES[i][phase])))  102 us
    unnamed x89, local copies, waits for them, and re-layouts  44.2 us
    ppermute x1, waiting for transfers between devices, other_quarter(): theirs = lax.ppermute(mine, 'xl', [(0, 1), (1, 0)])  30.1 us
    all_to_all x1, blocking collectives, local(): received = lax.all_to_all(packed, CHIPS, 0, 0, tiled=True)  27.9 us
    ppermute x27, starting transfers between devices, ring_slots(): held.append(lax.ppermute(held[-1], AXES, chip_ring(RING_AXES[i][phase])))  22.5 us
    pallas_call x1, Pallas kernels, score_forward(): pl.pallas_call(score_body, out_shape=(jax.ShapeDtypeStruct((2, group, hid...  21.5 us
    pallas_call x1, Pallas kernels, gen_forward(): pl.pallas_call(gen_body, out_shape=(shape, shape, jax.ShapeDtypeStruct((2...  20.2 us
    pallas_call x1, Pallas kernels, backward(): pl.pallas_call(back_body, out_shape=(jax.ShapeDtypeStruct((2, 2, rank, hi...  13.4 us
  transfers between devices with their start and end apart: 35, of which 23 were waited for; matrix products, arithmetic and copies ran while one was open for 8% of the time, Pallas kernels for 3%

profile of v3, /device:TPU:0, one launch (start us, length us, event | category | flops | bytes accessed | tf_op | source)
XLA Modules:
  0.0 347.5 jit_solution(15559765529238056161)
XLA Ops:
  7.2 1.8 fusion.45
  9.1 1.7 fusion.46
  10.7 1.7 collective-permute-start.2
  12.4 1.9 collective-permute-start.11
  14.3 1.5 collective-permute-start.20
  15.8 1.3 collective-permute-done.2
  17.5 2.0 collective-permute-done.11
  19.6 1.3 collective-permute-done.20
  22.5 0.9 collective-permute-done.3
  24.1 1.8 collective-permute-done.12
  26.0 1.2 collective-permute-done.21
  28.9 1.5 collective-permute-done.4
  30.4 1.9 collective-permute-start.5
  32.3 1.6 collective-permute-start.14
  34.1 2.0 collective-permute-start.23
  37.4 5.0 %collective-permute-done.5 = bf16[192,1536]{1,0:T(8,128)(2,1)S(1)} collective-permute-done((bf16[192,1536]{1,0:T(8,128)(2,1)S(1)}, bf16[192,1536]{1,0:T(8,128)(2,1)S(1)}, u32[]{:S(2)}, u32[]{:S(2)}) %collective-permute-start.5) | collective-permute-done | bytes 589856 | tf_op jit(solution)/shard_map/ppermute | solution.py:78
  42.6 0.9 constant_dynamic-update-slice_fusion.4
  43.7 1.2 collective-permute-start.15
  45.2 0.7 collective-permute-start.24
  46.0 0.9 constant_dynamic-update-slice_fusion.18
  46.9 11.5 %collective-permute-done.6 = bf16[192,1536]{1,0:T(8,128)(2,1)S(1)} collective-permute-done((bf16[192,1536]{1,0:T(8,128)(2,1)S(1)}, bf16[192,1536]{1,0:T(8,128)(2,1)S(1)}, u32[]{:S(2)}, u32[]{:S(2)}) %collective-permute-start.6) | collective-permute-done | bytes 589856 | tf_op jit(solution)/shard_map/ppermute | solution.py:78
  58.4 0.8 constant_dynamic-update-slice_fusion.3
  59.6 2.1 collective-permute-start.16
  62.1 0.9 constant_dynamic-update-slice_fusion.17
  63.0 6.5 %collective-permute-done.7 = bf16[192,1536]{1,0:T(8,128)(2,1)S(1)} collective-permute-done((bf16[192,1536]{1,0:T(8,128)(2,1)S(1)}, bf16[192,1536]{1,0:T(8,128)(2,1)S(1)}, u32[]{:S(2)}, u32[]{:S(2)}) %collective-permute-start.7) | collective-permute-done | bytes 589856 | tf_op jit(solution)/shard_map/ppermute | solution.py:78
  69.5 0.9 constant_dynamic-update-slice_fusion.2
  70.3 2.6 collective-permute-start.8
  73.0 1.0 collective-permute-start.17
  74.0 2.5 collective-permute-done.25
  76.5 0.8 constant_dynamic-update-slice_fusion.16
  77.3 1.3 fusion.54
  78.7 1.4 add_convert_fusion.1
  80.0 1.2 add_multiply_fusion
  82.5 1.4 multiply_add_fusion.1
  83.9 38.0 %collective-permute-done.8 = bf16[768,1536]{1,0:T(8,128)(2,1)} collective-permute-done((bf16[768,1536]{1,0:T(8,128)(2,1)}, bf16[768,1536]{1,0:T(8,128)(2,1)}, u32[]{:S(2)}, u32[]{:S(2)}) %collective-permute-start.8) | collective-permute-done | bytes 2359328 | tf_op jit(solution)/shard_map/ppermute | solution.py:78
  122.3 1.3 collective-permute-done.17
  123.7 0.9 collective-permute-start.27
  124.6 1.9 broadcast_subtract_fusion
  126.9 0.9 collective-permute-start
  127.9 24.4 %collective-permute-done.9 = bf16[768,1536]{1,0:T(8,128)(2,1)} collective-permute-done((bf16[768,1536]{1,0:T(8,128)(2,1)}, bf16[768,1536]{1,0:T(8,128)(2,1)}, u32[]{:S(2)}, u32[]{:S(2)}) %collective-permute-start.9) | collective-permute-done | bytes 2359328 | tf_op jit(solution)/shard_map/ppermute | solution.py:78
  152.3 1.7 collective-permute-done.18
  154.1 0.9 collective-permute-start.28
  155.0 0.9 collective-permute-start.1
  157.2 30.1 %collective-permute-done.1 = bf16[128,1536]{1,0:T(8,128)(2,1)S(1)} collective-permute-done((bf16[128,1536]{1,0:T(8,128)(2,1)S(1)}, bf16[128,1536]{1,0:T(8,128)(2,1)S(1)}, u32[]{:S(2)}, u32[]{:S(2)}) %collective-permute-start.1) | collective-permute-done | bytes 393248 | tf_op jit(solution)/shard_map/ppermute | solution.py:422
  187.4 0.9 pad_maximum_fusion.6
  188.3 1.1 convolution_convert_fusion.low.low_gen
  189.4 1.1 pad_maximum_fusion.u
  190.5 10.7 %load_weights.1 = (bf16[2,3072,1536]{2,1,0:T(8,128)(2,1)S(1)}, bf16[2,3072,1536]{2,1,0:T(8,128)(2,1)S(1)}) custom-call(s32[4]{0:T(128)} %pad_add_fusion.place_ref, bf16[16,48,1536]{2,1,0:T(8,128)(2,1)} %bitcast.16.refs_0_, bf16[16,48,1536]{2,1,0:T(8,128)(2,1)} %bitcast.52, bf16[16,48,1536]{2,1,0:T(8,128)(2,1)} %bitcast.18.refs_2_, ...), custom_call_target="tpu_custom_call" | custom-call | bytes 61341696 | tf_op jit(solution)/shard_map/load_weights/pallas_call | solution.py:168
  201.3 20.2 %gen_forward.1 = (bf16[2,3072,1536]{2,1,0:T(8,128)(2,1)S(1)}, bf16[2,3072,1536]{2,1,0:T(8,128)(2,1)S(1)}, f32[2,192,1536]{2,1,0:T(8,128)}, f32[96,3072]{1,0:T(8,128)}, bf16[96,3072]{1,0:T(8,128)(2,1)}) custom-call(s32[4]{0:T(128)} %pad_add_fusion.place_ref, bf16[192,3072]{1,0:T(8,128)(2,1)} %pad_maximum_fusion.u, ...), custom_call_target="tpu_custom_call", output_to_operand_aliasing={{0}: (7, {}), {1}: (8, {})} | custom-call | flops 7247757312 | bytes 10485760 | tf_op jit(solution)/shard_map/gen_forward/pallas_call | solution.py:220
  221.5 6.4 %copy-done.2 = bf16[2,3072,1536]{2,1,0:T(8,128)(2,1)} copy-done((bf16[2,3072,1536]{2,1,0:T(8,128)(2,1)}, bf16[2,3072,1536]{2,1,0:T(8,128)(2,1)S(1)}, u32[]{:S(2)}) %copy-start.2) | copy-done | bytes 18874392
  227.9 6.5 %copy-done.5 = bf16[2,3072,1536]{2,1,0:T(8,128)(2,1)} copy-done((bf16[2,3072,1536]{2,1,0:T(8,128)(2,1)}, bf16[2,3072,1536]{2,1,0:T(8,128)(2,1)S(1)}, u32[]{:S(2)}) %copy-start.5) | copy-done | bytes 18874392
  234.4 2.2 collective-permute-done.29
  236.6 1.9 fusion.11
  239.1 2.2 copy.27.adapt_in
  241.3 0.8 copy-done.22
  242.1 6.4 %copy-done.3 = bf16[2,3072,1536]{2,1,0:T(8,128)(2,1)S(1)} copy-done((bf16[2,3072,1536]{2,1,0:T(8,128)(2,1)S(1)}, bf16[2,3072,1536]{2,1,0:T(8,128)(2,1)}, u32[]{:S(2)}) %copy-start.3) | copy-done | bytes 18874392
  248.5 6.4 %copy-done.6 = bf16[2,3072,1536]{2,1,0:T(8,128)(2,1)S(1)} copy-done((bf16[2,3072,1536]{2,1,0:T(8,128)(2,1)S(1)}, bf16[2,3072,1536]{2,1,0:T(8,128)(2,1)}, u32[]{:S(2)}) %copy-start.6) | copy-done | bytes 18874392
  254.8 21.5 %score_forward.1 = (f32[2,192,1536]{2,1,0:T(8,128)}, bf16[192,64]{1,0:T(8,128)(2,1)}, f32[96,3072]{1,0:T(8,128)}, f32[96,3072]{1,0:T(8,128)}, bf16[192,3072]{1,0:T(8,128)(2,1)}) custom-call(bf16[96,3072]{1,0:T(8,128)(2,1)} %copy-done.16, bf16[96,3072]{1,0:T(8,128)(2,1)} %copy-done.22, bf16[3072,64]{1,0:T(8,128)(2,1)} %copy.27.adapt_in, ...), custom_call_target="tpu_custom_call" | custom-call | flops 10871635968 | bytes 10485760 | tf_op jit(solution)/shard_map/score_forward/pallas_call | solution.py:282
  276.9 2.7 collective-permute-done.31
  279.9 1.5 multiply_convert_fusion
  281.9 2.5 collective-permute-done.32.cots_other
  284.5 6.4 %copy-done.4 = bf16[2,3072,1536]{2,1,0:T(8,128)(2,1)S(1)} copy-done((bf16[2,3072,1536]{2,1,0:T(8,128)(2,1)S(1)}, bf16[2,3072,1536]{2,1,0:T(8,128)(2,1)}, u32[]{:S(2)}) %copy-start.4) | copy-done | bytes 18874392
  290.8 13.4 %backward.1 = (bf16[2,2,64,1536]{3,2,1,0:T(8,128)(2,1)S(1)}, f32[2,192,64]{2,1,0:T(8,128)S(1)}) custom-call(bf16[192,3072]{1,0:T(8,128)(2,1)S(1)} %pad_maximum_fusion.1.cots_mine, bf16[192,3072]{1,0:T(8,128)(2,1)S(1)} %collective-permute-done.32.cots_other, f32[2,192,1536]{2,1,0:T(8,128)S(1)} %copy-done.8, f32[2,192,1536]{2,1,0:T(8,128)S(1)} %copy-done.9, ...), custom_call_target="tpu_custom_call" | custom-call | flops 7247757312 | bytes 10485760 | tf_op jit(solution)/shard_map/backward/pallas_call | solution.py:338
  310.7 27.9 %all_to_all.5 = bf16[64,72,128]{2,1,0:T(8,128)(2,1)S(1)} all-to-all(bf16[64,72,128]{2,1,0:T(8,128)(2,1)S(1)} %pad_maximum_fusion.2), channel_id=1, replica_groups=mesh['z'=4,'y'=4,'xh'=2,'xl'=2,'core'=2] {'z','y','xh','xl'}, dimensions={0} | all-to-all | bytes 2359296 | tf_op jit(solution)/shard_map/all_to_all | solution.py:478
  (158 shorter events, 21.6 us)
Async XLA Ops:
  7.2 181.1 %copy-start = (bf16[3072,64]{0,1:T(8,128)(2,1)S(1)}, bf16[3072,64]{0,1:T(8,128)(2,1)}, u32[]{:S(2)}) copy-start(bf16[3072,64]{0,1:T(8,128)(2,1)} %param.19) | copy-start | bytes 1179652
  7.2 183.3 %all-gather.2.cloned.1.call-start = ((), (), s32[]{:S(2)}) async-start(), calls=%async_computation.1 | async-start | bytes 9584640 | tf_op jit(solution)/shard_map/all_gather | solution.py:417
  10.7 6.4 %collective-permute-start.2 = (bf16[48,1536]{1,0:T(8,128)(2,1)S(1)}, bf16[48,1536]{1,0:T(8,128)(2,1)S(1)}, u32[]{:S(2)}, u32[]{:S(2)}) collective-permute-start(bf16[48,1536]{1,0:T(8,128)(2,1)S(1)} %get-tuple-element.54), channel_id=1, source_target_pairs={{0,8},{1,25},{2,10},{3,27},{4,12},{5,29},{6,14},{7,31},{8,16},{9,1... | collective-permute-start | bytes 442376 | tf_op jit(solution)/shard_map/ppermute | solution.py:78
  12.4 7.2 %collective-permute-start.11 = (bf16[48,1536]{1,0:T(8,128)(2,1)S(1)}, bf16[48,1536]{1,0:T(8,128)(2,1)S(1)}, u32[]{:S(2)}, u32[]{:S(2)}) collective-permute-start(bf16[48,1536]{1,0:T(8,128)(2,1)S(1)} %get-tuple-element.51), channel_id=1, source_target_pairs={{0,32},{1,97},{2,34},{3,99},{4,36},{5,101},{6,38},{7,103},{8,40},{... | collective-permute-start | bytes 442376 | tf_op jit(solution)/shard_map/ppermute | solution.py:78
  14.3 6.6 %collective-permute-start.20 = (bf16[48,1536]{1,0:T(8,128)(2,1)}, bf16[48,1536]{1,0:T(8,128)(2,1)S(1)}, u32[]{:S(2)}, u32[]{:S(2)}) collective-permute-start(bf16[48,1536]{1,0:T(8,128)(2,1)} %get-tuple-element.50), channel_id=1, source_target_pairs={{0,2},{1,7},{2,4},{3,1},{4,6},{5,3},{6,0},{7,5},{8,10},{9,15},{10,... | collective-permute-start | bytes 442376 | tf_op jit(solution)/shard_map/ppermute | solution.py:78
  17.1 6.4 %collective-permute-start.3 = (bf16[48,1536]{1,0:T(8,128)(2,1)S(1)}, bf16[48,1536]{1,0:T(8,128)(2,1)S(1)}, u32[]{:S(2)}, u32[]{:S(2)}) collective-permute-start(bf16[48,1536]{1,0:T(8,128)(2,1)S(1)} %collective-permute-done.2), channel_id=1, source_target_pairs={{0,8},{1,25},{2,10},{3,27},{4,12},{5,29},{6,14},{7,31},{8,16},{9,1... | collective-permute-start | bytes 442376 | tf_op jit(solution)/shard_map/ppermute | solution.py:78
  19.6 6.4 %collective-permute-start.12 = (bf16[48,1536]{1,0:T(8,128)(2,1)S(1)}, bf16[48,1536]{1,0:T(8,128)(2,1)S(1)}, u32[]{:S(2)}, u32[]{:S(2)}) collective-permute-start(bf16[48,1536]{1,0:T(8,128)(2,1)S(1)} %collective-permute-done.11), channel_id=1, source_target_pairs={{0,32},{1,97},{2,34},{3,99},{4,36},{5,101},{6,38},{7,103},{8,40},{... | collective-permute-start | bytes 442376 | tf_op jit(solution)/shard_map/ppermute | solution.py:78
  20.9 6.4 %collective-permute-start.21 = (bf16[48,1536]{1,0:T(8,128)(2,1)S(1)}, bf16[48,1536]{1,0:T(8,128)(2,1)S(1)}, u32[]{:S(2)}, u32[]{:S(2)}) collective-permute-start(bf16[48,1536]{1,0:T(8,128)(2,1)S(1)} %collective-permute-done.20), channel_id=1, source_target_pairs={{0,2},{1,7},{2,4},{3,1},{4,6},{5,3},{6,0},{7,5},{8,10},{9,15},{10,... | collective-permute-start | bytes 442376 | tf_op jit(solution)/shard_map/ppermute | solution.py:78
  23.5 6.9 %collective-permute-start.4 = (bf16[48,1536]{1,0:T(8,128)(2,1)S(1)}, bf16[48,1536]{1,0:T(8,128)(2,1)S(1)}, u32[]{:S(2)}, u32[]{:S(2)}) collective-permute-start(bf16[48,1536]{1,0:T(8,128)(2,1)S(1)} %collective-permute-done.3), channel_id=1, source_target_pairs={{0,8},{1,25},{2,10},{3,27},{4,12},{5,29},{6,14},{7,31},{8,16},{9,1... | collective-permute-start | bytes 442376 | tf_op jit(solution)/shard_map/ppermute | solution.py:78
  25.9 6.4 %collective-permute-start.13 = (bf16[48,1536]{1,0:T(8,128)(2,1)S(1)}, bf16[48,1536]{1,0:T(8,128)(2,1)S(1)}, u32[]{:S(2)}, u32[]{:S(2)}) collective-permute-start(bf16[48,1536]{1,0:T(8,128)(2,1)S(1)} %collective-permute-done.12), channel_id=1, source_target_pairs={{0,32},{1,97},{2,34},{3,99},{4,36},{5,101},{6,38},{7,103},{8,40},{... | collective-permute-start | bytes 442376 | tf_op jit(solution)/shard_map/ppermute | solution.py:78
  27.2 6.8 %collective-permute-start.22 = (bf16[48,1536]{1,0:T(8,128)(2,1)S(1)}, bf16[48,1536]{1,0:T(8,128)(2,1)S(1)}, u32[]{:S(2)}, u32[]{:S(2)}) collective-permute-start(bf16[48,1536]{1,0:T(8,128)(2,1)S(1)} %collective-permute-done.21), channel_id=1, source_target_pairs={{0,2},{1,7},{2,4},{3,1},{4,6},{5,3},{6,0},{7,5},{8,10},{9,15},{10,... | collective-permute-start | bytes 442376 | tf_op jit(solution)/shard_map/ppermute | solution.py:78
  28.9 5.2 %copy-start.24 = (bf16[48,1536]{1,0:T(8,128)(2,1)S(1)}, bf16[48,1536]{1,0:T(8,128)(2,1)}, u32[]{:S(2)}) copy-start(bf16[48,1536]{1,0:T(8,128)(2,1)} %get-tuple-element.50) | copy-start | bytes 442372
  30.4 12.1 %collective-permute-start.5 = (bf16[192,1536]{1,0:T(8,128)(2,1)S(1)}, bf16[192,1536]{1,0:T(8,128)(2,1)S(1)}, u32[]{:S(2)}, u32[]{:S(2)}) collective-permute-start(bf16[192,1536]{1,0:T(8,128)(2,1)S(1)} %pad_maximum_fusion.3), channel_id=1, source_target_pairs={{0,32},{1,97},{2,34},{3,99},{4,36},{5,101},{6,38},{7,103},{8,40},{... | collective-permute-start | bytes 1769480 | tf_op jit(solution)/shard_map/ppermute | solution.py:78
  32.3 11.4 %collective-permute-start.14 = (bf16[192,1536]{1,0:T(8,128)(2,1)S(1)}, bf16[192,1536]{1,0:T(8,128)(2,1)S(1)}, u32[]{:S(2)}, u32[]{:S(2)}) collective-permute-start(bf16[192,1536]{1,0:T(8,128)(2,1)S(1)} %pad_maximum_fusion.4), channel_id=1, source_target_pairs={{0,2},{1,7},{2,4},{3,1},{4,6},{5,3},{6,0},{7,5},{8,10},{9,15},{10,... | collective-permute-start | bytes 1769480 | tf_op jit(solution)/shard_map/ppermute | solution.py:78
  34.1 11.2 %collective-permute-start.23 = (bf16[192,1536]{1,0:T(8,128)(2,1)S(1)}, bf16[192,1536]{1,0:T(8,128)(2,1)S(1)}, u32[]{:S(2)}, u32[]{:S(2)}) collective-permute-start(bf16[192,1536]{1,0:T(8,128)(2,1)S(1)} %pad_maximum_fusion.5), channel_id=1, source_target_pairs={{0,8},{1,25},{2,10},{3,27},{4,12},{5,29},{6,14},{7,31},{8,16},{9,1... | collective-permute-start | bytes 1769480 | tf_op jit(solution)/shard_map/ppermute | solution.py:78
  42.4 15.9 %collective-permute-start.6 = (bf16[192,1536]{1,0:T(8,128)(2,1)S(1)}, bf16[192,1536]{1,0:T(8,128)(2,1)S(1)}, u32[]{:S(2)}, u32[]{:S(2)}) collective-permute-start(bf16[192,1536]{1,0:T(8,128)(2,1)S(1)} %collective-permute-done.5), channel_id=1, source_target_pairs={{0,32},{1,97},{2,34},{3,99},{4,36},{5,101},{6,38},{7,103},{8,40},{... | collective-permute-start | bytes 1769480 | tf_op jit(solution)/shard_map/ppermute | solution.py:78
  43.7 16.0 %collective-permute-start.15 = (bf16[192,1536]{1,0:T(8,128)(2,1)S(1)}, bf16[192,1536]{1,0:T(8,128)(2,1)S(1)}, u32[]{:S(2)}, u32[]{:S(2)}) collective-permute-start(bf16[192,1536]{1,0:T(8,128)(2,1)S(1)} %collective-permute-done.14), channel_id=1, source_target_pairs={{0,2},{1,7},{2,4},{3,1},{4,6},{5,3},{6,0},{7,5},{8,10},{9,15},{10,... | collective-permute-start | bytes 1769480 | tf_op jit(solution)/shard_map/ppermute | solution.py:78
  45.2 16.6 %collective-permute-start.24 = (bf16[192,1536]{1,0:T(8,128)(2,1)S(1)}, bf16[192,1536]{1,0:T(8,128)(2,1)S(1)}, u32[]{:S(2)}, u32[]{:S(2)}) collective-permute-start(bf16[192,1536]{1,0:T(8,128)(2,1)S(1)} %collective-permute-done.23), channel_id=1, source_target_pairs={{0,8},{1,25},{2,10},{3,27},{4,12},{5,29},{6,14},{7,31},{8,16},{9,1... | collective-permute-start | bytes 1769480 | tf_op jit(solution)/shard_map/ppermute | solution.py:78
  58.4 11.1 %collective-permute-start.7 = (bf16[192,1536]{1,0:T(8,128)(2,1)S(1)}, bf16[192,1536]{1,0:T(8,128)(2,1)S(1)}, u32[]{:S(2)}, u32[]{:S(2)}) collective-permute-start(bf16[192,1536]{1,0:T(8,128)(2,1)S(1)} %collective-permute-done.6), channel_id=1, source_target_pairs={{0,32},{1,97},{2,34},{3,99},{4,36},{5,101},{6,38},{7,103},{8,40},{... | collective-permute-start | bytes 1769480 | tf_op jit(solution)/shard_map/ppermute | solution.py:78
  59.6 13.3 %collective-permute-start.16 = (bf16[192,1536]{1,0:T(8,128)(2,1)S(1)}, bf16[192,1536]{1,0:T(8,128)(2,1)S(1)}, u32[]{:S(2)}, u32[]{:S(2)}) collective-permute-start(bf16[192,1536]{1,0:T(8,128)(2,1)S(1)} %collective-permute-done.15), channel_id=1, source_target_pairs={{0,2},{1,7},{2,4},{3,1},{4,6},{5,3},{6,0},{7,5},{8,10},{9,15},{10,... | collective-permute-start | bytes 1769480 | tf_op jit(solution)/shard_map/ppermute | solution.py:78
  61.8 14.6 %collective-permute-start.25 = (bf16[192,1536]{1,0:T(8,128)(2,1)S(1)}, bf16[192,1536]{1,0:T(8,128)(2,1)S(1)}, u32[]{:S(2)}, u32[]{:S(2)}) collective-permute-start(bf16[192,1536]{1,0:T(8,128)(2,1)S(1)} %collective-permute-done.24), channel_id=1, source_target_pairs={{0,8},{1,25},{2,10},{3,27},{4,12},{5,29},{6,14},{7,31},{8,16},{9,1... | collective-permute-start | bytes 1769480 | tf_op jit(solution)/shard_map/ppermute | solution.py:78
  70.3 7.0 %copy-start.35 = (s32[12]{0:T(128)S(1)}, s32[12]{0:T(128)}, u32[]{:S(2)}) copy-start(s32[12]{0:T(128)} %param.15) | copy-start | bytes 148
  70.3 11.5 %copy-start.13 = (bf16[96,3072]{1,0:T(8,128)(2,1)S(1)}, bf16[96,3072]{1,0:T(8,128)(2,1)}, u32[]{:S(2)}) copy-start(bf16[96,3072]{1,0:T(8,128)(2,1)} %param.13) | copy-start | bytes 1769476
  70.3 51.6 %collective-permute-start.8 = (bf16[768,1536]{1,0:T(8,128)(2,1)}, bf16[768,1536]{1,0:T(8,128)(2,1)}, u32[]{:S(2)}, u32[]{:S(2)}) collective-permute-start(bf16[768,1536]{1,0:T(8,128)(2,1)} %constant_dynamic-update-slice_fusion.2), channel_id=1, source_target_pairs={{0,2},{1,7},{2,4},{3,1},{4,6},{5,3},{6,0},{7,5},{8,10},{9,15},{10,... | collective-permute-start | bytes 7077896 | tf_op jit(solution)/shard_map/ppermute | solution.py:78
  73.0 53.6 %copy-start.14 = (bf16[768,1536]{1,0:T(8,128)(2,1)}, bf16[768,1536]{1,0:T(8,128)(2,1)S(1)}, u32[]{:S(2)}) copy-start(bf16[768,1536]{1,0:T(8,128)(2,1)S(1)} %constant_dynamic-update-slice_fusion.9) | copy-start | bytes 7077892
  73.0 9.6 %copy-start.32 = (f32[3072]{0:T(1024)S(1)}, f32[3072]{0:T(1024)}, u32[]{:S(2)}) copy-start(f32[3072]{0:T(1024)} %param.23) | copy-start | bytes 36868
  73.0 50.7 %collective-permute-start.17 = (bf16[768,1536]{1,0:T(8,128)(2,1)S(1)}, bf16[768,1536]{1,0:T(8,128)(2,1)}, u32[]{:S(2)}, u32[]{:S(2)}) collective-permute-start(bf16[768,1536]{1,0:T(8,128)(2,1)S(1)} %constant_dynamic-update-slice_fusion.9), channel_id=1, source_target_pairs={{0,8},{1,25},{2,10},{3,27},{4,12},{5,29},{6,14},{7,31},{8,16},{9,1... | collective-permute-start | bytes 7077896 | tf_op jit(solution)/shard_map/ppermute | solution.py:78
  77.3 50.5 %copy-start.25 = (bf16[64,1536]{1,0:T(8,128)(2,1)S(1)}, bf16[64,1536]{1,0:T(8,128)(2,1)}, u32[]{:S(2)}) copy-start(bf16[64,1536]{1,0:T(8,128)(2,1)} %param.20) | copy-start | bytes 589828
  77.3 46.4 %collective-permute-start.26 = (bf16[768,1536]{1,0:T(8,128)(2,1)}, bf16[768,1536]{1,0:T(8,128)(2,1)}, u32[]{:S(2)}, u32[]{:S(2)}) collective-permute-start(bf16[768,1536]{1,0:T(8,128)(2,1)} %constant_dynamic-update-slice_fusion.16), channel_id=1, source_target_pairs={{0,32},{1,97},{2,34},{3,99},{4,36},{5,101},{6,38},{7,103},{8,40},{... | collective-permute-start | bytes 7077896 | tf_op jit(solution)/shard_map/ppermute | solution.py:78
  81.9 73.1 %copy-start.26 = (bf16[64,1536]{1,0:T(8,128)(2,1)S(1)}, bf16[64,1536]{1,0:T(8,128)(2,1)}, u32[]{:S(2)}) copy-start(bf16[64,1536]{1,0:T(8,128)(2,1)} %param.22) | copy-start | bytes 589828
  121.9 30.4 %collective-permute-start.9 = (bf16[768,1536]{1,0:T(8,128)(2,1)}, bf16[768,1536]{1,0:T(8,128)(2,1)}, u32[]{:S(2)}, u32[]{:S(2)}) collective-permute-start(bf16[768,1536]{1,0:T(8,128)(2,1)} %collective-permute-done.8), channel_id=1, source_target_pairs={{0,2},{1,7},{2,4},{3,1},{4,6},{5,3},{6,0},{7,5},{8,10},{9,15},{10,... | collective-permute-start | bytes 7077896 | tf_op jit(solution)/shard_map/ppermute | solution.py:78
  123.7 30.4 %collective-permute-start.18 = (bf16[768,1536]{1,0:T(8,128)(2,1)}, bf16[768,1536]{1,0:T(8,128)(2,1)}, u32[]{:S(2)}, u32[]{:S(2)}) collective-permute-start(bf16[768,1536]{1,0:T(8,128)(2,1)} %collective-permute-done.17), channel_id=1, source_target_pairs={{0,8},{1,25},{2,10},{3,27},{4,12},{5,29},{6,14},{7,31},{8,16},{9,1... | collective-permute-start | bytes 7077896 | tf_op jit(solution)/shard_map/ppermute | solution.py:78
  123.7 30.4 %collective-permute-start.27 = (bf16[768,1536]{1,0:T(8,128)(2,1)}, bf16[768,1536]{1,0:T(8,128)(2,1)}, u32[]{:S(2)}, u32[]{:S(2)}) collective-permute-start(bf16[768,1536]{1,0:T(8,128)(2,1)} %collective-permute-done.26), channel_id=1, source_target_pairs={{0,32},{1,97},{2,34},{3,99},{4,36},{5,101},{6,38},{7,103},{8,40},{... | collective-permute-start | bytes 7077896 | tf_op jit(solution)/shard_map/ppermute | solution.py:78
  126.6 30.0 %copy-start.28 = (f32[2,3072]{1,0:T(2,128)S(1)}, f32[2,3072]{1,0:T(2,128)}, u32[]{:S(2)}) copy-start(f32[2,3072]{1,0:T(2,128)} %get-tuple-element.79) | copy-start | bytes 73732
  126.9 61.3 %collective-permute-start = (bf16[96,3072]{1,0:T(8,128)(2,1)S(1)}, bf16[96,3072]{1,0:T(8,128)(2,1)S(1)}, u32[]{:S(2)}, u32[]{:S(2)}) collective-permute-start(bf16[96,3072]{1,0:T(8,128)(2,1)S(1)} %fusion.9), channel_id=1, source_target_pairs={{0,1},{1,0},{2,3},{3,2},{4,5},{5,4},{6,7},{7,6},{8,9},{9,8},{10,11... | collective-permute-start | bytes 1769480 | tf_op jit(solution)/shard_map/ppermute | solution.py:55
  152.3 48.9 %collective-permute-start.10 = (bf16[768,1536]{1,0:T(8,128)(2,1)}, bf16[768,1536]{1,0:T(8,128)(2,1)}, u32[]{:S(2)}, u32[]{:S(2)}) collective-permute-start(bf16[768,1536]{1,0:T(8,128)(2,1)} %collective-permute-done.9), channel_id=1, source_target_pairs={{0,2},{1,7},{2,4},{3,1},{4,6},{5,3},{6,0},{7,5},{8,10},{9,15},{10,... | collective-permute-start | bytes 7077896 | tf_op jit(solution)/shard_map/ppermute | solution.py:78
  154.0 47.2 %collective-permute-start.19 = (bf16[768,1536]{1,0:T(8,128)(2,1)}, bf16[768,1536]{1,0:T(8,128)(2,1)}, u32[]{:S(2)}, u32[]{:S(2)}) collective-permute-start(bf16[768,1536]{1,0:T(8,128)(2,1)} %collective-permute-done.18), channel_id=1, source_target_pairs={{0,8},{1,25},{2,10},{3,27},{4,12},{5,29},{6,14},{7,31},{8,16},{9,1... | collective-permute-start | bytes 7077896 | tf_op jit(solution)/shard_map/ppermute | solution.py:78
  154.1 47.1 %collective-permute-start.28 = (bf16[768,1536]{1,0:T(8,128)(2,1)}, bf16[768,1536]{1,0:T(8,128)(2,1)}, u32[]{:S(2)}, u32[]{:S(2)}) collective-permute-start(bf16[768,1536]{1,0:T(8,128)(2,1)} %collective-permute-done.27), channel_id=1, source_target_pairs={{0,32},{1,97},{2,34},{3,99},{4,36},{5,101},{6,38},{7,103},{8,40},{... | collective-permute-start | bytes 7077896 | tf_op jit(solution)/shard_map/ppermute | solution.py:78
  155.0 32.3 %collective-permute-start.1 = (bf16[128,1536]{1,0:T(8,128)(2,1)S(1)}, bf16[128,1536]{1,0:T(8,128)(2,1)S(1)}, u32[]{:S(2)}, u32[]{:S(2)}) collective-permute-start(bf16[128,1536]{1,0:T(8,128)(2,1)S(1)} %constant_dynamic-update-slice_fusion), channel_id=1, source_target_pairs={{0,2},{2,0},{1,3},{3,1},{4,6},{6,4},{5,7},{7,5},{8,10},{10,8},{9,1... | collective-permute-start | bytes 1179656 | tf_op jit(solution)/shard_map/ppermute | solution.py:422
  201.2 33.1 %copy-start.27 = (f32[2,3072]{1,0:T(2,128)S(1)}, f32[2,3072]{1,0:T(2,128)}, u32[]{:S(2)}) copy-start(f32[2,3072]{1,0:T(2,128)} %get-tuple-element.80) | copy-start | bytes 73732
  201.2 35.3 %copy-start.15 = (bf16[96,3072]{1,0:T(8,128)(2,1)S(1)}, bf16[96,3072]{1,0:T(8,128)(2,1)}, u32[]{:S(2)}) copy-start(bf16[96,3072]{1,0:T(8,128)(2,1)} %param.14) | copy-start | bytes 1769476
  201.3 35.3 %copy-start.30 = (f32[3072]{0:T(1024)S(1)}, f32[3072]{0:T(1024)}, u32[]{:S(2)}) copy-start(f32[3072]{0:T(1024)} %param.25) | copy-start | bytes 36868
  201.3 35.3 %copy-start.33 = (f32[96]{0:T(128)S(1)}, f32[96]{0:T(128)}, u32[]{:S(2)}) copy-start(f32[96]{0:T(128)} %get-tuple-element.38) | copy-start | bytes 1156
  201.3 35.3 %copy-start.34 = (f32[96]{0:T(128)S(1)}, f32[96]{0:T(128)}, u32[]{:S(2)}) copy-start(f32[96]{0:T(128)} %get-tuple-element.39) | copy-start | bytes 1156
  221.5 6.4 %copy-start.2 = (bf16[2,3072,1536]{2,1,0:T(8,128)(2,1)}, bf16[2,3072,1536]{2,1,0:T(8,128)(2,1)S(1)}, u32[]{:S(2)}) copy-start(bf16[2,3072,1536]{2,1,0:T(8,128)(2,1)S(1)} %get-tuple-element.24.down) | copy-start | bytes 56623108
  227.9 6.5 %copy-start.5 = (bf16[2,3072,1536]{2,1,0:T(8,128)(2,1)}, bf16[2,3072,1536]{2,1,0:T(8,128)(2,1)S(1)}, u32[]{:S(2)}) copy-start(bf16[2,3072,1536]{2,1,0:T(8,128)(2,1)S(1)} %get-tuple-element.23.up) | copy-start | bytes 56623108
  234.4 2.2 collective-permute-start.29
  238.8 2.4 collective-permute-start.30
  242.1 6.4 %copy-start.3 = (bf16[2,3072,1536]{2,1,0:T(8,128)(2,1)S(1)}, bf16[2,3072,1536]{2,1,0:T(8,128)(2,1)}, u32[]{:S(2)}) copy-start(bf16[2,3072,1536]{2,1,0:T(8,128)(2,1)} %copy-done.2) | copy-start | bytes 56623108
  248.5 6.4 %copy-start.6 = (bf16[2,3072,1536]{2,1,0:T(8,128)(2,1)S(1)}, bf16[2,3072,1536]{2,1,0:T(8,128)(2,1)}, u32[]{:S(2)}) copy-start(bf16[2,3072,1536]{2,1,0:T(8,128)(2,1)} %copy-done.5) | copy-start | bytes 56623108
  276.4 3.5 copy-start.20
  276.4 3.5 copy-start.21
  276.4 3.5 copy-start.31
  276.4 3.2 collective-permute-start.31
  279.9 4.6 %copy-start.8 = (f32[2,192,1536]{2,1,0:T(8,128)S(1)}, f32[2,192,1536]{2,1,0:T(8,128)}, u32[]{:S(2)}) copy-start(f32[2,192,1536]{2,1,0:T(8,128)} %get-tuple-element.28.slope_gen) | copy-start | bytes 7077892
  279.9 4.6 %copy-start.9 = (f32[2,192,1536]{2,1,0:T(8,128)S(1)}, f32[2,192,1536]{2,1,0:T(8,128)}, u32[]{:S(2)}) copy-start(f32[2,192,1536]{2,1,0:T(8,128)} %get-tuple-element.29.slope_fake) | copy-start | bytes 7077892
  281.4 3.0 copy-start.7
  281.4 3.0 copy-start.10
  281.4 3.0 copy-start.11
  281.4 3.1 copy-start.12
  281.5 2.9 collective-permute-start.32
  284.5 6.4 %copy-start.4 = (bf16[2,3072,1536]{2,1,0:T(8,128)(2,1)S(1)}, bf16[2,3072,1536]{2,1,0:T(8,128)(2,1)}, u32[]{:S(2)}) copy-start(bf16[2,3072,1536]{2,1,0:T(8,128)(2,1)} %copy-done.2) | copy-start | bytes 56623108
  304.4 2.0 collective-permute-start.33
  310.7 30.0 %copy-start.1 = (bf16[3072,64]{0,1:T(8,128)(2,1)S(1)}, bf16[3072,64]{0,1:T(8,128)(2,1)}, u32[]{:S(2)}) copy-start(bf16[3072,64]{0,1:T(8,128)(2,1)} %param.19) | copy-start | bytes 1179652
  (7 other events, 9.5 us)
Sparse Core Ops, SparseCore 0:
  11.3 97.7 all-gather.1

commit v4 on v3

--- a/solution.py
+++ b/solution.py
@@ -1,3 +1,4 @@
+import functools
 import math
 
 import jax
@@ -70,20 +71,34 @@
     return pairs
 
 
-def ring_slots(pieces):
-    for phase in range(3):
-        slots = [[piece] for piece in pieces]
-        for _ in range(RING - 1):
-            for i, held in enumerate(slots):
-                held.append(lax.ppermute(held[-1], AXES, chip_ring(RING_AXES[i][phase])))
-        if phase < 2:
-            pieces = [jnp.concatenate(held, axis=0) for held in slots]
+def ring(pieces, phase):
+    slots = [[piece] for piece in pieces]
+    for _ in range(RING - 1):
+        for i, held in enumerate(slots):
+            held.append(lax.ppermute(held[-1], AXES, chip_ring(RING_AXES[i][phase])))
     return slots
+
+
+def ring_slots(pieces, early, middle):
+    slots = ring([jnp.concatenate(held, axis=0) for held in ring(pieces, 0)], 1)
+    halves = [[jnp.concatenate(held[2 * h : 2 * h + 2], axis=0) for held in slots] for h in range(2)]
+    halves[0], early = lax.optimization_barrier((halves[0], early))
+    found = [[[piece] for piece in half] for half in halves]
+    for step in range(1, RING):
+        for h in range(2):
+            for i in range(3):
+                found[h][i].append(lax.ppermute(found[h][i][-1], AXES, chip_ring(RING_AXES[i][2])))
+        if step == RING - 2:
+            held = [found[0][i][-1] for i in range(3)]
+            held, middle = lax.optimization_barrier((held, middle))
+            for i in range(3):
+                found[0][i][-1] = held[i]
+    return found, early, middle
 
 
 PIECE = 48
 TILE = 256
-SCOPED = 20 * 2**20
+MIB = 2**20
 ANYWHERE = pl.BlockSpec(memory_space=pl.ANY)
 IN_VMEM = pl.BlockSpec(memory_space=pltpu.VMEM)
 IN_SMEM = pl.BlockSpec(memory_space=pltpu.SMEM)
@@ -105,7 +120,7 @@
     return pre * half, slope
 
 
-def start_slot(place_ref, i, step, slot, target, part, sem):
+def start_slot(place_ref, half, i, step, slot, target, part, sem):
     me = {"z": place_ref[0], "y": place_ref[1], "x": place_ref[2]}
     direction = place_ref[3]
     first, second, third = RING_AXES[i]
@@ -116,7 +131,7 @@
     def one(k, carry):
         at = {
             first: source(first, lax.rem(k, RING)),
-            second: source(second, lax.div(k, RING)),
+            second: source(second, 2 * half + lax.div(k, RING)),
             third: source(third, step),
         }
         quarter = lax.rem(at["x"], 2)
@@ -125,7 +140,7 @@
         pltpu.make_async_copy(slot.at[k], target.at[quarter, rows], sem).start()
         return carry
 
-    lax.fori_loop(0, 16, one, 0, unroll=4)
+    lax.fori_loop(0, 2 * RING, one, 0, unroll=4)
 
 
 def wait_slot(slot, sem):
@@ -133,25 +148,25 @@
 
 
 def load_body(place_ref, *refs):
-    slots, (whole, up, down, sems) = refs[:9], refs[9:]
+    slots, (whole, up, down, sems) = refs[:18], refs[18:]
     targets = ((up, 0), (up, 1), (down, 0))
-    for step in range(3):
-        for i, (target, part) in enumerate(targets):
-            n = step * 3 + i
-            start_slot(place_ref, i, step, slots[n], target, part, sems.at[n])
+    for n, slot in enumerate(slots):
+        step, half, i = n // 6, n // 3 % 2, n % 3
+        target, part = targets[i]
+        start_slot(place_ref, half, i, step, slot, target, part, sems.at[n])
 
     def one(group, carry):
         rows = pl.ds(pl.multiple_of(group * 2 * PIECE + PIECE, 16), PIECE)
         for quarter in range(2):
             pltpu.make_async_copy(
-                whole.at[group, quarter], down.at[quarter, rows], sems.at[9]
+                whole.at[group, quarter], down.at[quarter, rows], sems.at[18]
             ).start()
         return carry
 
     lax.fori_loop(0, 32, one, 0, unroll=2)
-    for n in range(9):
-        wait_slot(slots[n], sems.at[n])
-    wait_slot(whole, sems.at[9])
+    for n, slot in enumerate(slots):
+        wait_slot(slot, sems.at[n])
+    wait_slot(whole, sems.at[18])
 
 
 def weights_shape(width, hidden):
@@ -163,15 +178,20 @@
 
 
 def load_weights(coords, slots, whole, width, hidden):
-    flat = [slots[i][step].reshape(16, PIECE, hidden) for step in range(3) for i in range(3)]
+    flat = [
+        slots[half][i][step].reshape(2 * RING, PIECE, hidden)
+        for step in range(3)
+        for half in range(2)
+        for i in range(3)
+    ]
     shape = weights_shape(width, hidden)
     return pl.pallas_call(
         load_body,
         out_shape=(shape, shape),
-        in_specs=[IN_SMEM] + [ANYWHERE] * 10,
+        in_specs=[IN_SMEM] + [ANYWHERE] * 19,
         out_specs=(IN_VMEM, IN_VMEM),
-        scratch_shapes=[pltpu.SemaphoreType.DMA((10,))],
-        compiler_params=pltpu.CompilerParams(vmem_limit_bytes=SCOPED),
+        scratch_shapes=[pltpu.SemaphoreType.DMA((19,))],
+        compiler_params=pltpu.CompilerParams(vmem_limit_bytes=4 * MIB),
         cost_estimate=pl.CostEstimate(
             flops=0, bytes_accessed=13 * 16 * PIECE * hidden * 4, transcendentals=0
         ),
@@ -179,15 +199,16 @@
     )(coords, *flat, whole.reshape(32, 2, PIECE, hidden))
 
 
-def gen_body(
-    place_ref, u, low, adapt, slot_a, slot_b, slot_c, up_in, down_in, up, down, slope, mine, other, act, sems
-):
+def gen_body(place_ref, u, low, adapt, *refs):
+    slots, (_, _, up, down, slope, mine, other, act, sems) = refs[:6], refs[6:]
     rows = mine.shape[0]
-    start_slot(place_ref, 0, 3, slot_a, up, 0, sems.at[0])
-    start_slot(place_ref, 1, 3, slot_b, up, 1, sems.at[1])
-    start_slot(place_ref, 2, 3, slot_c, down, 0, sems.at[2])
-    wait_slot(slot_a, sems.at[0])
-    wait_slot(slot_b, sems.at[1])
+    targets = ((up, 0), (up, 1), (down, 0))
+    for i, (target, part) in enumerate(targets):
+        for half in range(2):
+            n = 2 * i + half
+            start_slot(place_ref, half, i, 3, slots[n], target, part, sems.at[n])
+    for n in range(4):
+        wait_slot(slots[n], sems.at[n])
     for q in range(2):
 
         def hidden_tile(n, carry, q=q):
@@ -198,7 +219,8 @@
             return carry
 
         lax.fori_loop(0, up.shape[2] // TILE, hidden_tile, 0)
-    wait_slot(slot_c, sems.at[2])
+    for n in range(4, 6):
+        wait_slot(slots[n], sems.at[n])
 
     def width_tile(n, carry):
         cols = pl.ds(pl.multiple_of(n * TILE, TILE), TILE)
@@ -216,7 +238,9 @@
     rows = group // 2
     shape = weights_shape(width, hidden)
     f32, bf16 = jnp.float32, jnp.bfloat16
-    last = [slots[i][3].reshape(16, PIECE, hidden) for i in range(3)]
+    last = [
+        slots[half][i][3].reshape(2 * RING, PIECE, hidden) for i in range(3) for half in range(2)
+    ]
     return pl.pallas_call(
         gen_body,
         out_shape=(
@@ -226,11 +250,11 @@
             jax.ShapeDtypeStruct((rows, width), f32),
             jax.ShapeDtypeStruct((rows, width), bf16),
         ),
-        in_specs=[IN_SMEM] + [IN_VMEM] * 3 + [ANYWHERE] * 3 + [IN_VMEM] * 2,
+        in_specs=[IN_SMEM] + [IN_VMEM] * 3 + [ANYWHERE] * 6 + [IN_VMEM] * 2,
         out_specs=(IN_VMEM,) * 5,
-        scratch_shapes=[pltpu.VMEM((2, group, hidden), bf16), pltpu.SemaphoreType.DMA((3,))],
-        input_output_aliases={7: 0, 8: 1},
-        compiler_params=pltpu.CompilerParams(vmem_limit_bytes=SCOPED),
+        scratch_shapes=[pltpu.VMEM((2, group, hidden), bf16), pltpu.SemaphoreType.DMA((6,))],
+        input_output_aliases={10: 0, 11: 1},
+        compiler_params=pltpu.CompilerParams(vmem_limit_bytes=12 * MIB),
         cost_estimate=pl.CostEstimate(
             flops=8 * group * width * hidden,
             bytes_accessed=10 * 2**20,
@@ -247,8 +271,7 @@
     group = 2 * rows
     u[:rows] = u_mine[...]
     u[rows:] = u_other[...]
-    low = dot(u[...], adapt_in[...]).astype(low_ref.dtype)
-    low_ref[...] = low
+    low_ref[...] = dot(u[...], adapt_in[...], NT).astype(low_ref.dtype)
     for q in range(2):
 
         def hidden_tile(n, carry, q=q):
@@ -283,7 +306,7 @@
         score_body,
         out_shape=(
             jax.ShapeDtypeStruct((2, group, hidden), f32),
-            jax.ShapeDtypeStruct((group, adapt_in.shape[1]), bf16),
+            jax.ShapeDtypeStruct((group, adapt_in.shape[0]), bf16),
             jax.ShapeDtypeStruct((rows, width), f32),
             jax.ShapeDtypeStruct((rows, width), f32),
             jax.ShapeDtypeStruct((group, width), bf16),
@@ -291,7 +314,7 @@
         in_specs=[IN_VMEM] * 6,
         out_specs=(IN_VMEM,) * 5,
         scratch_shapes=[pltpu.VMEM((group, width), bf16), pltpu.VMEM((2, 2 * group, hidden), bf16)],
-        compiler_params=pltpu.CompilerParams(vmem_limit_bytes=SCOPED),
+        compiler_params=pltpu.CompilerParams(vmem_limit_bytes=16 * MIB),
         cost_estimate=pl.CostEstimate(
             flops=12 * group * width * hidden,
             bytes_accessed=10 * 2**20,
@@ -344,12 +367,88 @@
         in_specs=[IN_VMEM] * 9,
         out_specs=(IN_VMEM,) * 2,
         scratch_shapes=[pltpu.VMEM((2 * group, width), bf16)],
-        compiler_params=pltpu.CompilerParams(vmem_limit_bytes=SCOPED),
+        compiler_params=pltpu.CompilerParams(vmem_limit_bytes=16 * MIB),
         cost_estimate=pl.CostEstimate(
             flops=8 * group * width * hidden, bytes_accessed=10 * 2**20, transcendentals=0
         ),
         name="backward",
     )(cots_mine, cots_other, slope_gen, slope_fake, low_gen, low_fake, gen_out, fake_out, in_vmem(down))
+
+
+STRIP = 16
+
+
+def noise_body(ends, blends, given, noise, mine, other, mods, gate, latents_ref, noised_ref, u_ref):
+    f32 = jnp.float32
+
+    def strip(n, carry):
+        rows = pl.ds(pl.multiple_of(n * STRIP, STRIP), STRIP)
+        in_last = n * STRIP + lax.broadcasted_iota(jnp.int32, (STRIP, 1), 0) >= ends[0]
+        out = mine[rows] + other[rows].astype(f32)
+        latents = (given[rows].astype(f32) + gate[...] * out).astype(latents_ref.dtype)
+        latents_ref[rows] = latents
+        blend = jnp.where(in_last, blends[1], blends[0])
+        noised = (
+            (1.0 - blend) * latents.astype(f32) + blend * noise[rows].astype(f32)
+        ).astype(noised_ref.dtype)
+        noised_ref[rows] = noised
+        scale = jnp.where(in_last, mods[1:2], mods[0:1])
+        shift = jnp.where(in_last, mods[3:4], mods[2:3])
+        u_ref[rows] = modulate(noised, scale, shift)
+        return carry
+
+    lax.fori_loop(0, given.shape[0] // STRIP, strip, 0)
+
+
+def add_noise(ends, blends, given, noise, mine, other, mods, gate):
+    shape = jax.ShapeDtypeStruct(given.shape, given.dtype)
+    return pl.pallas_call(
+        noise_body,
+        out_shape=(shape,) * 3,
+        in_specs=[IN_SMEM] * 2 + [IN_VMEM] * 6,
+        out_specs=(IN_VMEM,) * 3,
+        compiler_params=pltpu.CompilerParams(vmem_limit_bytes=10 * MIB),
+        cost_estimate=pl.CostEstimate(flops=0, bytes_accessed=6 * MIB, transcendentals=0),
+        name="add_noise",
+    )(ends, blends, given, noise, mine, other, mods, gate)
+
+
+def cotangent_body(scale, real, fake, others, gate_ref, noise, latents, noised, diff_ref, cots):
+    f32 = jnp.float32
+    count = real.shape[0]
+
+    def strip(n, carry):
+        start = pl.multiple_of(n * STRIP, STRIP)
+        rows, second = pl.ds(start, STRIP), pl.ds(count + start, STRIP)
+        gate = gate_ref[...]
+        out_real = real[rows] + others[rows].astype(f32)
+        out_fake = fake[rows] + others[second].astype(f32)
+        diff = (gate * (out_fake - out_real)).astype(diff_ref.dtype)
+        diff_ref[rows] = diff
+        cots[rows] = (gate * diff.astype(f32) * scale).astype(cots.dtype)
+        target = noise[rows].astype(f32) - latents[rows].astype(f32)
+        cots[second] = (
+            gate * (noised[rows].astype(f32) + gate * out_fake - target) * scale
+        ).astype(cots.dtype)
+        return carry
+
+    lax.fori_loop(0, count // STRIP, strip, 0)
+
+
+def cotangents(scale, real, fake, others, gate, noise, latents, noised):
+    rows, width = real.shape
+    return pl.pallas_call(
+        functools.partial(cotangent_body, scale),
+        out_shape=(
+            jax.ShapeDtypeStruct((rows, width), noise.dtype),
+            jax.ShapeDtypeStruct((2 * rows, width), noise.dtype),
+        ),
+        in_specs=[IN_VMEM] * 7,
+        out_specs=(IN_VMEM,) * 2,
+        compiler_params=pltpu.CompilerParams(vmem_limit_bytes=12 * MIB),
+        cost_estimate=pl.CostEstimate(flops=0, bytes_accessed=8 * MIB, transcendentals=0),
+        name="cotangents",
+    )(real, fake, others, gate, noise, latents, noised)
 
 
 def three_terms(value):
@@ -394,12 +493,7 @@
 
     def modulation(steps):
         embed = embedding(two_steps(steps), width)
-        scale = 1.0 + modulation_scale[None, :] * embed
-        shift = modulation_shift[None, :] * embed
-        return (
-            jnp.where(in_last, scale[1:], scale[:1]),
-            jnp.where(in_last, shift[1:], shift[:1]),
-        )
+        return 1.0 + modulation_scale[None, :] * embed, modulation_shift[None, :] * embed
 
     def both_rows(mine):
         return jnp.concatenate([mine, swap_cores(mine)], axis=0)
@@ -415,42 +509,45 @@
     down_rows = base_down.T
     half = base_up.shape[0] // 2
     last_quarter = lax.all_gather(down_rows[half:], CHIPS, axis=0, tiled=True)
-    slots = ring_slots([base_up[:half], base_up[half:], down_rows[:half]])
-    up_part, down_part = load_weights(coords, slots, last_quarter, width, hidden)
-
     def other_quarter(mine):
         theirs = lax.ppermute(mine, "xl", [(0, 1), (1, 0)])
         return jnp.stack([jnp.where(xl == 0, mine, theirs), jnp.where(xl == 0, theirs, mine)])
 
     adapt_out = other_quarter(jnp.concatenate([gen_adapt_out, fake_adapt_out], axis=0))
-    gen_out, fake_out = adapt_out[:, :rank], adapt_out[:, rank:]
-
-    u_mine = modulate(gen_input, *modulation(gen_steps))
+    gen_scale, gen_shift = modulation(gen_steps)
+    u_mine = modulate(
+        gen_input,
+        jnp.where(in_last, gen_scale[1:], gen_scale[:1]),
+        jnp.where(in_last, gen_shift[1:], gen_shift[:1]),
+    )
     u_gen = both_rows(u_mine)
     low_gen = matmul(u_gen, gen_adapt_in).astype(bf16)
+    mods = jnp.concatenate(modulation(score_steps), axis=0)
+    blends = (two_steps(score_steps).astype(f32) + 0.5) / 1000.0
+    ends = (last_image * IMG_TOK - first_row).astype(jnp.int32).reshape(1)
+    slots, adapt_out, prepared = ring_slots(
+        [base_up[:half], base_up[half:], down_rows[:half]],
+        adapt_out,
+        (u_gen, low_gen, mods, blends, ends, coords),
+    )
+    u_gen, low_gen, mods, blends, ends, coords = prepared
+    gen_out, fake_out = adapt_out[:, :rank], adapt_out[:, rank:]
+    up_part, down_part = load_weights(coords, slots, last_quarter, width, hidden)
+
     up_all, down_all, slope_gen, out_mine, out_other = gen_forward(
         coords, u_gen, low_gen, gen_out, slots, up_part, down_part
     )
-    out_mine = out_mine + swap_cores(out_other).astype(f32)
-    latents = (gen_input.astype(f32) + output_gate * out_mine).astype(bf16)
-    two_blend = (two_steps(score_steps).astype(f32) + 0.5) / 1000.0
-    blend = jnp.where(in_last, two_blend[1], two_blend[0])
-    noised = ((1.0 - blend) * latents.astype(f32) + blend * noise_score.astype(f32)).astype(bf16)
-    u_score = modulate(noised, *modulation(score_steps))
+    gate = output_gate.reshape(1, width)
+    latents, noised, u_score = add_noise(
+        ends, blends, gen_input, noise_score, out_mine, swap_cores(out_other), mods, gate
+    )
     u_score_other = swap_cores(u_score)
     slope_fake, low_fake, out_real, out_fake, outs_other = score_forward(
-        u_score, u_score_other, fake_adapt_in, fake_out, up_all, down_all
-    )
-    got = swap_cores(outs_other).astype(f32)
-    out_real = out_real + got[:shard_rows]
-    out_fake = out_fake + got[shard_rows:]
-    score_diff = (output_gate * (out_fake - out_real)).astype(bf16)
-    cot_gen = (output_gate * score_diff.astype(f32) * loss_scale).astype(bf16)
-    target = noise_score.astype(f32) - latents.astype(f32)
-    cot_fake = (
-        output_gate * (noised.astype(f32) + output_gate * out_fake - target) * loss_scale
-    ).astype(bf16)
-    cots = jnp.concatenate([cot_gen, cot_fake], axis=0)
+        u_score, u_score_other, fake_adapt_in.T, fake_out, up_all, down_all
+    )
+    score_diff, cots = cotangents(
+        loss_scale, out_real, out_fake, swap_cores(outs_other), gate, noise_score, latents, noised
+    )
     out_grads, mix = backward(
         cots, swap_cores(cots), slope_gen, slope_fake, low_gen, low_fake, gen_out, fake_out, down_all
     )

time: 348 us -> 371 us (1.066)
  local copies, waits for them, and re-layouts: 56.1 us -> 88.8 us
  waiting for transfers between devices: 140 us -> 117 us
  starting transfers between devices: 26.3 us -> 37.1 us
  Pallas kernels: 65.8 us -> 71.1 us
  other arithmetic: 14.7 us -> 10.9 us
    ppermute x1, waiting for transfers between devices: 30.1 us -> 0.01 us  [other_quarter(): theirs = lax.ppermute(mine, 'xl', [(0, 1), (1, 0)])]
    unnamed x89 -> x127, local copies, waits for them, and re-layouts: 44.2 us -> 74.1 us
    ppermute x27 -> x36, starting transfers between devices: 22.5 us -> 34.9 us  [the longest x18 17.5 us: ring_slots(): lax.ppermute(found[h][i][-1], AXES, chip_ring(RING_AXES[i][2]))]
    ppermute x27 -> x36, waiting for transfers between devices: 102 us -> 107 us  [the longest x18 56.5 us: ring(): held.append(lax.ppermute(held[-1], AXES, chip_ring(RING_AXES[i][phase])))]
  transfers between devices with their start and end apart: 35 -> 44, of which waited for: 23 -> 23; matrix products, arithmetic and copies ran while one was open for 8% -> 7% of each run, Pallas kernels for 3% -> 4%
where the time goes in v4:
time: 371 us; the launch traced here: 370 us
  waiting for transfers between devices  117 us (32%)
  local copies, waits for them, and re-layouts  88.8 us (24%)
  Pallas kernels  71.1 us (19%)
  starting transfers between devices  37.1 us (10%)
  blocking collectives  28.1 us (8%)
  between operations  14.7 us (4%)
  other arithmetic  10.9 us (3%)
    unnamed x127, local copies, waits for them, and re-layouts  74.1 us
    ppermute x18, waiting for transfers between devices, ring(): held.append(lax.ppermute(held[-1], AXES, chip_ring(RING_AXES[i][phase])))  56.5 us
    ppermute x18, waiting for transfers between devices, ring_slots(): lax.ppermute(found[h][i][-1], AXES, chip_ring(RING_AXES[i][2]))  50.7 us
    all_to_all x1, blocking collectives, local(): received = lax.all_to_all(packed, CHIPS, 0, 0, tiled=True)  28.1 us
    pallas_call x1, Pallas kernels, gen_forward(): pl.pallas_call(gen_body, out_shape=(shape, shape, jax.ShapeDtypeStruct((2...  20 us
    pallas_call x1, Pallas kernels, score_forward(): pl.pallas_call(score_body, out_shape=(jax.ShapeDtypeStruct((2, group, hid...  20 us
    ppermute x18, starting transfers between devices, ring_slots(): lax.ppermute(found[h][i][-1], AXES, chip_ring(RING_AXES[i][2]))  17.5 us
    ppermute x18, starting transfers between devices, ring(): held.append(lax.ppermute(held[-1], AXES, chip_ring(RING_AXES[i][phase])))  17.4 us
  transfers between devices with their start and end apart: 44, of which 23 were waited for; matrix products, arithmetic and copies ran while one was open for 7% of the time, Pallas kernels for 4%

profile of v4, /device:TPU:0, one launch (start us, length us, event | category | flops | bytes accessed | tf_op | source)
XLA Modules:
  0.0 370.3 jit_solution(10491059007416553867)
XLA Ops:
  7.3 1.8 fusion.28
  10.2 1.7 collective-permute-start.12
  12.3 1.7 fusion.29
  14.0 2.0 collective-permute-start.4
  16.0 1.6 collective-permute-start
  18.2 1.4 add_convert_fusion
  19.5 1.4 add_multiply_fusion
  24.2 2.2 collective-permute-start.9
  26.4 1.9 collective-permute-start.5
  28.3 1.6 collective-permute-start.1
  39.1 1.2 collective-permute-start.11
  41.3 1.6 collective-permute-start.3
  44.7 9.0 %collective-permute-done.11 = bf16[192,1536]{1,0:T(8,128)(2,1)S(1)} collective-permute-done((bf16[192,1536]{1,0:T(8,128)(2,1)S(1)}, bf16[192,1536]{1,0:T(8,128)(2,1)S(1)}, u32[]{:S(2)}, u32[]{:S(2)}) %collective-permute-start.11) | collective-permute-done | bytes 589856 | tf_op jit(solution)/shard_map/ppermute | solution.py:78
  54.3 2.9 collective-permute-done.3
  57.2 1.2 collective-permute-done.7
  59.3 6.3 %collective-permute-done.33 = bf16[192,1536]{1,0:T(8,128)(2,1)S(1)} collective-permute-done((bf16[192,1536]{1,0:T(8,128)(2,1)S(1)}, bf16[192,1536]{1,0:T(8,128)(2,1)S(1)}, u32[]{:S(2)}, u32[]{:S(2)}) %collective-permute-start.33) | collective-permute-done | bytes 589856 | tf_op jit(solution)/shard_map/ppermute | solution.py:78
  67.3 2.3 collective-permute-done.27
  69.6 1.8 collective-permute-start.17
  71.4 17.8 %collective-permute-done.34 = bf16[192,1536]{1,0:T(8,128)(2,1)S(1)} collective-permute-done((bf16[192,1536]{1,0:T(8,128)(2,1)S(1)}, bf16[192,1536]{1,0:T(8,128)(2,1)S(1)}, u32[]{:S(2)}, u32[]{:S(2)}) %collective-permute-start.34) | collective-permute-done | bytes 589856 | tf_op jit(solution)/shard_map/ppermute | solution.py:78
  89.3 1.4 collective-permute-start.35
  91.0 17.5 %collective-permute-done.13 = bf16[384,1536]{1,0:T(8,128)(2,1)} collective-permute-done((bf16[384,1536]{1,0:T(8,128)(2,1)S(1)}, bf16[384,1536]{1,0:T(8,128)(2,1)}, u32[]{:S(2)}, u32[]{:S(2)}) %collective-permute-start.13) | collective-permute-done | bytes 1179680 | tf_op jit(solution)/shard_map/ppermute | solution.py:90
  108.5 1.6 collective-permute-start.22
  110.9 3.8 %collective-permute-done.28 = bf16[192,1536]{1,0:T(8,128)(2,1)S(1)} collective-permute-done((bf16[192,1536]{1,0:T(8,128)(2,1)S(1)}, bf16[192,1536]{1,0:T(8,128)(2,1)S(1)}, u32[]{:S(2)}, u32[]{:S(2)}) %collective-permute-start.28) | collective-permute-done | bytes 589856 | tf_op jit(solution)/shard_map/ppermute | solution.py:78
  115.7 1.7 collective-permute-start.16
  117.4 10.2 %collective-permute-done.22 = bf16[192,1536]{1,0:T(8,128)(2,1)S(1)} collective-permute-done((bf16[192,1536]{1,0:T(8,128)(2,1)S(1)}, bf16[192,1536]{1,0:T(8,128)(2,1)S(1)}, u32[]{:S(2)}, u32[]{:S(2)}) %collective-permute-start.22) | collective-permute-done | bytes 589856 | tf_op jit(solution)/shard_map/ppermute | solution.py:78
  127.7 1.5 collective-permute-start.23
  130.2 1.5 collective-permute-start.29
  132.4 1.6 convolution_convert_fusion.low.low_gen
  134.0 1.3 pad_maximum_fusion.u
  136.1 9.2 %collective-permute-done.18 = bf16[384,1536]{1,0:T(8,128)(2,1)} collective-permute-done((bf16[384,1536]{1,0:T(8,128)(2,1)}, bf16[384,1536]{1,0:T(8,128)(2,1)}, u32[]{:S(2)}, u32[]{:S(2)}) %collective-permute-start.18) | collective-permute-done | bytes 1179680 | tf_op jit(solution)/shard_map/ppermute | solution.py:90
  148.3 1.5 collective-permute-start.20
  149.8 1.5 collective-permute-start.26
  151.2 6.7 %collective-permute-done.36 = bf16[384,1536]{1,0:T(8,128)(2,1)} collective-permute-done((bf16[384,1536]{1,0:T(8,128)(2,1)S(1)}, bf16[384,1536]{1,0:T(8,128)(2,1)}, u32[]{:S(2)}, u32[]{:S(2)}) %collective-permute-start.36) | collective-permute-done | bytes 1179680 | tf_op jit(solution)/shard_map/ppermute | solution.py:90
  158.0 5.8 %collective-permute-done.24 = bf16[384,1536]{1,0:T(8,128)(2,1)} collective-permute-done((bf16[384,1536]{1,0:T(8,128)(2,1)}, bf16[384,1536]{1,0:T(8,128)(2,1)}, u32[]{:S(2)}, u32[]{:S(2)}) %collective-permute-start.24) | collective-permute-done | bytes 1179680 | tf_op jit(solution)/shard_map/ppermute | solution.py:90
  163.8 1.6 collective-permute-start.37
  165.7 1.5 collective-permute-start.25
  167.1 9.2 %collective-permute-done.20 = bf16[384,1536]{1,0:T(8,128)(2,1)S(1)} collective-permute-done((bf16[384,1536]{1,0:T(8,128)(2,1)}, bf16[384,1536]{1,0:T(8,128)(2,1)S(1)}, u32[]{:S(2)}, u32[]{:S(2)}) %collective-permute-start.20) | collective-permute-done | bytes 1179680 | tf_op jit(solution)/shard_map/ppermute | solution.py:90
  177.4 1.4 collective-permute-start.31
  179.6 1.3 copy-done.13
  180.9 1.3 copy-done.19
  182.1 1.3 copy-done.22
  183.4 14.1 %load_weights.1 = (bf16[2,3072,1536]{2,1,0:T(8,128)(2,1)S(1)}, bf16[2,3072,1536]{2,1,0:T(8,128)(2,1)S(1)}) custom-call(s32[4]{0:T(128)S(1)} %pad_add_fusion.place_ref, bf16[8,48,1536]{2,1,0:T(8,128)(2,1)S(1)} %bitcast.60, bf16[8,48,1536]{2,1,0:T(8,128)(2,1)} %bitcast.19.refs_1_, bf16[8,48,1536]{2,1,0:T(8,128)(2,1)} %bitcast.20.refs_2_, ...), custom_call_target="tpu_custom_call" | custom-call | bytes 61341696 | tf_op jit(solution)/shard_map/load_weights/pallas_call | solution.py:188
  197.6 6.4 %copy-done.2 = bf16[2,3072,1536]{2,1,0:T(8,128)(2,1)} copy-done((bf16[2,3072,1536]{2,1,0:T(8,128)(2,1)}, bf16[2,3072,1536]{2,1,0:T(8,128)(2,1)S(1)}, u32[]{:S(2)}) %copy-start.2) | copy-done | bytes 18874392
  204.0 6.4 %copy-done.7 = bf16[2,3072,1536]{2,1,0:T(8,128)(2,1)} copy-done((bf16[2,3072,1536]{2,1,0:T(8,128)(2,1)}, bf16[2,3072,1536]{2,1,0:T(8,128)(2,1)S(1)}, u32[]{:S(2)}) %copy-start.7) | copy-done | bytes 18874392
  210.4 6.4 %copy-done.3 = bf16[2,3072,1536]{2,1,0:T(8,128)(2,1)S(1)} copy-done((bf16[2,3072,1536]{2,1,0:T(8,128)(2,1)S(1)}, bf16[2,3072,1536]{2,1,0:T(8,128)(2,1)}, u32[]{:S(2)}) %copy-start.3) | copy-done | bytes 18874392
  216.8 6.4 %copy-done.8 = bf16[2,3072,1536]{2,1,0:T(8,128)(2,1)S(1)} copy-done((bf16[2,3072,1536]{2,1,0:T(8,128)(2,1)S(1)}, bf16[2,3072,1536]{2,1,0:T(8,128)(2,1)}, u32[]{:S(2)}) %copy-start.8) | copy-done | bytes 18874392
  223.1 20.0 %gen_forward.1 = (bf16[2,3072,1536]{2,1,0:T(8,128)(2,1)S(1)}, bf16[2,3072,1536]{2,1,0:T(8,128)(2,1)S(1)}, f32[2,192,1536]{2,1,0:T(8,128)}, f32[96,3072]{1,0:T(8,128)S(1)}, bf16[96,3072]{1,0:T(8,128)(2,1)S(1)}) custom-call(s32[4]{0:T(128)S(1)} %pad_add_fusion.place_ref, ...), custom_call_target="tpu_custom_call", output_to_operand_aliasing={{0}: (10, {}), {1}: (11, {})} | custom-call | flops 7247757312 | bytes 10485760 | tf_op jit(solution)/shard_map/gen_forward/pallas_call | solution.py:244
  243.2 6.4 %copy-done.4 = bf16[2,3072,1536]{2,1,0:T(8,128)(2,1)} copy-done((bf16[2,3072,1536]{2,1,0:T(8,128)(2,1)}, bf16[2,3072,1536]{2,1,0:T(8,128)(2,1)S(1)}, u32[]{:S(2)}) %copy-start.4) | copy-done | bytes 18874392
  249.5 6.4 %copy-done.9 = bf16[2,3072,1536]{2,1,0:T(8,128)(2,1)} copy-done((bf16[2,3072,1536]{2,1,0:T(8,128)(2,1)}, bf16[2,3072,1536]{2,1,0:T(8,128)(2,1)S(1)}, u32[]{:S(2)}) %copy-start.9) | copy-done | bytes 18874392
  256.0 2.0 collective-permute-done.38.other
  258.0 1.9 add_noise.1
  260.1 1.9 collective-permute-done.39.u_other
  262.0 6.6 %copy-done.5 = bf16[2,3072,1536]{2,1,0:T(8,128)(2,1)S(1)} copy-done((bf16[2,3072,1536]{2,1,0:T(8,128)(2,1)S(1)}, bf16[2,3072,1536]{2,1,0:T(8,128)(2,1)}, u32[]{:S(2)}) %copy-start.5) | copy-done | bytes 18874392
  268.5 6.4 %copy-done.10 = bf16[2,3072,1536]{2,1,0:T(8,128)(2,1)S(1)} copy-done((bf16[2,3072,1536]{2,1,0:T(8,128)(2,1)S(1)}, bf16[2,3072,1536]{2,1,0:T(8,128)(2,1)}, u32[]{:S(2)}) %copy-start.10) | copy-done | bytes 18874392
  274.9 20.0 %score_forward.1 = (f32[2,192,1536]{2,1,0:T(8,128)}, bf16[192,64]{1,0:T(8,128)(2,1)S(1)}, f32[96,3072]{1,0:T(8,128)}, f32[96,3072]{1,0:T(8,128)}, bf16[192,3072]{1,0:T(8,128)(2,1)}) custom-call(bf16[96,3072]{1,0:T(8,128)(2,1)S(1)} %get-tuple-element.54.u_mine, bf16[96,3072]{1,0:T(8,128)(2,1)S(1)} %collective-permute-done.39.u_other, ...), custom_call_target="tpu_custom_call" | custom-call | flops 10871635968 | bytes 10485760 | tf_op jit(solution)/shard_map/score_forward/pallas_call | solution.py:305
  295.0 3.0 collective-permute-done.40.others
  298.0 1.3 copy-done.25
  299.2 1.3 copy-done.26
  300.5 1.7 cotangents.1
  302.3 2.7 collective-permute-done.41.cots_other
  305.0 6.4 %copy-done.6 = bf16[2,3072,1536]{2,1,0:T(8,128)(2,1)S(1)} copy-done((bf16[2,3072,1536]{2,1,0:T(8,128)(2,1)S(1)}, bf16[2,3072,1536]{2,1,0:T(8,128)(2,1)}, u32[]{:S(2)}) %copy-start.6) | copy-done | bytes 18874392
  311.4 13.4 %backward.1 = (bf16[2,2,64,1536]{3,2,1,0:T(8,128)(2,1)S(1)}, f32[2,192,64]{2,1,0:T(8,128)S(1)}) custom-call(bf16[192,3072]{1,0:T(8,128)(2,1)S(1)} %get-tuple-element.63.cots_mine, bf16[192,3072]{1,0:T(8,128)(2,1)S(1)} %collective-permute-done.41.cots_other, f32[2,192,1536]{2,1,0:T(8,128)S(1)} %copy-done.14, f32[2,192,1536]{2,1,0:T(8,128)S(1)} %copy-done.15, ...), custom_call_target="tpu_custom_call" | custom-call | flops 7247757312 | bytes 10485760 | tf_op jit(solution)/shard_map/backward/pallas_call | solution.py:361
  326.6 1.4 reshape.194
  333.3 28.1 %all_to_all.5 = bf16[64,72,128]{2,1,0:T(8,128)(2,1)S(1)} all-to-all(bf16[64,72,128]{2,1,0:T(8,128)(2,1)S(1)} %pad_maximum_fusion.1), channel_id=1, replica_groups=mesh['z'=4,'y'=4,'xh'=2,'xl'=2,'core'=2] {'z','y','xh','xl'}, dimensions={0} | all-to-all | bytes 2359296 | tf_op jit(solution)/shard_map/all_to_all | solution.py:575
  (212 shorter events, 39.9 us)
Async XLA Ops:
  7.2 125.3 %copy-start = (bf16[3072,64]{0,1:T(8,128)(2,1)S(1)}, bf16[3072,64]{0,1:T(8,128)(2,1)}, u32[]{:S(2)}) copy-start(bf16[3072,64]{0,1:T(8,128)(2,1)} %param.19) | copy-start | bytes 1179652
  7.2 172.4 %all-gather.2.cloned.1.call-start = ((), (), s32[]{:S(2)}) async-start(), calls=%async_computation.1 | async-start | bytes 9584640 | tf_op jit(solution)/shard_map/all_gather | solution.py:511
  7.3 13.6 %copy-start.11 = (bf16[96,3072]{1,0:T(8,128)(2,1)S(1)}, bf16[96,3072]{1,0:T(8,128)(2,1)}, u32[]{:S(2)}) copy-start(bf16[96,3072]{1,0:T(8,128)(2,1)} %given.1) | copy-start | bytes 1769476
  9.1 12.4 %copy-start.53 = (f32[3072]{0:T(1024)S(1)}, f32[3072]{0:T(1024)}, u32[]{:S(2)}) copy-start(f32[3072]{0:T(1024)} %param.23) | copy-start | bytes 36868
  10.2 26.7 %collective-permute-start.12 = (bf16[128,1536]{1,0:T(8,128)(2,1)S(1)}, bf16[128,1536]{1,0:T(8,128)(2,1)}, u32[]{:S(2)}, u32[]{:S(2)}) collective-permute-start(bf16[128,1536]{1,0:T(8,128)(2,1)S(1)} %constant_dynamic-update-slice_fusion.15), channel_id=1, source_target_pairs={{0,2},{2,0},{1,3},{3,1},{4,6},{6,4},{5,7},{7,5},{8,10},{10,8},{9,1... | collective-permute-start | bytes 1179656 | tf_op jit(solution)/shard_map/ppermute | solution.py:513
  11.8 12.3 %collective-permute-start.8 = (bf16[48,1536]{1,0:T(8,128)(2,1)S(1)}, bf16[48,1536]{1,0:T(8,128)(2,1)S(1)}, u32[]{:S(2)}, u32[]{:S(2)}) collective-permute-start(bf16[48,1536]{1,0:T(8,128)(2,1)S(1)} %get-tuple-element.77), channel_id=1, source_target_pairs={{0,2},{1,7},{2,4},{3,1},{4,6},{5,3},{6,0},{7,5},{8,10},{9,15},{10,... | collective-permute-start | bytes 442376 | tf_op jit(solution)/shard_map/ppermute | solution.py:78
  14.0 22.9 %copy-start.39 = (bf16[48,1536]{1,0:T(8,128)(2,1)}, bf16[48,1536]{1,0:T(8,128)(2,1)S(1)}, u32[]{:S(2)}) copy-start(bf16[48,1536]{1,0:T(8,128)(2,1)S(1)} %get-tuple-element.81) | copy-start | bytes 442372
  14.0 12.4 %collective-permute-start.4 = (bf16[48,1536]{1,0:T(8,128)(2,1)S(1)}, bf16[48,1536]{1,0:T(8,128)(2,1)S(1)}, u32[]{:S(2)}, u32[]{:S(2)}) collective-permute-start(bf16[48,1536]{1,0:T(8,128)(2,1)S(1)} %get-tuple-element.78), channel_id=1, source_target_pairs={{0,32},{1,97},{2,34},{3,99},{4,36},{5,101},{6,38},{7,103},{8,40},{... | collective-permute-start | bytes 442376 | tf_op jit(solution)/shard_map/ppermute | solution.py:78
  16.0 12.3 %collective-permute-start = (bf16[48,1536]{1,0:T(8,128)(2,1)S(1)}, bf16[48,1536]{1,0:T(8,128)(2,1)S(1)}, u32[]{:S(2)}, u32[]{:S(2)}) collective-permute-start(bf16[48,1536]{1,0:T(8,128)(2,1)S(1)} %get-tuple-element.81), channel_id=1, source_target_pairs={{0,8},{1,25},{2,10},{3,27},{4,12},{5,29},{6,14},{7,31},{8,16},{9,1... | collective-permute-start | bytes 442376 | tf_op jit(solution)/shard_map/ppermute | solution.py:78
  24.2 12.7 %copy-start.43 = (bf16[48,1536]{1,0:T(8,128)(2,1)}, bf16[48,1536]{1,0:T(8,128)(2,1)S(1)}, u32[]{:S(2)}) copy-start(bf16[48,1536]{1,0:T(8,128)(2,1)S(1)} %collective-permute-done.8) | copy-start | bytes 442372
  24.2 7.1 %collective-permute-start.9 = (bf16[48,1536]{1,0:T(8,128)(2,1)S(1)}, bf16[48,1536]{1,0:T(8,128)(2,1)S(1)}, u32[]{:S(2)}, u32[]{:S(2)}) collective-permute-start(bf16[48,1536]{1,0:T(8,128)(2,1)S(1)} %collective-permute-done.8), channel_id=1, source_target_pairs={{0,2},{1,7},{2,4},{3,1},{4,6},{5,3},{6,0},{7,5},{8,10},{9,15},{10,... | collective-permute-start | bytes 442376 | tf_op jit(solution)/shard_map/ppermute | solution.py:78
  26.4 6.6 %collective-permute-start.5 = (bf16[48,1536]{1,0:T(8,128)(2,1)S(1)}, bf16[48,1536]{1,0:T(8,128)(2,1)S(1)}, u32[]{:S(2)}, u32[]{:S(2)}) collective-permute-start(bf16[48,1536]{1,0:T(8,128)(2,1)S(1)} %collective-permute-done.4), channel_id=1, source_target_pairs={{0,32},{1,97},{2,34},{3,99},{4,36},{5,101},{6,38},{7,103},{8,40},{... | collective-permute-start | bytes 442376 | tf_op jit(solution)/shard_map/ppermute | solution.py:78
  28.3 6.6 %collective-permute-start.1 = (bf16[48,1536]{1,0:T(8,128)(2,1)S(1)}, bf16[48,1536]{1,0:T(8,128)(2,1)S(1)}, u32[]{:S(2)}, u32[]{:S(2)}) collective-permute-start(bf16[48,1536]{1,0:T(8,128)(2,1)S(1)} %collective-permute-done), channel_id=1, source_target_pairs={{0,8},{1,25},{2,10},{3,27},{4,12},{5,29},{6,14},{7,31},{8,16},{9,1... | collective-permute-start | bytes 442376 | tf_op jit(solution)/shard_map/ppermute | solution.py:78
  31.3 7.8 %collective-permute-start.10 = (bf16[48,1536]{1,0:T(8,128)(2,1)S(1)}, bf16[48,1536]{1,0:T(8,128)(2,1)S(1)}, u32[]{:S(2)}, u32[]{:S(2)}) collective-permute-start(bf16[48,1536]{1,0:T(8,128)(2,1)S(1)} %collective-permute-done.9), channel_id=1, source_target_pairs={{0,2},{1,7},{2,4},{3,1},{4,6},{5,3},{6,0},{7,5},{8,10},{9,15},{10,... | collective-permute-start | bytes 442376 | tf_op jit(solution)/shard_map/ppermute | solution.py:78
  33.0 9.9 %collective-permute-start.6 = (bf16[48,1536]{1,0:T(8,128)(2,1)S(1)}, bf16[48,1536]{1,0:T(8,128)(2,1)S(1)}, u32[]{:S(2)}, u32[]{:S(2)}) collective-permute-start(bf16[48,1536]{1,0:T(8,128)(2,1)S(1)} %collective-permute-done.5), channel_id=1, source_target_pairs={{0,32},{1,97},{2,34},{3,99},{4,36},{5,101},{6,38},{7,103},{8,40},{... | collective-permute-start | bytes 442376 | tf_op jit(solution)/shard_map/ppermute | solution.py:78
  34.9 6.4 %collective-permute-start.2 = (bf16[48,1536]{1,0:T(8,128)(2,1)S(1)}, bf16[48,1536]{1,0:T(8,128)(2,1)S(1)}, u32[]{:S(2)}, u32[]{:S(2)}) collective-permute-start(bf16[48,1536]{1,0:T(8,128)(2,1)S(1)} %collective-permute-done.1), channel_id=1, source_target_pairs={{0,8},{1,25},{2,10},{3,27},{4,12},{5,29},{6,14},{7,31},{8,16},{9,1... | collective-permute-start | bytes 442376 | tf_op jit(solution)/shard_map/ppermute | solution.py:78
  39.1 14.5 %collective-permute-start.11 = (bf16[192,1536]{1,0:T(8,128)(2,1)S(1)}, bf16[192,1536]{1,0:T(8,128)(2,1)S(1)}, u32[]{:S(2)}, u32[]{:S(2)}) collective-permute-start(bf16[192,1536]{1,0:T(8,128)(2,1)S(1)} %pad_maximum_fusion.5), channel_id=1, source_target_pairs={{0,8},{1,25},{2,10},{3,27},{4,12},{5,29},{6,14},{7,31},{8,16},{9,1... | collective-permute-start | bytes 1769480 | tf_op jit(solution)/shard_map/ppermute | solution.py:78
  41.3 15.9 %collective-permute-start.3 = (bf16[192,1536]{1,0:T(8,128)(2,1)S(1)}, bf16[192,1536]{1,0:T(8,128)(2,1)S(1)}, u32[]{:S(2)}, u32[]{:S(2)}) collective-permute-start(bf16[192,1536]{1,0:T(8,128)(2,1)S(1)} %pad_maximum_fusion.3), channel_id=1, source_target_pairs={{0,32},{1,97},{2,34},{3,99},{4,36},{5,101},{6,38},{7,103},{8,40},{... | collective-permute-start | bytes 1769480 | tf_op jit(solution)/shard_map/ppermute | solution.py:78
  43.0 15.5 %collective-permute-start.7 = (bf16[192,1536]{1,0:T(8,128)(2,1)S(1)}, bf16[192,1536]{1,0:T(8,128)(2,1)S(1)}, u32[]{:S(2)}, u32[]{:S(2)}) collective-permute-start(bf16[192,1536]{1,0:T(8,128)(2,1)S(1)} %pad_maximum_fusion.4), channel_id=1, source_target_pairs={{0,2},{1,7},{2,4},{3,1},{4,6},{5,3},{6,0},{7,5},{8,10},{9,15},{10,... | collective-permute-start | bytes 1769480 | tf_op jit(solution)/shard_map/ppermute | solution.py:78
  53.6 12.0 %collective-permute-start.33 = (bf16[192,1536]{1,0:T(8,128)(2,1)S(1)}, bf16[192,1536]{1,0:T(8,128)(2,1)S(1)}, u32[]{:S(2)}, u32[]{:S(2)}) collective-permute-start(bf16[192,1536]{1,0:T(8,128)(2,1)S(1)} %collective-permute-done.11), channel_id=1, source_target_pairs={{0,8},{1,25},{2,10},{3,27},{4,12},{5,29},{6,14},{7,31},{8,16},{9,1... | collective-permute-start | bytes 1769480 | tf_op jit(solution)/shard_map/ppermute | solution.py:78
  57.2 32.0 %collective-permute-start.21 = (bf16[192,1536]{1,0:T(8,128)(2,1)S(1)}, bf16[192,1536]{1,0:T(8,128)(2,1)S(1)}, u32[]{:S(2)}, u32[]{:S(2)}) collective-permute-start(bf16[192,1536]{1,0:T(8,128)(2,1)S(1)} %collective-permute-done.3), channel_id=1, source_target_pairs={{0,32},{1,97},{2,34},{3,99},{4,36},{5,101},{6,38},{7,103},{8,40},{... | collective-permute-start | bytes 1769480 | tf_op jit(solution)/shard_map/ppermute | solution.py:78
  58.5 11.1 %collective-permute-start.27 = (bf16[192,1536]{1,0:T(8,128)(2,1)S(1)}, bf16[192,1536]{1,0:T(8,128)(2,1)S(1)}, u32[]{:S(2)}, u32[]{:S(2)}) collective-permute-start(bf16[192,1536]{1,0:T(8,128)(2,1)S(1)} %collective-permute-done.7), channel_id=1, source_target_pairs={{0,2},{1,7},{2,4},{3,1},{4,6},{5,3},{6,0},{7,5},{8,10},{9,15},{10,... | collective-permute-start | bytes 1769480 | tf_op jit(solution)/shard_map/ppermute | solution.py:78
  65.7 23.5 %collective-permute-start.34 = (bf16[192,1536]{1,0:T(8,128)(2,1)S(1)}, bf16[192,1536]{1,0:T(8,128)(2,1)S(1)}, u32[]{:S(2)}, u32[]{:S(2)}) collective-permute-start(bf16[192,1536]{1,0:T(8,128)(2,1)S(1)} %collective-permute-done.33), channel_id=1, source_target_pairs={{0,8},{1,25},{2,10},{3,27},{4,12},{5,29},{6,14},{7,31},{8,16},{9,1... | collective-permute-start | bytes 1769480 | tf_op jit(solution)/shard_map/ppermute | solution.py:78
  66.7 23.9 %copy-start.50 = (f32[1,3072]{1,0:T(1,128)S(1)}, f32[1,3072]{1,0:T(1,128)}, u32[]{:S(2)}) copy-start(f32[1,3072]{1,0:T(1,128)} %get-tuple-element.99) | copy-start | bytes 36868
  66.7 23.9 %copy-start.51 = (f32[1,3072]{1,0:T(1,128)S(1)}, f32[1,3072]{1,0:T(1,128)}, u32[]{:S(2)}) copy-start(f32[1,3072]{1,0:T(1,128)} %get-tuple-element.104) | copy-start | bytes 36868
  66.7 23.9 %copy-start.52 = (f32[1,3072]{1,0:T(1,128)S(1)}, f32[1,3072]{1,0:T(1,128)}, u32[]{:S(2)}) copy-start(f32[1,3072]{1,0:T(1,128)} %get-tuple-element.105) | copy-start | bytes 36868
  66.7 23.9 %copy-start.56 = (f32[96]{0:T(128)S(1)}, f32[96]{0:T(128)}, u32[]{:S(2)}) copy-start(f32[96]{0:T(128)} %add_rsqrt_fusion) | copy-start | bytes 1156
  66.7 41.8 %collective-permute-start.13 = (bf16[384,1536]{1,0:T(8,128)(2,1)S(1)}, bf16[384,1536]{1,0:T(8,128)(2,1)}, u32[]{:S(2)}, u32[]{:S(2)}) collective-permute-start(bf16[384,1536]{1,0:T(8,128)(2,1)S(1)} %constant_dynamic-update-slice_fusion), channel_id=1, source_target_pairs={{0,2},{1,7},{2,4},{3,1},{4,6},{5,3},{6,0},{7,5},{8,10},{9,15},{10,... | collective-permute-start | bytes 3538952 | tf_op jit(solution)/shard_map/ppermute | solution.py:90
  66.9 48.8 %collective-permute-start.15 = (bf16[384,1536]{1,0:T(8,128)(2,1)}, bf16[384,1536]{1,0:T(8,128)(2,1)}, u32[]{:S(2)}, u32[]{:S(2)}) collective-permute-start(bf16[384,1536]{1,0:T(8,128)(2,1)} %constant_dynamic-update-slice_fusion.5), channel_id=1, source_target_pairs={{0,8},{1,25},{2,10},{3,27},{4,12},{5,29},{6,14},{7,31},{8,16},{9,1... | collective-permute-start | bytes 3538952 | tf_op jit(solution)/shard_map/ppermute | solution.py:90
  69.6 46.1 %collective-permute-start.17 = (bf16[384,1536]{1,0:T(8,128)(2,1)}, bf16[384,1536]{1,0:T(8,128)(2,1)}, u32[]{:S(2)}, u32[]{:S(2)}) collective-permute-start(bf16[384,1536]{1,0:T(8,128)(2,1)} %constant_dynamic-update-slice_fusion.10), channel_id=1, source_target_pairs={{0,32},{1,97},{2,34},{3,99},{4,36},{5,101},{6,38},{7,103},{8,40},{... | collective-permute-start | bytes 3538952 | tf_op jit(solution)/shard_map/ppermute | solution.py:90
  89.2 25.5 %collective-permute-start.28 = (bf16[192,1536]{1,0:T(8,128)(2,1)S(1)}, bf16[192,1536]{1,0:T(8,128)(2,1)S(1)}, u32[]{:S(2)}, u32[]{:S(2)}) collective-permute-start(bf16[192,1536]{1,0:T(8,128)(2,1)S(1)} %collective-permute-done.27), channel_id=1, source_target_pairs={{0,2},{1,7},{2,4},{3,1},{4,6},{5,3},{6,0},{7,5},{8,10},{9,15},{10,... | collective-permute-start | bytes 1769480 | tf_op jit(solution)/shard_map/ppermute | solution.py:78
  89.2 21.7 %copy-start.12 = (bf16[384,1536]{1,0:T(8,128)(2,1)}, bf16[384,1536]{1,0:T(8,128)(2,1)S(1)}, u32[]{:S(2)}) copy-start(bf16[384,1536]{1,0:T(8,128)(2,1)S(1)} %constant_dynamic-update-slice_fusion.21) | copy-start | bytes 3538948
  89.3 39.9 %collective-permute-start.35 = (bf16[384,1536]{1,0:T(8,128)(2,1)S(1)}, bf16[384,1536]{1,0:T(8,128)(2,1)S(1)}, u32[]{:S(2)}, u32[]{:S(2)}) collective-permute-start(bf16[384,1536]{1,0:T(8,128)(2,1)S(1)} %constant_dynamic-update-slice_fusion.21), channel_id=1, source_target_pairs={{0,32},{1,97},{2,34},{3,99},{4,36},{5,101},{6,38},{7,103},{8,40},{... | collective-permute-start | bytes 3538952 | tf_op jit(solution)/shard_map/ppermute | solution.py:90
  91.0 23.8 %copy-start.36 = (bf16[96,3072]{1,0:T(8,128)(2,1)}, bf16[96,3072]{1,0:T(8,128)(2,1)S(1)}, u32[]{:S(2)}) copy-start(bf16[96,3072]{1,0:T(8,128)(2,1)S(1)} %fusion.3) | copy-start | bytes 1769476
  108.5 19.1 %collective-permute-start.22 = (bf16[192,1536]{1,0:T(8,128)(2,1)S(1)}, bf16[192,1536]{1,0:T(8,128)(2,1)S(1)}, u32[]{:S(2)}, u32[]{:S(2)}) collective-permute-start(bf16[192,1536]{1,0:T(8,128)(2,1)S(1)} %collective-permute-done.21), channel_id=1, source_target_pairs={{0,32},{1,97},{2,34},{3,99},{4,36},{5,101},{6,38},{7,103},{8,40},{... | collective-permute-start | bytes 1769480 | tf_op jit(solution)/shard_map/ppermute | solution.py:78
  114.7 12.9 %collective-permute-start.19 = (bf16[96,3072]{1,0:T(8,128)(2,1)S(1)}, bf16[96,3072]{1,0:T(8,128)(2,1)}, u32[]{:S(2)}, u32[]{:S(2)}) collective-permute-start(bf16[96,3072]{1,0:T(8,128)(2,1)S(1)} %fusion.3), channel_id=1, source_target_pairs={{0,1},{1,0},{2,3},{3,2},{4,5},{5,4},{6,7},{7,6},{8,9},{9,8},{10,11... | collective-permute-start | bytes 1769480 | tf_op jit(solution)/shard_map/ppermute | solution.py:56
  115.7 16.8 %copy-start.37 = (bf16[96,3072]{1,0:T(8,128)(2,1)S(1)}, bf16[96,3072]{1,0:T(8,128)(2,1)}, u32[]{:S(2)}) copy-start(bf16[96,3072]{1,0:T(8,128)(2,1)} %copy-done.36) | copy-start | bytes 1769476
  115.7 19.7 %collective-permute-start.14 = (bf16[384,1536]{1,0:T(8,128)(2,1)}, bf16[384,1536]{1,0:T(8,128)(2,1)}, u32[]{:S(2)}, u32[]{:S(2)}) collective-permute-start(bf16[384,1536]{1,0:T(8,128)(2,1)} %collective-permute-done.13), channel_id=1, source_target_pairs={{0,2},{1,7},{2,4},{3,1},{4,6},{5,3},{6,0},{7,5},{8,10},{9,15},{10,... | collective-permute-start | bytes 3538952 | tf_op jit(solution)/shard_map/ppermute | solution.py:90
  115.7 20.4 %collective-permute-start.16 = (bf16[384,1536]{1,0:T(8,128)(2,1)}, bf16[384,1536]{1,0:T(8,128)(2,1)}, u32[]{:S(2)}, u32[]{:S(2)}) collective-permute-start(bf16[384,1536]{1,0:T(8,128)(2,1)} %collective-permute-done.15), channel_id=1, source_target_pairs={{0,8},{1,25},{2,10},{3,27},{4,12},{5,29},{6,14},{7,31},{8,16},{9,1... | collective-permute-start | bytes 3538952 | tf_op jit(solution)/shard_map/ppermute | solution.py:90
  127.6 17.7 %collective-permute-start.18 = (bf16[384,1536]{1,0:T(8,128)(2,1)}, bf16[384,1536]{1,0:T(8,128)(2,1)}, u32[]{:S(2)}, u32[]{:S(2)}) collective-permute-start(bf16[384,1536]{1,0:T(8,128)(2,1)} %collective-permute-done.17), channel_id=1, source_target_pairs={{0,32},{1,97},{2,34},{3,99},{4,36},{5,101},{6,38},{7,103},{8,40},{... | collective-permute-start | bytes 3538952 | tf_op jit(solution)/shard_map/ppermute | solution.py:90
  127.7 18.4 %collective-permute-start.23 = (bf16[384,1536]{1,0:T(8,128)(2,1)S(1)}, bf16[384,1536]{1,0:T(8,128)(2,1)}, u32[]{:S(2)}, u32[]{:S(2)}) collective-permute-start(bf16[384,1536]{1,0:T(8,128)(2,1)S(1)} %constant_dynamic-update-slice_fusion.17), channel_id=1, source_target_pairs={{0,2},{1,7},{2,4},{3,1},{4,6},{5,3},{6,0},{7,5},{8,10},{9,15},{10,... | collective-permute-start | bytes 3538952 | tf_op jit(solution)/shard_map/ppermute | solution.py:90
  130.2 17.7 %collective-permute-start.29 = (bf16[384,1536]{1,0:T(8,128)(2,1)}, bf16[384,1536]{1,0:T(8,128)(2,1)}, u32[]{:S(2)}, u32[]{:S(2)}) collective-permute-start(bf16[384,1536]{1,0:T(8,128)(2,1)} %constant_dynamic-update-slice_fusion.19), channel_id=1, source_target_pairs={{0,8},{1,25},{2,10},{3,27},{4,12},{5,29},{6,14},{7,31},{8,16},{9,1... | collective-permute-start | bytes 3538952 | tf_op jit(solution)/shard_map/ppermute | solution.py:90
  134.0 76.4 %copy-start.29 = (bf16[192,64]{1,0:T(8,128)(2,1)}, bf16[192,64]{1,0:T(8,128)(2,1)S(1)}, u32[]{:S(2)}) copy-start(bf16[192,64]{1,0:T(8,128)(2,1)S(1)} %convolution_convert_fusion.low.low_gen) | copy-start | bytes 73732
  134.0 44.8 %copy-start.34 = (bf16[2,128,1536]{2,1,0:T(8,128)(2,1)S(1)}, bf16[2,128,1536]{2,1,0:T(8,128)(2,1)}, u32[]{:S(2)}) copy-start(bf16[2,128,1536]{2,1,0:T(8,128)(2,1)} %pad_maximum_fusion.2) | copy-start | bytes 2359300
  135.5 22.5 %collective-permute-start.36 = (bf16[384,1536]{1,0:T(8,128)(2,1)S(1)}, bf16[384,1536]{1,0:T(8,128)(2,1)}, u32[]{:S(2)}, u32[]{:S(2)}) collective-permute-start(bf16[384,1536]{1,0:T(8,128)(2,1)S(1)} %copy-done.21), channel_id=1, source_target_pairs={{0,32},{1,97},{2,34},{3,99},{4,36},{5,101},{6,38},{7,103},{8,40},{... | collective-permute-start | bytes 3538952 | tf_op jit(solution)/shard_map/ppermute | solution.py:90
  146.1 17.7 %collective-permute-start.24 = (bf16[384,1536]{1,0:T(8,128)(2,1)}, bf16[384,1536]{1,0:T(8,128)(2,1)}, u32[]{:S(2)}, u32[]{:S(2)}) collective-permute-start(bf16[384,1536]{1,0:T(8,128)(2,1)} %collective-permute-done.23), channel_id=1, source_target_pairs={{0,2},{1,7},{2,4},{3,1},{4,6},{5,3},{6,0},{7,5},{8,10},{9,15},{10,... | collective-permute-start | bytes 3538952 | tf_op jit(solution)/shard_map/ppermute | solution.py:90
  147.9 17.7 %collective-permute-start.30 = (bf16[384,1536]{1,0:T(8,128)(2,1)}, bf16[384,1536]{1,0:T(8,128)(2,1)}, u32[]{:S(2)}, u32[]{:S(2)}) collective-permute-start(bf16[384,1536]{1,0:T(8,128)(2,1)} %collective-permute-done.29), channel_id=1, source_target_pairs={{0,8},{1,25},{2,10},{3,27},{4,12},{5,29},{6,14},{7,31},{8,16},{9,1... | collective-permute-start | bytes 3538952 | tf_op jit(solution)/shard_map/ppermute | solution.py:90
  148.3 28.0 %collective-permute-start.20 = (bf16[384,1536]{1,0:T(8,128)(2,1)}, bf16[384,1536]{1,0:T(8,128)(2,1)S(1)}, u32[]{:S(2)}, u32[]{:S(2)}) collective-permute-start(bf16[384,1536]{1,0:T(8,128)(2,1)} %collective-permute-done.14), channel_id=1, source_target_pairs={{0,2},{1,7},{2,4},{3,1},{4,6},{5,3},{6,0},{7,5},{8,10},{9,15},{10,... | collective-permute-start | bytes 3538952 | tf_op jit(solution)/shard_map/ppermute | solution.py:90
  149.8 60.6 %collective-permute-start.26 = (bf16[384,1536]{1,0:T(8,128)(2,1)}, bf16[384,1536]{1,0:T(8,128)(2,1)}, u32[]{:S(2)}, u32[]{:S(2)}) collective-permute-start(bf16[384,1536]{1,0:T(8,128)(2,1)} %collective-permute-done.16), channel_id=1, source_target_pairs={{0,8},{1,25},{2,10},{3,27},{4,12},{5,29},{6,14},{7,31},{8,16},{9,1... | collective-permute-start | bytes 3538952 | tf_op jit(solution)/shard_map/ppermute | solution.py:90
  158.0 52.4 %collective-permute-start.32 = (bf16[384,1536]{1,0:T(8,128)(2,1)}, bf16[384,1536]{1,0:T(8,128)(2,1)}, u32[]{:S(2)}, u32[]{:S(2)}) collective-permute-start(bf16[384,1536]{1,0:T(8,128)(2,1)} %collective-permute-done.18), channel_id=1, source_target_pairs={{0,32},{1,97},{2,34},{3,99},{4,36},{5,101},{6,38},{7,103},{8,40},{... | collective-permute-start | bytes 3538952 | tf_op jit(solution)/shard_map/ppermute | solution.py:90
  163.8 46.6 %collective-permute-start.37 = (bf16[384,1536]{1,0:T(8,128)(2,1)}, bf16[384,1536]{1,0:T(8,128)(2,1)}, u32[]{:S(2)}, u32[]{:S(2)}) collective-permute-start(bf16[384,1536]{1,0:T(8,128)(2,1)} %collective-permute-done.36), channel_id=1, source_target_pairs={{0,32},{1,97},{2,34},{3,99},{4,36},{5,101},{6,38},{7,103},{8,40},{... | collective-permute-start | bytes 3538952 | tf_op jit(solution)/shard_map/ppermute | solution.py:90
  165.7 44.7 %collective-permute-start.25 = (bf16[384,1536]{1,0:T(8,128)(2,1)}, bf16[384,1536]{1,0:T(8,128)(2,1)}, u32[]{:S(2)}, u32[]{:S(2)}) collective-permute-start(bf16[384,1536]{1,0:T(8,128)(2,1)} %collective-permute-done.24), channel_id=1, source_target_pairs={{0,2},{1,7},{2,4},{3,1},{4,6},{5,3},{6,0},{7,5},{8,10},{9,15},{10,... | collective-permute-start | bytes 3538952 | tf_op jit(solution)/shard_map/ppermute | solution.py:90
  177.4 33.0 %collective-permute-start.31 = (bf16[384,1536]{1,0:T(8,128)(2,1)}, bf16[384,1536]{1,0:T(8,128)(2,1)}, u32[]{:S(2)}, u32[]{:S(2)}) collective-permute-start(bf16[384,1536]{1,0:T(8,128)(2,1)} %collective-permute-done.30), channel_id=1, source_target_pairs={{0,8},{1,25},{2,10},{3,27},{4,12},{5,29},{6,14},{7,31},{8,16},{9,1... | collective-permute-start | bytes 3538952 | tf_op jit(solution)/shard_map/ppermute | solution.py:90
  183.4 27.0 %copy-start.24 = (bf16[384,1536]{1,0:T(8,128)(2,1)S(1)}, bf16[384,1536]{1,0:T(8,128)(2,1)}, u32[]{:S(2)}) copy-start(bf16[384,1536]{1,0:T(8,128)(2,1)} %copy-done.23) | copy-start | bytes 3538948
  223.1 34.8 %copy-start.16 = (bf16[96,3072]{1,0:T(8,128)(2,1)S(1)}, bf16[96,3072]{1,0:T(8,128)(2,1)}, u32[]{:S(2)}) copy-start(bf16[96,3072]{1,0:T(8,128)(2,1)} %noise.3) | copy-start | bytes 1769476
  223.1 34.8 %copy-start.31 = (f32[4,3072]{1,0:T(4,128)S(1)}, f32[4,3072]{1,0:T(4,128)}, u32[]{:S(2)}) copy-start(f32[4,3072]{1,0:T(4,128)} %pad_maximum_fusion.7.mods) | copy-start | bytes 147460
  223.1 34.8 %copy-start.32 = (f32[3072]{0:T(1024)S(1)}, f32[3072]{0:T(1024)}, u32[]{:S(2)}) copy-start(f32[3072]{0:T(1024)} %param.25) | copy-start | bytes 36868
  255.9 2.0 collective-permute-start.38
  259.9 2.1 collective-permute-start.39
  262.0 33.0 %copy-start.27 = (bf16[96,3072]{1,0:T(8,128)(2,1)}, bf16[96,3072]{1,0:T(8,128)(2,1)S(1)}, u32[]{:S(2)}) copy-start(bf16[96,3072]{1,0:T(8,128)(2,1)S(1)} %collective-permute-done.39.u_other) | copy-start | bytes 1769476
  294.9 3.1 collective-permute-start.40
  302.2 2.8 collective-permute-start.41
  325.6 2.4 collective-permute-start.42
  333.3 30.2 %copy-start.1 = (bf16[3072,64]{0,1:T(8,128)(2,1)S(1)}, bf16[3072,64]{0,1:T(8,128)(2,1)}, u32[]{:S(2)}) copy-start(bf16[3072,64]{0,1:T(8,128)(2,1)} %param.19) | copy-start | bytes 1179652
  (37 other events, 161.7 us)
Sparse Core Ops, SparseCore 0:
  10.8 98.2 all-gather.1
